TPU v7x, 768 devices: a whole 4x8x12 slice. The times are simulated.
768 devices in a mesh: frame: 8 (over x, core), fsdp: 24 (over z, y_lo), head: 4 (over y_hi).
Axes of the slice: x: 4, y: 8 (y_hi: 4, y_lo: 2; y = y_hi * 2 + y_lo), z: 12, core: 2. Of those that a mesh axis runs over, the one named last changes fastest.
Arguments:
- queries: bfloat16 [2048, 61440], P('frame', ('fsdp', 'head')), may hold values from -6 to 6
- noisy_keys: bfloat16 [2048, 61440], P('frame', ('fsdp', 'head')), may hold values from -6 to 6
- noisy_values: bfloat16 [2048, 61440], P('frame', ('fsdp', 'head')), may hold values from -6 to 6
- clean_keys: bfloat16 [2048, 61440], P('frame', ('fsdp', 'head')), may hold values from -10 to 10
- clean_values: bfloat16 [2048, 61440], P('frame', ('fsdp', 'head')), may hold values from -6 to 6
- gain_query: float32 [5120], replicated, may hold values from 0.5 to 2
- gain_key: float32 [5120], replicated, may hold values from 0.5 to 2
- out_grad: bfloat16 [2048, 61440], P('frame', ('fsdp', 'head')), may hold values from -6 to 6
Outputs:
- attended: bfloat16 [2048, 61440], P('frame', ('fsdp', 'head'))
- grad_queries: bfloat16 [2048, 61440], P('frame', ('fsdp', 'head'))
- grad_keys: bfloat16 [2048, 61440], P('frame', ('fsdp', 'head'))
- grad_values: bfloat16 [2048, 61440], P('frame', ('fsdp', 'head'))
- grad_gain_query: float32 [5120], replicated
- grad_gain_key: float32 [5120], replicated
All inputs are finite; a program needn't handle non-finite values.
Results may differ from a plain program's by a relative error of at most 0.012.
Values may be sent and summed in bfloat16 or wider, within the bound.
No kernel may reach another device: no remote copies, remote signals or barrier semaphores. Data moves between devices by JAX's collectives and lax.ppermute only.
A program may use at most 64 MiB of HBM per device.

v0:
```python
import math

import jax
import jax.numpy as jnp
from jax import lax
from jax.sharding import Mesh
from jax.sharding import PartitionSpec as P

D = 5120
DH = 128
FRAME = ("frame_0", "frame_1")
FSDP = ("fsdp_0", "fsdp_1")
FRAME_FSDP_HEAD = ("frame_0", "frame_1", "fsdp_0", "fsdp_1", "head")
FSDP_HEAD = ("fsdp_0", "fsdp_1", "head")


EPSILON = 1e-06
MASKED = -1e30


def shifted(block, axis, distance):
    devices = range(lax.axis_size(axis))
    route = [((i - distance) % len(devices), i) for i in devices]
    return lax.ppermute(block, axis, route)


def side_by_side(arrays, axis, dim, along):
    widths = [a.shape[along] for a in arrays]
    both = jnp.concatenate(arrays, axis=along)
    out = lax.all_gather(both, axis, axis=dim, tiled=True)
    return tuple(jnp.split(out, [sum(widths[:k]) for k in range(1, len(widths))], axis=along))


def one_axis_at_a_time(x, axes):
    for axis in axes:
        x = lax.psum(x, axis)
    return x


def project(left_side, right_side):
    return jnp.einsum("qhd,khd->hqk", left_side, right_side, preferred_element_type=jnp.float32)


def on_device(
    queries, noisy_keys, noisy_values, clean_keys, clean_values, gain_query, gain_key, out_grad
):
    length = queries.shape[0]
    width_dev = queries.shape[1]
    head_count = width_dev // DH
    scaling = 1.0 / math.sqrt(DH)
    own_frame = lax.axis_index(FRAME)
    own_start = own_frame * length
    pair_reach = lax.axis_size(FSDP) // 2
    half_index = lax.axis_index(FSDP) // pair_reach
    column_start = (half_index * lax.axis_size("head") + lax.axis_index("head")) * width_dev
    gain_q = lax.dynamic_slice_in_dim(gain_query, column_start, width_dev)
    gain_k = lax.dynamic_slice_in_dim(gain_key, column_start, width_dev)

    def with_partner(stats):
        other = shifted(stats, FSDP, pair_reach)
        return stats + other

    q_full = queries.astype(jnp.float32)
    k_full = noisy_keys.astype(jnp.float32)
    squares_q, squares_k = lax.psum(
        (jnp.sum(q_full * q_full, axis=1), jnp.sum(k_full * k_full, axis=1)), "head"
    )
    squares = with_partner(jnp.stack([squares_q, squares_k]))
    rate_q = lax.rsqrt(squares[0] / D + EPSILON)
    rate_k = lax.rsqrt(squares[1] / D + EPSILON)
    normed_q = (
        (q_full * rate_q[:, None] * gain_q).astype(jnp.bfloat16).reshape(length, head_count, DH)
    )
    normed_k = (
        (k_full * rate_k[:, None] * gain_k).astype(jnp.bfloat16).reshape(length, head_count, DH)
    )
    values_own = noisy_values.reshape(length, head_count, DH)
    grads_out = out_grad.reshape(length, head_count, DH)
    own_scores = project(normed_q, normed_k) * scaling
    row_max = jnp.max(own_scores, axis=2)
    expo = jnp.exp(own_scores - row_max[:, :, None])
    totals = jnp.sum(expo, axis=2)
    summed = jnp.einsum(
        "hqk,khd->hqd", expo.astype(jnp.bfloat16), values_own, preferred_element_type=jnp.float32
    )

    def split_piece(portion):
        key_piece, value_piece = portion
        row_count = key_piece.shape[0]
        return (
            key_piece.reshape(row_count, head_count, DH),
            value_piece.reshape(row_count, head_count, DH),
            row_count,
        )

    def visible_scores(key_piece, row_count):
        scores = project(normed_q, key_piece) * scaling
        frame_of = jnp.arange(row_count, dtype=jnp.int32) // length
        return jnp.where((frame_of < own_frame)[None, None, :], scores, MASKED)

    initial = (row_max, totals, summed)
    key_piece, value_piece, row_count = split_piece(
        side_by_side((clean_keys, clean_values), FRAME, 0, 1)
    )

    def attend(status):
        running, denominator, accumulated = status
        scores = visible_scores(key_piece, row_count)
        newest = jnp.maximum(running, jnp.max(scores, axis=2))
        exponent = jnp.exp(scores - newest[:, :, None])
        factor = jnp.exp(running - newest)
        added = jnp.einsum(
            "hqk,khd->hqd",
            exponent.astype(jnp.bfloat16),
            value_piece,
            preferred_element_type=jnp.float32,
        )
        return (
            newest,
            denominator * factor + jnp.sum(exponent, axis=2),
            accumulated * factor[:, :, None] + added,
        )

    running, denominator, accumulated = lax.cond(
        jnp.int32(0) < own_start, attend, lambda status: status, initial
    )
    log_total = running + jnp.log(denominator)
    output_f32 = accumulated / denominator[:, :, None]
    attended = jnp.transpose(output_f32, (1, 0, 2)).reshape(length, width_dev).astype(jnp.bfloat16)
    delta = jnp.sum(jnp.transpose(grads_out.astype(jnp.float32), (1, 0, 2)) * output_f32, axis=2)
    soft_probs = jnp.exp(own_scores - log_total[:, :, None])
    grad_probs = project(grads_out, values_own)
    grad_scores = (soft_probs * (grad_probs - delta[:, :, None])).astype(jnp.bfloat16)
    grad_qn = (
        jnp.einsum("hqk,khd->qhd", grad_scores, normed_k, preferred_element_type=jnp.float32)
        * scaling
    )
    grad_kn = (
        jnp.einsum("hqk,qhd->khd", grad_scores, normed_q, preferred_element_type=jnp.float32)
        * scaling
    )
    grad_vv = jnp.einsum(
        "hqk,qhd->khd",
        soft_probs.astype(jnp.bfloat16),
        grads_out,
        preferred_element_type=jnp.float32,
    )
    reflect_key_piece, reflect_value_piece, reflect_row_count = split_piece(
        side_by_side((clean_keys, clean_values), FRAME, 0, 1)
    )

    def attend_back(current):
        scores = visible_scores(reflect_key_piece, reflect_row_count)
        piece_probs = jnp.exp(scores - log_total[:, :, None])
        piece_grads = project(grads_out, reflect_value_piece)
        weighted = (piece_probs * (piece_grads - delta[:, :, None])).astype(jnp.bfloat16)
        return (
            current
            + jnp.einsum(
                "hqk,khd->qhd", weighted, reflect_key_piece, preferred_element_type=jnp.float32
            )
            * scaling
        )

    grad_qn = lax.cond(jnp.int32(0) < own_start, attend_back, lambda current: current, grad_qn)
    plain_q = grad_qn.reshape(length, width_dev)
    plain_k = grad_kn.reshape(length, width_dev)
    flat_q = plain_q * gain_q
    flat_k = plain_k * gain_k
    inner_q, inner_k = lax.psum(
        (jnp.sum(q_full * flat_q, axis=1), jnp.sum(k_full * flat_k, axis=1)), "head"
    )
    inners = with_partner(jnp.stack([inner_q, inner_k]))
    cube_q = rate_q * rate_q * rate_q * inners[0] / D
    cube_k = rate_k * rate_k * rate_k * inners[1] / D
    grad_queries = (rate_q[:, None] * flat_q - q_full * cube_q[:, None]).astype(jnp.bfloat16)
    grad_keys = (rate_k[:, None] * flat_k - k_full * cube_k[:, None]).astype(jnp.bfloat16)
    part_q = jnp.sum(plain_q * q_full * rate_q[:, None], axis=0)
    part_k = jnp.sum(plain_k * k_full * rate_k[:, None], axis=0)
    blank = jnp.zeros((D,), jnp.float32)
    spread_q = lax.dynamic_update_slice_in_dim(blank, part_q, column_start, 0)
    spread_k = lax.dynamic_update_slice_in_dim(blank, part_k, column_start, 0)
    grad_gain_query, grad_gain_key = (
        one_axis_at_a_time(spread_q, FRAME_FSDP_HEAD),
        one_axis_at_a_time(spread_k, FRAME_FSDP_HEAD),
    )
    grad_values = grad_vv.reshape(length, width_dev).astype(jnp.bfloat16)
    return (attended, grad_queries, grad_keys, grad_values, grad_gain_query, grad_gain_key)


def solution(mesh):
    torus = Mesh(
        mesh.devices.reshape(4, 2, 12, 2, mesh.shape["head"]),
        ("frame_0", "frame_1", "fsdp_0", "fsdp_1", "head"),
    )
    in_specs = (
        P(FRAME, FSDP_HEAD),
        P(FRAME, FSDP_HEAD),
        P(FRAME, FSDP_HEAD),
        P(FRAME, FSDP_HEAD),
        P(FRAME, FSDP_HEAD),
        P(),
        P(),
        P(FRAME, FSDP_HEAD),
    )
    out_specs = (
        P(FRAME, FSDP_HEAD),
        P(FRAME, FSDP_HEAD),
        P(FRAME, FSDP_HEAD),
        P(FRAME, FSDP_HEAD),
        P(),
        P(),
    )
    return jax.shard_map(
        on_device, mesh=torus, in_specs=in_specs, out_specs=out_specs, check_vma=False
    )
```

profile of v0, /device:TPU:8, one launch (start us, length us, event | category | flops | bytes accessed | tf_op | source)
XLA Modules:
  0.0 221.7 jit_solution(2468481087181807031)
XLA Ops:
  7.2 0.0 all-gather.2.cloned.1.call-start
  7.2 1.2 copy.45
  8.5 1.2 copy.46
  9.7 0.9 pad_maximum_fusion
  10.6 0.0 all-gather.2.cloned.1.call-update
  10.6 0.2 copy.38
  10.8 0.2 copy.39
  11.0 0.1 fusion.37
  11.1 0.1 fusion.45
  11.2 12.0 %all-reduce.2 = (f32[1,256]{1,0:T(1,128)S(1)}, f32[1,256]{1,0:T(1,128)S(1)}) all-reduce(f32[1,256]{1,0:T(1,128)S(1)} %bitcast.84, f32[1,256]{1,0:T(1,128)S(1)} %bitcast.83), channel_id=1, replica_groups=mesh['frame_0'=4,'frame_1'=2,'fsdp_0'=12,'fsdp_1'=2,'head'=4] {'head'}, use_global_device_ids=true, to_apply=%region_3.4 | all-reduce | flops 512 | bytes 4096 | tf_op jit(solution)/shard_map/psum | solution.py:65
  23.2 15.1 %collective-permute-start = (f32[2,256]{1,0:T(2,128)S(1)}, f32[2,256]{1,0:T(2,128)S(1)}, u32[]{:S(2)}, u32[]{:S(2)}) collective-permute-start(f32[2,256]{1,0:T(2,128)S(1)} %pad_maximum_fusion.1), channel_id=1, source_target_pairs={{48,0},{52,4},{56,8},{60,12},{64,16},{68,20},{72,24},{76,28},{80,3... | collective-permute-start | bytes 6152 | tf_op jit(solution)/shard_map/ppermute | solution.py:24
  38.4 0.8 dynamic_slice.6
  39.2 0.8 dynamic_slice.7
  39.9 0.2 copy.42
  40.1 0.9 copy.51
  41.1 0.2 fusion.39
  41.2 0.2 fusion.47
  41.4 0.4 fusion.69
  41.8 0.3 copy-done.7
  42.1 0.2 fusion.32
  42.3 0.6 copy-done
  42.9 1.3 fusion.35
  44.2 21.8 %all-gather.2.cloned.1.call-done = bf16[2048,1280]{0,1:T(8,128)(2,1)} async-done(((bf16[256,1280]{0,1:T(8,128)(2,1)}), bf16[2048,1280]{0,1:T(8,128)(2,1)}) %all-gather.2.cloned.1.call-update) | async-done | bytes 5242896 | tf_op jit(solution)/shard_map/all_gather | solution.py:30
  65.9 4.7 %fusion.67 = (bf16[2048,640]{0,1:T(8,128)(2,1)}, bf16[2048,640]{0,1:T(8,128)(2,1)S(1)}) fusion(bf16[2048,1280]{0,1:T(8,128)(2,1)} %all-gather.2.cloned.1.call-done), kind=kLoop, calls=%fused_computation.102 | loop fusion | bytes 10485760 | tf_op jit(solution)/shard_map/split | solution.py:31
  70.6 2.2 copy.50
  72.8 2.1 fusion.53
  74.9 2.0 fusion.29
  76.9 1.1 fusion.30
  78.0 0.4 convolution_multiply_fusion.1
  78.4 0.4 fusion.52
  78.7 0.5 copy-done.4
  79.2 1.6 fusion.44
  80.8 0.3 dynamic_update_slice.7
  81.1 0.3 dynamic_update_slice.6
  81.4 42.1 %all-reduce.3 = (f32[5120]{0:T(1024)S(1)}, f32[5120]{0:T(1024)S(1)}) all-reduce(f32[5120]{0:T(1024)S(1)} %dynamic_update_slice.6, f32[5120]{0:T(1024)S(1)} %dynamic_update_slice.7), channel_id=1, replica_groups=mesh['frame_0'=4,'frame_1'=2,'fsdp_0'=12,'fsdp_1'=2,'head'=4] {'frame_0'}, use_global_device_ids=true, to_apply=%region_18.19 | all-reduce | flops 10240 | bytes 81920 | tf_op jit(solution)/shard_map/psum | solution.py:36
  123.5 3.5 %all-reduce.5 = (f32[5120]{0:T(1024)S(1)}, f32[5120]{0:T(1024)S(1)}) all-reduce(f32[5120]{0:T(1024)S(1)} %get-tuple-element.158, f32[5120]{0:T(1024)S(1)} %get-tuple-element.159), channel_id=1, replica_groups=mesh['frame_0'=4,'frame_1'=2,'fsdp_0'=12,'fsdp_1'=2,'head'=4] {'frame_1'}, use_global_device_ids=true, to_apply=%region_19.20 | all-reduce | flops 10240 | bytes 81920 | tf_op jit(solution)/shard_map/psum | solution.py:36
  127.0 44.6 %all-reduce = (f32[5120]{0:T(1024)S(1)}, f32[5120]{0:T(1024)S(1)}) all-reduce(f32[5120]{0:T(1024)S(1)} %get-tuple-element.162, f32[5120]{0:T(1024)S(1)} %get-tuple-element.163), channel_id=1, replica_groups=mesh['frame_0'=4,'frame_1'=2,'fsdp_0'=12,'fsdp_1'=2,'head'=4] {'fsdp_0'}, use_global_device_ids=true, to_apply=%region_20.21 | all-reduce | flops 10240 | bytes 81920 | tf_op jit(solution)/shard_map/psum | solution.py:36
  171.6 7.5 %all-reduce.4 = (f32[5120]{0:T(1024)S(1)}, f32[5120]{0:T(1024)S(1)}) all-reduce(f32[5120]{0:T(1024)S(1)} %get-tuple-element.150, f32[5120]{0:T(1024)S(1)} %get-tuple-element.151), channel_id=1, replica_groups=mesh['frame_0'=4,'frame_1'=2,'fsdp_0'=12,'fsdp_1'=2,'head'=4] {'fsdp_1'}, use_global_device_ids=true, to_apply=%region_21.22 | all-reduce | flops 10240 | bytes 81920 | tf_op jit(solution)/shard_map/psum | solution.py:36
  179.1 20.7 %all-reduce.1 = (f32[1,256]{1,0:T(1,128)S(1)}, f32[1,256]{1,0:T(1,128)S(1)}, f32[5120]{0:T(1024)}, f32[5120]{0:T(1024)}) all-reduce(f32[1,256]{1,0:T(1,128)S(1)} %bitcast.87, f32[1,256]{1,0:T(1,128)S(1)} %bitcast.88, ...), channel_id=1, replica_groups=mesh['frame_0'=4,'frame_1'=2,'fsdp_0'=12,'fsdp_1'=2,'head'=4] {'head'}, use_global_device_ids=true, to_apply=%region_16.17 | all-reduce | flops 10752 | bytes 86016 | tf_op jit(solution)/shard_map/psum | solution.py:170
  199.8 6.4 %collective-permute-start.1 = (f32[2,256]{1,0:T(2,128)S(1)}, f32[2,256]{1,0:T(2,128)S(1)}, u32[]{:S(2)}, u32[]{:S(2)}) collective-permute-start(f32[2,256]{1,0:T(2,128)S(1)} %pad_maximum_fusion.2), channel_id=1, source_target_pairs={{48,0},{52,4},{56,8},{60,12},{64,16},{68,20},{72,24},{76,28},{80,3... | collective-permute-start | bytes 6152 | tf_op jit(solution)/shard_map/ppermute | solution.py:24
  206.2 1.8 convolution_convert_fusion
  208.0 0.9 copy.64
  208.9 0.9 copy.61
  209.8 1.8 collective-permute-done.1
  211.7 0.2 fusion.50
  211.8 0.9 copy.63
  212.7 1.2 fusion.42
  214.0 0.9 copy.62
  (39 shorter events, 0.1 us)
Async XLA Ops:
  7.2 3.4 %copy-start.10 = (bf16[256,640]{1,0:T(8,128)(2,1)S(1)}, bf16[256,640]{1,0:T(8,128)(2,1)}, u32[]{:S(2)}) copy-start(bf16[256,640]{1,0:T(8,128)(2,1)} %param.12) | copy-start | bytes 983044
  7.2 3.6 %copy-start.11 = (bf16[256,640]{1,0:T(8,128)(2,1)S(1)}, bf16[256,640]{1,0:T(8,128)(2,1)}, u32[]{:S(2)}) copy-start(bf16[256,640]{1,0:T(8,128)(2,1)} %param.13) | copy-start | bytes 983044
  7.2 32.8 %copy-start.12 = (bf16[256,640]{1,0:T(8,128)(2,1)S(1)}, bf16[256,640]{1,0:T(8,128)(2,1)}, u32[]{:S(2)}) copy-start(bf16[256,640]{1,0:T(8,128)(2,1)} %param.14) | copy-start | bytes 983044
  7.2 58.7 %all-gather.2.cloned.1.call-start = ((), (), s32[]{:S(2)}) async-start(), calls=%async_computation | async-start | bytes 5898240 | tf_op jit(solution)/shard_map/all_gather | solution.py:30
  8.5 31.7 %copy-start.13 = (bf16[256,640]{1,0:T(8,128)(2,1)S(1)}, bf16[256,640]{1,0:T(8,128)(2,1)}, u32[]{:S(2)}) copy-start(bf16[256,640]{1,0:T(8,128)(2,1)} %param.19) | copy-start | bytes 983044
  11.0 30.9 %copy-start.1 = (bf16[256,640]{0,1:T(8,128)(2,1)}, bf16[256,640]{0,1:T(8,128)(2,1)S(1)}, u32[]{:S(2)}) copy-start(bf16[256,640]{0,1:T(8,128)(2,1)S(1)} %copy.39) | copy-start | bytes 983044
  23.2 17.9 %collective-permute-start = (f32[2,256]{1,0:T(2,128)S(1)}, f32[2,256]{1,0:T(2,128)S(1)}, u32[]{:S(2)}, u32[]{:S(2)}) collective-permute-start(f32[2,256]{1,0:T(2,128)S(1)} %pad_maximum_fusion.1), channel_id=1, source_target_pairs={{48,0},{52,4},{56,8},{60,12},{64,16},{68,20},{72,24},{76,28},{80,3... | collective-permute-start | bytes 6152 | tf_op jit(solution)/shard_map/ppermute | solution.py:24
  40.1 2.2 copy-start.6
  41.4 0.7 copy-start.7
  41.8 1.1 copy-start
  72.8 4.1 %copy-start.8 = (bf16[256,640]{0,1:T(8,128)(2,1)S(1)}, bf16[256,640]{0,1:T(8,128)(2,1)}, u32[]{:S(2)}) copy-start(bf16[256,640]{0,1:T(8,128)(2,1)} %copy-done.7) | copy-start | bytes 983044
  74.9 3.5 %copy-start.2 = (bf16[256,640]{0,1:T(8,128)(2,1)S(1)}, bf16[256,640]{0,1:T(8,128)(2,1)}, u32[]{:S(2)}) copy-start(bf16[256,640]{0,1:T(8,128)(2,1)} %copy-done.1) | copy-start | bytes 983044
  78.3 0.9 copy-start.4
  79.2 129.7 %copy-start.9 = (bf16[5,256,128]{1,2,0:T(8,128)(2,1)S(1)}, bf16[5,256,128]{1,2,0:T(8,128)(2,1)}, u32[]{:S(2)}) copy-start(bf16[5,256,128]{1,2,0:T(8,128)(2,1)} %get-tuple-element.171) | copy-start | bytes 983044
  79.2 132.4 %copy-start.3 = (bf16[256,640]{0,1:T(8,128)(2,1)S(1)}, bf16[256,640]{0,1:T(8,128)(2,1)}, u32[]{:S(2)}) copy-start(bf16[256,640]{0,1:T(8,128)(2,1)} %copy-done.1) | copy-start | bytes 983044
  79.2 132.4 %copy-start.5 = (f32[5,128,256]{2,1,0:T(8,128)S(1)}, f32[5,128,256]{2,1,0:T(8,128)}, u32[]{:S(2)}) copy-start(f32[5,128,256]{2,1,0:T(8,128)} %copy-done.4) | copy-start | bytes 1966084
  199.8 11.8 %collective-permute-start.1 = (f32[2,256]{1,0:T(2,128)S(1)}, f32[2,256]{1,0:T(2,128)S(1)}, u32[]{:S(2)}, u32[]{:S(2)}) collective-permute-start(f32[2,256]{1,0:T(2,128)S(1)} %pad_maximum_fusion.2), channel_id=1, source_target_pairs={{48,0},{52,4},{56,8},{60,12},{64,16},{68,20},{72,24},{76,28},{80,3... | collective-permute-start | bytes 6152 | tf_op jit(solution)/shard_map/ppermute | solution.py:24
Sparse Core Ops, SparseCore 0:
  10.7 55.1 all-gather.1
where the time goes:
time: 222 us
  blocking collectives  130 us (59%)
  waiting for transfers between devices  23.6 us (11%)
  starting transfers between devices  21.6 us (10%)
  local copies, waits for them, and re-layouts  17.9 us (8%)
  between operations  14.4 us (6%)
  other arithmetic  7.06 us (3%)
  matrix products  6.86 us (3%)
    psum x4, blocking collectives, one_axis_at_a_time(): x = lax.psum(x, axis)  97.7 us
    all_gather x1, waiting for transfers between devices, side_by_side(): out = lax.all_gather(both, axis, axis=dim, tiled=True)  21.8 us
    ppermute x2, starting transfers between devices, shifted(): return lax.ppermute(block, axis, route)  21.5 us
    psum x1, blocking collectives, on_device(): lax.psum((jnp.sum(q_full * flat_q, axis=1), jnp.sum(k_full * flat_k, axis...  20.7 us
    psum x1, blocking collectives, on_device(): lax.psum((jnp.sum(q_full * q_full, axis=1), jnp.sum(k_full * k_full, axis...  12 us
    unnamed x38, local copies, waits for them, and re-layouts  8.84 us
    split x1, local copies, waits for them, and re-layouts, side_by_side(): jnp.split(out, [sum(widths[:k]) for k in range(1, len(widths))], axis=along)  4.7 us
  transfers between devices with their start and end apart: 3, of which 2 were waited for; matrix products, arithmetic and copies ran while one was open for 4% of the time, Pallas kernels for 0%

commit v1 on v0

--- a/solution.py
+++ b/solution.py
@@ -8,20 +8,17 @@
 
 D = 5120
 DH = 128
-FRAME = ("frame_0", "frame_1")
-FSDP = ("fsdp_0", "fsdp_1")
-FRAME_FSDP_HEAD = ("frame_0", "frame_1", "fsdp_0", "fsdp_1", "head")
-FSDP_HEAD = ("fsdp_0", "fsdp_1", "head")
+FRAME = ("x", "core")
+FSDP_HEAD = ("half", "video_z", "video_y", "head")
+HALF_HEAD = ("half", "head")
+FRAMES = 8
+VIDEOS = 12
+HEAD_PARTS = 4
+COLUMN_PARTS = 2 * HEAD_PARTS
 
 
 EPSILON = 1e-06
 MASKED = -1e30
-
-
-def shifted(block, axis, distance):
-    devices = range(lax.axis_size(axis))
-    route = [((i - distance) % len(devices), i) for i in devices]
-    return lax.ppermute(block, axis, route)
 
 
 def side_by_side(arrays, axis, dim, along):
@@ -31,10 +28,8 @@
     return tuple(jnp.split(out, [sum(widths[:k]) for k in range(1, len(widths))], axis=along))
 
 
-def one_axis_at_a_time(x, axes):
-    for axis in axes:
-        x = lax.psum(x, axis)
-    return x
+def from_all(x, axes, devices):
+    return lax.all_to_all(jnp.broadcast_to(x[None], (devices,) + x.shape), axes, 0, 0)
 
 
 def project(left_side, right_side):
@@ -50,22 +45,14 @@
     scaling = 1.0 / math.sqrt(DH)
     own_frame = lax.axis_index(FRAME)
     own_start = own_frame * length
-    pair_reach = lax.axis_size(FSDP) // 2
-    half_index = lax.axis_index(FSDP) // pair_reach
-    column_start = (half_index * lax.axis_size("head") + lax.axis_index("head")) * width_dev
+    column_start = lax.axis_index(HALF_HEAD) * width_dev
     gain_q = lax.dynamic_slice_in_dim(gain_query, column_start, width_dev)
     gain_k = lax.dynamic_slice_in_dim(gain_key, column_start, width_dev)
 
-    def with_partner(stats):
-        other = shifted(stats, FSDP, pair_reach)
-        return stats + other
-
     q_full = queries.astype(jnp.float32)
     k_full = noisy_keys.astype(jnp.float32)
-    squares_q, squares_k = lax.psum(
-        (jnp.sum(q_full * q_full, axis=1), jnp.sum(k_full * k_full, axis=1)), "head"
-    )
-    squares = with_partner(jnp.stack([squares_q, squares_k]))
+    squares = jnp.stack([jnp.sum(q_full * q_full, axis=1), jnp.sum(k_full * k_full, axis=1)])
+    squares = jnp.sum(from_all(squares, HALF_HEAD, COLUMN_PARTS), axis=0)
     rate_q = lax.rsqrt(squares[0] / D + EPSILON)
     rate_k = lax.rsqrt(squares[1] / D + EPSILON)
     normed_q = (
@@ -167,31 +154,32 @@
     plain_k = grad_kn.reshape(length, width_dev)
     flat_q = plain_q * gain_q
     flat_k = plain_k * gain_k
-    inner_q, inner_k = lax.psum(
-        (jnp.sum(q_full * flat_q, axis=1), jnp.sum(k_full * flat_k, axis=1)), "head"
-    )
-    inners = with_partner(jnp.stack([inner_q, inner_k]))
+    inners = jnp.stack([jnp.sum(q_full * flat_q, axis=1), jnp.sum(k_full * flat_k, axis=1)])
+    part_q = jnp.sum(plain_q * q_full * rate_q[:, None], axis=0)
+    part_k = jnp.sum(plain_k * k_full * rate_k[:, None], axis=0)
+    piece_width = width_dev // FRAMES
+    pieces = jnp.stack([part_q.reshape(FRAMES, piece_width), part_k.reshape(FRAMES, piece_width)], axis=1)
+    piece = jnp.sum(lax.all_to_all(pieces, FRAME, 0, 0), axis=0)
+    sent = jnp.concatenate([inners.reshape(2 * length), piece.reshape(2 * piece_width)])
+    got = from_all(sent, FSDP_HEAD, 2 * VIDEOS * HEAD_PARTS).reshape(2, VIDEOS, HEAD_PARTS, sent.shape[0])
+    video = lax.axis_index(("video_z", "video_y"))
+    same_video = lax.dynamic_index_in_dim(got[:, :, :, : 2 * length], video, 1, keepdims=False)
+    inners = jnp.sum(same_video, axis=(0, 1)).reshape(2, length)
+    gains = jnp.sum(got[:, :, :, 2 * length :], axis=1)
+    gains = from_all(gains.reshape(COLUMN_PARTS * 2 * piece_width), FRAME, FRAMES)
+    gains = gains.reshape(FRAMES, COLUMN_PARTS, 2, piece_width).transpose(2, 1, 0, 3).reshape(2, D)
     cube_q = rate_q * rate_q * rate_q * inners[0] / D
     cube_k = rate_k * rate_k * rate_k * inners[1] / D
     grad_queries = (rate_q[:, None] * flat_q - q_full * cube_q[:, None]).astype(jnp.bfloat16)
     grad_keys = (rate_k[:, None] * flat_k - k_full * cube_k[:, None]).astype(jnp.bfloat16)
-    part_q = jnp.sum(plain_q * q_full * rate_q[:, None], axis=0)
-    part_k = jnp.sum(plain_k * k_full * rate_k[:, None], axis=0)
-    blank = jnp.zeros((D,), jnp.float32)
-    spread_q = lax.dynamic_update_slice_in_dim(blank, part_q, column_start, 0)
-    spread_k = lax.dynamic_update_slice_in_dim(blank, part_k, column_start, 0)
-    grad_gain_query, grad_gain_key = (
-        one_axis_at_a_time(spread_q, FRAME_FSDP_HEAD),
-        one_axis_at_a_time(spread_k, FRAME_FSDP_HEAD),
-    )
     grad_values = grad_vv.reshape(length, width_dev).astype(jnp.bfloat16)
-    return (attended, grad_queries, grad_keys, grad_values, grad_gain_query, grad_gain_key)
+    return (attended, grad_queries, grad_keys, grad_values, gains[0], gains[1])
 
 
 def solution(mesh):
     torus = Mesh(
-        mesh.devices.reshape(4, 2, 12, 2, mesh.shape["head"]),
-        ("frame_0", "frame_1", "fsdp_0", "fsdp_1", "head"),
+        mesh.devices.reshape(4, 2, 2, 6, 2, HEAD_PARTS),
+        ("x", "core", "half", "video_z", "video_y", "head"),
     )
     in_specs = (
         P(FRAME, FSDP_HEAD),

time: 222 us -> 175 us (0.79)
  the two profiles are of different devices: /device:TPU:8 before, /device:TPU:1 now
where the time goes in v1:
time: 175 us; the launch traced here: 174 us
  starting transfers between devices  48 us (27%)
  waiting for transfers between devices  47.2 us (27%)
  matrix products  30.5 us (17%)
  local copies, waits for them, and re-layouts  23.3 us (13%)
  between operations  14.4 us (8%)
  other arithmetic  10.6 us (6%)
    all_to_all x3, starting transfers between devices, from_all(): lax.all_to_all(jnp.broadcast_to(x[None], (devices,) + x.shape), axes, 0, 0)  43.7 us
    all_to_all x3, waiting for transfers between devices, from_all(): lax.all_to_all(jnp.broadcast_to(x[None], (devices,) + x.shape), axes, 0, 0)  24.4 us
    all_gather x1, waiting for transfers between devices, side_by_side(): out = lax.all_gather(both, axis, axis=dim, tiled=True)  18.2 us
    unnamed x41, local copies, waits for them, and re-layouts  10.8 us
    dot_general x1, matrix products, attend_back(): jnp.einsum('hqk,khd->qhd', weighted, reflect_key_piece, preferred_element...  10.3 us
    dot_general x4, matrix products, project(): jnp.einsum('qhd,khd->hqk', left_side, right_side, preferred_element_type=...  9.84 us
    dot_general x1, matrix products, attend(): jnp.einsum('hqk,khd->hqd', exponent.astype(jnp.bfloat16), value_piece, pr...  5.36 us
    split x1, local copies, waits for them, and re-layouts, side_by_side(): jnp.split(out, [sum(widths[:k]) for k in range(1, len(widths))], axis=along)  4.7 us
  transfers between devices with their start and end apart: 5, of which 5 were waited for; matrix products, arithmetic and copies ran while one was open for 8% of the time, Pallas kernels for 0%

profile of v1, /device:TPU:1, one launch (start us, length us, event | category | flops | bytes accessed | tf_op | source)
XLA Modules:
  0.0 174.2 jit_solution(2458660859537356967)
XLA Ops:
  7.2 1.2 copy.164
  8.5 1.2 copy.165
  9.7 0.9 pad_maximum_fusion
  11.2 0.6 broadcast_in_dim.34
  11.8 20.3 %all-to-all-start = ((f32[8,2,256]{2,1,0:T(2,128)}), f32[8,2,256]{2,1,0:T(2,128)S(1)}, u32[]{:S(2)}, u32[]{:S(2)}) async-start(f32[8,2,256]{2,1,0:T(2,128)} %broadcast_in_dim.34), calls=%async_computation | async-start | bytes 32768 | tf_op jit(solution)/shard_map/all_to_all | solution.py:32
  32.2 0.8 dynamic_slice.10
  32.9 0.8 dynamic_slice.11
  33.9 0.9 copy.170
  34.8 11.1 %all-to-all-done = f32[8,2,256]{2,1,0:T(2,128)S(1)} async-done(((f32[8,2,256]{2,1,0:T(2,128)}), f32[8,2,256]{2,1,0:T(2,128)S(1)}, u32[]{:S(2)}, u32[]{:S(2)}) %all-to-all-start) | async-done | bytes 16416 | tf_op jit(solution)/shard_map/all_to_all | solution.py:32
  46.3 0.4 fusion.67
  46.7 0.3 copy-done.9
  47.2 0.6 copy-done
  47.8 1.3 fusion.35
  49.0 18.2 %all-gather.2.cloned.1.call-done = bf16[2048,1280]{0,1:T(8,128)(2,1)} async-done(((bf16[256,1280]{0,1:T(8,128)(2,1)}), bf16[2048,1280]{0,1:T(8,128)(2,1)}) %all-gather.2.cloned.1.call-update) | async-done | bytes 5242896 | tf_op jit(solution)/shard_map/all_gather | solution.py:27
  67.3 4.7 %fusion.65 = (bf16[2048,640]{0,1:T(8,128)(2,1)}, bf16[2048,640]{0,1:T(8,128)(2,1)S(1)}) fusion(bf16[2048,1280]{0,1:T(8,128)(2,1)} %all-gather.2.cloned.1.call-done), kind=kLoop, calls=%fused_computation.104 | loop fusion | bytes 10485760 | tf_op jit(solution)/shard_map/split | solution.py:28
  72.0 9.5 %conditional.2 = (f32[5,256]{1,0:T(8,128)S(1)}, f32[5,256,128]{2,1,0:T(8,128)}, f32[5,256]{1,0:T(8,128)S(1)}) conditional(s32[]{:T(128)} %convert_element_type.56, (f32[5,256]{1,0:T(8,128)S(1)}, f32[5,256]{1,0:T(8,128)S(1)}, f32[5,256,128]{2,1,0:T(8,128)}) %tuple.41, (s32[]{:T(128)}, bf16[256,5,128]{0,2,1:T(8,128)(2,1)S(1)}, ...), branch_computations={%region_5.0_spmd.clone, %region_6.9_spmd.clone} | conditional | flops 1371361792 | bytes 38428700 | solution.py:111
  72.0 1.9 %fusion.13 = (f32[5,256]{1,0:T(8,128)S(1)}, f32[5,256,2048]{2,1,0:T(8,128)S(1)}) fusion(pred[2048]{0:T(1024)(128)(4,1)S(1)} %fusion.22, bf16[256,5,128]{0,2,1:T(8,128)(2,1)S(1)} %get-tuple-element.207, bf16[2048,5,128]{0,2,1:T(8,128)(2,1)S(1)} %get-tuple-element.208), kind=kOutput, calls=%fused_computation.19 | convolution fusion | flops 678951680 | bytes 13442048 | tf_op jit(solution)/shard_map/cond/branch_1_fun/qhd,khd->hqk/dot_general | solution.py:36
  73.9 2.2 %fusion.15 = f32[5,256]{1,0:T(8,128)S(1)} fusion(f32[5,256,2048]{2,1,0:T(8,128)S(1)} %get-tuple-element.237, f32[5,256]{1,0:T(8,128)S(1)} %max.3, pred[2048]{0:T(1024)(128)(4,1)S(1)} %fusion.22), kind=kLoop, calls=%fused_computation.21 | loop fusion | flops 10484480 | bytes 10498048 | tf_op jit(solution)/shard_map/cond/branch_1_fun/reduce_sum | solution.py:107
  76.2 5.4 %fusion.19 = f32[5,256,128]{2,1,0:T(8,128)} fusion(bf16[2048,5,128]{0,2,1:T(8,128)(2,1)} %get-tuple-element.212, f32[5,256,2048]{2,1,0:T(8,128)S(1)} %get-tuple-element.237, f32[5,256]{1,0:T(8,128)S(1)} %max.3, pred[2048]{0:T(1024)(128)(4,1)S(1)} %fusion.22, f32[5,256,128]{2,1,0:T(8,128)} %get-tuple-element.104, f32[5,256]{1,0:T(8,128)S(1)} %get-tuple-element.235), kind=kOutput, calls=%fused_computation.24 | convolution fusion | flops 681902080 | bytes 14430208 | tf_op jit(solution)/shard_map/cond/branch_1_fun/hqk,khd->hqd/dot_general | solution.py:99
  81.5 2.2 %copy.169 = f32[5,256,128]{1,2,0:T(8,128)} copy(f32[5,256,128]{2,1,0:T(8,128)} %get-tuple-element.228) | data formatting | bytes 1310720 | tf_op jit(solution)/shard_map/cond | solution.py:111
  83.7 2.1 %fusion.53 = (f32[5,256]{1,0:T(8,128)S(1)}, bf16[5,256,128]{1,2,0:T(8,128)(2,1)}) fusion(bf16[256,5,128]{0,2,1:T(8,128)(2,1)} %bitcast.73, f32[5,256,128]{1,2,0:T(8,128)} %copy.169, f32[5,256]{1,0:T(8,128)S(1)} %get-tuple-element.227), kind=kLoop, calls=%fused_computation.80 | loop fusion | flops 817920 | bytes 1320960 | tf_op jit(solution)/shard_map/reduce_sum | solution.py:117
  85.8 2.0 %fusion.29 = bf16[5,256,256]{1,2,0:T(8,128)(2,1)S(1)} fusion(bf16[256,5,128]{0,2,1:T(8,128)(2,1)} %bitcast.74, bf16[256,5,128]{0,2,1:T(8,128)(2,1)} %bitcast.78, f32[5,256,256]{1,2,0:T(8,128)} %copy-done, f32[5,256]{1,0:T(8,128)S(1)} %get-tuple-element.266, f32[5,256]{1,0:T(8,128)S(1)} %log_add_fusion), kind=kOutput, calls=%fused_computation.40 | convolution fusion | flops 85196800 | bytes 2631680 | tf_op jit(solution)/shard_map/qhd,khd->hqk/dot_general | solution.py:36
  87.7 1.1 fusion.30
  88.9 0.4 convolution_multiply_fusion.1
  89.2 0.4 fusion.48
  89.6 0.5 copy-done.5
  90.2 16.1 %conditional.3 = (f32[256,640]{0,1:T(8,128)}) conditional(s32[]{:T(128)} %convert_element_type.56, f32[256,5,128]{0,2,1:T(8,128)} %fusion.30, (s32[]{:T(128)}, bf16[256,5,128]{0,2,1:T(8,128)(2,1)S(1)}, bf16[2048,5,128]{0,2,1:T(8,128)(2,1)S(1)}, f32[5,256]{1,0:T(8,128)S(1)}, bf16[256,5,128]{0,2,1:T(8,128)(2,1)}, ...), branch_computations={%region_10.11_spmd, %region_11.12_spmd} | conditional | flops 2029340672 | bytes 30816268 | solution.py:152
  90.4 5.5 %fusion.68 = f32[5,256,2048]{2,1,0:T(8,128)} fusion(bf16[256,5,128]{0,2,1:T(8,128)(2,1)S(1)} %get-tuple-element.214, bf16[2048,5,128]{0,2,1:T(8,128)(2,1)S(1)} %get-tuple-element.70), kind=kOutput, calls=%fused_computation.107 | convolution fusion | flops 671088640 | bytes 13434880 | tf_op jit(solution)/shard_map/cond/branch_1_fun/qhd,khd->hqk/dot_general | solution.py:36
  95.9 10.3 %fusion.6 = f32[256,5,128]{0,2,1:T(8,128)} fusion(f32[256,5,128]{0,2,1:T(8,128)} %get-tuple-element.67, bf16[2048,5,128]{0,2,1:T(8,128)(2,1)S(1)} %get-tuple-element.70, f32[5,256,2048]{2,1,0:T(8,128)} %fusion.68, f32[5,256]{1,0:T(8,128)S(1)} %get-tuple-element.74, f32[5,256]{1,0:T(8,128)S(1)} %get-tuple-element.71, pred[2048]{0:T(1024)(128)(4,1)S(1)} %fusion.7, ...), kind=kOutput, calls=%fused_computation.6 | convolution fusion | flops 1358233600 | bytes 17379328 | tf_op jit(solution)/shard_map/cond/branch_1_fun/hqk,khd->qhd/dot_general | solution.py:146
  106.3 1.6 fusion.40
  107.9 0.6 pad_maximum_fusion.1
  108.5 4.2 %all-to-all-start.1 = ((f32[8,2,80]{2,1,0:T(2,128)}), f32[8,2,80]{2,1,0:T(2,128)S(1)}, u32[]{:S(2)}, u32[]{:S(2)}) async-start(f32[8,2,80]{2,1,0:T(2,128)} %pad_maximum_fusion.1), calls=%async_computation.1 | async-start | bytes 16384 | tf_op jit(solution)/shard_map/all_to_all | solution.py:162
  112.8 4.6 %all-to-all-done.1 = f32[8,2,80]{2,1,0:T(2,128)S(1)} async-done(((f32[8,2,80]{2,1,0:T(2,128)}), f32[8,2,80]{2,1,0:T(2,128)S(1)}, u32[]{:S(2)}, u32[]{:S(2)}) %all-to-all-start.1) | async-done | bytes 5152 | tf_op jit(solution)/shard_map/all_to_all | solution.py:162
  117.5 0.9 broadcast_in_dim.35
  118.3 16.7 %all-to-all-start.2 = ((f32[96,1,672]{2,1,0:T(1,128)}), f32[96,1,672]{2,1,0:T(1,128)}, u32[]{:S(2)}, u32[]{:S(2)}) async-start(f32[96,1,672]{2,1,0:T(1,128)} %broadcast_in_dim.35), calls=%async_computation.2 | async-start | bytes 589824 | tf_op jit(solution)/shard_map/all_to_all | solution.py:32
  135.1 2.2 %convolution_convert_fusion = bf16[5,256,128]{1,2,0:T(8,128)(2,1)} fusion(bf16[256,5,128]{0,2,1:T(8,128)(2,1)} %bitcast.76, f32[5,256,256]{1,2,0:T(8,128)S(1)} %copy-done.1, f32[5,256]{1,0:T(8,128)S(1)} %log_add_fusion), kind=kOutput, calls=%fused_computation.56 | convolution fusion | flops 84705280 | bytes 1971200 | tf_op jit(solution)/shard_map/hqk,qhd->khd/dot_general | solution.py:129
  137.3 1.9 %copy.186 = bf16[256,640]{1,0:T(8,128)(2,1)} copy(bf16[256,640]{0,1:T(8,128)(2,1)} %bitcast.82) | data formatting | bytes 655360
  139.2 1.9 %copy.183 = bf16[256,640]{1,0:T(8,128)(2,1)} copy(bf16[256,640]{0,1:T(8,128)(2,1)} %bitcast.81) | data formatting | bytes 655360
  141.1 10.6 %all-to-all-done.2 = f32[96,1,672]{2,1,0:T(1,128)} async-done(((f32[96,1,672]{2,1,0:T(1,128)}), f32[96,1,672]{2,1,0:T(1,128)}, u32[]{:S(2)}, u32[]{:S(2)}) %all-to-all-start.2) | async-done | bytes 258080 | tf_op jit(solution)/shard_map/all_to_all | solution.py:32
  151.6 1.7 reduce.1
  153.6 0.6 broadcast_in_dim.37
  154.2 6.7 %all-to-all-start.3 = ((f32[8,1,1280]{2,1,0:T(1,128)}), f32[8,1,1280]{2,1,0:T(1,128)S(1)}, u32[]{:S(2)}, u32[]{:S(2)}) async-start(f32[8,1,1280]{2,1,0:T(1,128)} %broadcast_in_dim.37), calls=%async_computation.3 | async-start | bytes 81920 | tf_op jit(solution)/shard_map/all_to_all | solution.py:32
  160.9 0.3 fusion.44
  161.2 0.9 copy.184
  162.1 0.9 copy.185
  163.0 2.7 %all-to-all-done.3 = f32[8,1,1280]{2,1,0:T(1,128)S(1)} async-done(((f32[8,1,1280]{2,1,0:T(1,128)}), f32[8,1,1280]{2,1,0:T(1,128)S(1)}, u32[]{:S(2)}, u32[]{:S(2)}) %all-to-all-start.3) | async-done | bytes 40992 | tf_op jit(solution)/shard_map/all_to_all | solution.py:32
  166.0 0.7 squeeze.7
  166.7 0.7 squeeze.6
  (64 shorter events, 2.3 us)
Async XLA Ops:
  7.2 3.4 %copy-start.11 = (bf16[256,640]{1,0:T(8,128)(2,1)S(1)}, bf16[256,640]{1,0:T(8,128)(2,1)}, u32[]{:S(2)}) copy-start(bf16[256,640]{1,0:T(8,128)(2,1)} %param.12) | copy-start | bytes 983044
  7.2 3.6 %copy-start.12 = (bf16[256,640]{1,0:T(8,128)(2,1)S(1)}, bf16[256,640]{1,0:T(8,128)(2,1)}, u32[]{:S(2)}) copy-start(bf16[256,640]{1,0:T(8,128)(2,1)} %param.13) | copy-start | bytes 983044
  7.2 26.5 %copy-start.13 = (bf16[256,640]{1,0:T(8,128)(2,1)S(1)}, bf16[256,640]{1,0:T(8,128)(2,1)}, u32[]{:S(2)}) copy-start(bf16[256,640]{1,0:T(8,128)(2,1)} %param.14) | copy-start | bytes 983044
  7.2 60.1 %all-gather.2.cloned.1.call-start = ((), (), s32[]{:S(2)}) async-start(), calls=%async_computation.4 | async-start | bytes 5898240 | tf_op jit(solution)/shard_map/all_gather | solution.py:27
  8.5 25.4 %copy-start.14 = (bf16[256,640]{1,0:T(8,128)(2,1)S(1)}, bf16[256,640]{1,0:T(8,128)(2,1)}, u32[]{:S(2)}) copy-start(bf16[256,640]{1,0:T(8,128)(2,1)} %param.19) | copy-start | bytes 983044
  11.0 35.7 %copy-start.2 = (bf16[256,640]{0,1:T(8,128)(2,1)}, bf16[256,640]{0,1:T(8,128)(2,1)S(1)}, u32[]{:S(2)}) copy-start(bf16[256,640]{0,1:T(8,128)(2,1)S(1)} %copy.157) | copy-start | bytes 983044
  11.8 34.1 %all-to-all-start = ((f32[8,2,256]{2,1,0:T(2,128)}), f32[8,2,256]{2,1,0:T(2,128)S(1)}, u32[]{:S(2)}, u32[]{:S(2)}) async-start(f32[8,2,256]{2,1,0:T(2,128)} %broadcast_in_dim.34), calls=%async_computation | async-start | bytes 32768 | tf_op jit(solution)/shard_map/all_to_all | solution.py:32
  33.9 13.3 %copy-start.8 = (bf16[256,640]{0,1:T(8,128)(2,1)}, bf16[256,640]{0,1:T(8,128)(2,1)S(1)}, u32[]{:S(2)}) copy-start(bf16[256,640]{0,1:T(8,128)(2,1)S(1)} %copy.161) | copy-start | bytes 983044
  46.3 0.7 copy-start.9
  46.7 1.1 copy-start
  83.7 4.1 %copy-start.10 = (bf16[256,640]{0,1:T(8,128)(2,1)S(1)}, bf16[256,640]{0,1:T(8,128)(2,1)}, u32[]{:S(2)}) copy-start(bf16[256,640]{0,1:T(8,128)(2,1)} %copy-done.9) | copy-start | bytes 983044
  85.8 3.5 %copy-start.3 = (bf16[256,640]{0,1:T(8,128)(2,1)S(1)}, bf16[256,640]{0,1:T(8,128)(2,1)}, u32[]{:S(2)}) copy-start(bf16[256,640]{0,1:T(8,128)(2,1)} %copy-done.2) | copy-start | bytes 983044
  89.2 0.9 copy-start.5
  106.3 28.9 %copy-start.1 = (f32[5,256,256]{1,2,0:T(8,128)S(1)}, f32[5,256,256]{1,2,0:T(8,128)}, u32[]{:S(2)}) copy-start(f32[5,256,256]{1,2,0:T(8,128)} %copy-done) | copy-start | bytes 3932164
  108.5 8.8 %all-to-all-start.1 = ((f32[8,2,80]{2,1,0:T(2,128)}), f32[8,2,80]{2,1,0:T(2,128)S(1)}, u32[]{:S(2)}, u32[]{:S(2)}) async-start(f32[8,2,80]{2,1,0:T(2,128)} %pad_maximum_fusion.1), calls=%async_computation.1 | async-start | bytes 16384 | tf_op jit(solution)/shard_map/all_to_all | solution.py:162
  118.3 33.3 %all-to-all-start.2 = ((f32[96,1,672]{2,1,0:T(1,128)}), f32[96,1,672]{2,1,0:T(1,128)}, u32[]{:S(2)}, u32[]{:S(2)}) async-start(f32[96,1,672]{2,1,0:T(1,128)} %broadcast_in_dim.35), calls=%async_computation.2 | async-start | bytes 589824 | tf_op jit(solution)/shard_map/all_to_all | solution.py:32
  135.1 25.8 %copy-start.4 = (bf16[256,640]{0,1:T(8,128)(2,1)S(1)}, bf16[256,640]{0,1:T(8,128)(2,1)}, u32[]{:S(2)}) copy-start(bf16[256,640]{0,1:T(8,128)(2,1)} %copy-done.2) | copy-start | bytes 983044
  135.1 25.8 %copy-start.6 = (f32[5,128,256]{2,1,0:T(8,128)S(1)}, f32[5,128,256]{2,1,0:T(8,128)}, u32[]{:S(2)}) copy-start(f32[5,128,256]{2,1,0:T(8,128)} %copy-done.5) | copy-start | bytes 1966084
  135.1 25.8 %copy-start.7 = (f32[256,640]{0,1:T(8,128)S(1)}, f32[256,640]{0,1:T(8,128)}, u32[]{:S(2)}) copy-start(f32[256,640]{0,1:T(8,128)} %get-tuple-element.92) | copy-start | bytes 1966084
  154.2 11.4 %all-to-all-start.3 = ((f32[8,1,1280]{2,1,0:T(1,128)}), f32[8,1,1280]{2,1,0:T(1,128)S(1)}, u32[]{:S(2)}, u32[]{:S(2)}) async-start(f32[8,1,1280]{2,1,0:T(1,128)} %broadcast_in_dim.37), calls=%async_computation.3 | async-start | bytes 81920 | tf_op jit(solution)/shard_map/all_to_all | solution.py:32
Sparse Core Ops, SparseCore 0:
  10.7 56.5 all-gather.1

commit v2 on v1

v2 whole, which is shorter than its diff:
```python
import functools
import math

import jax
import jax.numpy as jnp
from jax import lax
from jax.experimental import pallas as pl
from jax.experimental.pallas import tpu as pltpu
from jax.sharding import Mesh
from jax.sharding import PartitionSpec as P

D = 5120
DH = 128
FRAME = ("x", "core")
FSDP_HEAD = ("half", "video_z", "video_y", "head")
HALF_HEAD = ("half", "head")
FRAMES = 8
VIDEOS = 12
HEAD_PARTS = 4
COLUMN_PARTS = 2 * HEAD_PARTS
EPSILON = 1e-06
MASKED = -1e30
SCALING = 1.0 / math.sqrt(DH)
LOG2E = math.log2(math.e)
NT = ((1,), (1,))
NN = ((1,), (0,))
TN = ((0,), (0,))
KEY_BLOCKS = 11
BLOCKS_USED = (1, 3, 7, 11)


def from_all(x, axes, devices):
    return lax.all_to_all(jnp.broadcast_to(x[None], (devices,) + x.shape), axes, 0, 0)


def other_core(block):
    return lax.ppermute(block, "core", [(0, 1), (1, 0)])


def gather_before(block):
    rows = block.shape[0] // 2
    near = lax.ppermute(block, "x", [(0, 1), (1, 2), (2, 3)])
    far_high = lax.ppermute(block[rows:], "x", [(0, 3), (1, 0)])
    far_low = lax.ppermute(block[:rows], "x", [(0, 3)])
    sibling = lax.ppermute(block, "core", [(0, 1)])
    middle_high = lax.ppermute(far_high, "x", [(0, 3), (3, 2)])
    onward = jnp.where(lax.axis_index("x") == 3, far_low, near[:rows])
    middle_low = lax.ppermute(onward, "x", [(2, 3), (3, 2)])
    halves = [far_high, far_low, middle_high, middle_low]
    near_other = other_core(near)
    others = [other_core(half) for half in halves]
    return [sibling, near, near_other, halves[2], others[2], halves[3], others[3], halves[0], others[0], halves[1], others[1]]


def dot(a, b, dims):
    return lax.dot_general(a, b, (dims, ((), ())), preferred_element_type=jnp.float32)


NT = ((1,), (1,))
NN = ((1,), (0,))
TN = ((0,), (0,))


def column(row):
    return jnp.transpose(jnp.broadcast_to(row, (8, row.shape[1])))[:, :1]


def attention_kernel(where_ref, squares_ref, gain_q_ref, gain_k_ref, q_ref, k_ref, v_ref, do_ref, *refs):
    pairs = refs[:KEY_BLOCKS]
    att_ref, flat_q_ref, flat_k_ref, gv_ref, inner_ref, part_ref, expo_ref, sum_q_ref, sum_k_ref = refs[KEY_BLOCKS:]
    rows, width = q_ref.shape
    rates = lax.rsqrt(jnp.sum(squares_ref[...], axis=0, keepdims=True) / D + EPSILON)
    rate_q, rate_k = column(rates[:, :rows]), column(rates[:, rows:])
    own_x, own_core = where_ref[0], where_ref[1]
    sum_q_ref[...] = jnp.zeros_like(sum_q_ref)
    sum_k_ref[...] = jnp.zeros_like(sum_k_ref)

    def one_head(remote, start):
        lanes = pl.ds(pl.multiple_of(start, DH), DH)
        value_lanes = pl.ds(pl.multiple_of(start + width, DH), DH)
        gain_q, gain_k = gain_q_ref[:, lanes], gain_k_ref[:, lanes]
        q_full, k_full = q_ref[:, lanes].astype(jnp.float32), k_ref[:, lanes].astype(jnp.float32)
        normed_q = (q_full * rate_q * gain_q).astype(jnp.bfloat16)
        normed_k = (k_full * rate_k * gain_k).astype(jnp.bfloat16)
        value, do = v_ref[:, lanes], do_ref[:, lanes]
        used = BLOCKS_USED[remote]
        starts = [0]
        for b in range(used):
            starts.append(starts[-1] + (rows if b == 0 else pairs[b - 1].shape[0]))
        starts.append(starts[-1] + pairs[used - 1].shape[0])
        key_of = lambda b: normed_k if b == 0 else pairs[b - 1][:, lanes]
        value_of = lambda b: value if b == 0 else pairs[b - 1][:, value_lanes]
        held = lambda b: slice(starts[b], starts[b + 1])
        top = None
        for b in range(1 + used):
            scores = dot(key_of(b), normed_q, NT)
            if b == 1:
                scores = jnp.where(own_core == 1, scores, MASKED)
            expo_ref[held(b), :] = scores
            highest = jnp.max(scores, axis=0, keepdims=True)
            top = highest if top is None else jnp.maximum(top, highest)
        shift = top * (SCALING * LOG2E)
        total = jnp.zeros_like(top)
        out = jnp.zeros((DH, rows), jnp.float32)
        for b in range(1 + used):
            expo = jnp.exp2(expo_ref[held(b), :] * (SCALING * LOG2E) - shift)
            expo_ref[held(b), :] = expo
            total += jnp.sum(expo, axis=0, keepdims=True)
            out += dot(value_of(b), expo.astype(jnp.bfloat16), TN)
        inverse = 1.0 / total
        out = out * inverse
        att_ref[:, lanes] = jnp.transpose(out).astype(jnp.bfloat16)
        delta = jnp.sum(jnp.transpose(do.astype(jnp.float32)) * out, axis=0, keepdims=True)
        grad_q = jnp.zeros((DH, rows), jnp.float32)
        for b in range(1, 1 + used):
            grad_probs = dot(value_of(b), do, NT)
            weighted = (expo_ref[held(b), :] * (grad_probs - delta)).astype(jnp.bfloat16)
            grad_q += dot(key_of(b), weighted, TN)
        probs = expo_ref[held(0), :] * inverse
        weighted = (probs * (dot(value, do, NT) - delta)).astype(jnp.bfloat16)
        grad_q = (grad_q * inverse + dot(normed_k, weighted, TN)) * SCALING
        grad_k = dot(weighted, normed_q, NN) * SCALING
        gv_ref[:, lanes] = dot(probs.astype(jnp.bfloat16), do, NN).astype(jnp.bfloat16)
        plain_q = jnp.transpose(grad_q)
        flat_q, flat_k = plain_q * gain_q, grad_k * gain_k
        flat_q_ref[:, lanes] = flat_q
        flat_k_ref[:, lanes] = flat_k
        part_ref[0:1, lanes] = jnp.sum(plain_q * q_full * rate_q, axis=0, keepdims=True)
        part_ref[1:2, lanes] = jnp.sum(grad_k * k_full * rate_k, axis=0, keepdims=True)
        sum_q_ref[...] += q_full * flat_q
        sum_k_ref[...] += k_full * flat_k

    def run(remote):
        @pl.loop(0, width, step=DH)
        def _(start):
            one_head(remote, start)

    for remote in range(4):
        pl.when(own_x == remote)(functools.partial(run, remote))
    inner_ref[0:1, :] = jnp.sum(jnp.transpose(sum_q_ref[...]), axis=0, keepdims=True)
    inner_ref[1:2, :] = jnp.sum(jnp.transpose(sum_k_ref[...]), axis=0, keepdims=True)


def attention(where, squares, gain_q, gain_k, queries, noisy_keys, noisy_values, out_grad, pairs):
    rows, width = queries.shape
    f32 = lambda *shape: jax.ShapeDtypeStruct(shape, jnp.float32)
    low = jax.ShapeDtypeStruct((rows, width), jnp.bfloat16)
    whole = pl.BlockSpec(memory_space=pltpu.VMEM)
    return pl.pallas_call(
        attention_kernel,
        in_specs=[pl.BlockSpec(memory_space=pltpu.SMEM)] + [whole] * (7 + KEY_BLOCKS),
        out_specs=[whole] * 6,
        scratch_shapes=[
            pltpu.VMEM((FRAMES * rows, rows), jnp.float32),
            pltpu.VMEM((rows, DH), jnp.float32),
            pltpu.VMEM((rows, DH), jnp.float32),
        ],
        out_shape=[low, f32(rows, width), f32(rows, width), low, f32(2, rows), f32(2, width)],
        compiler_params=pltpu.CompilerParams(vmem_limit_bytes=40 * 1024 * 1024),
        cost_estimate=pl.CostEstimate(flops=8_000_000_000, bytes_accessed=10_000_000, transcendentals=2_600_000),
        name="attention",
    )(where, squares, gain_q, gain_k, queries, noisy_keys, noisy_values, out_grad, *pairs)


def on_device(
    queries, noisy_keys, noisy_values, clean_keys, clean_values, gain_query, gain_key, out_grad
):
    length, width_dev = queries.shape
    column_start = lax.axis_index(HALF_HEAD) * width_dev
    gain_q = lax.dynamic_slice_in_dim(gain_query, column_start, width_dev)
    gain_k = lax.dynamic_slice_in_dim(gain_key, column_start, width_dev)
    pairs = gather_before(jnp.concatenate([clean_keys, clean_values], axis=1))
    q_full = queries.astype(jnp.float32)
    k_full = noisy_keys.astype(jnp.float32)
    squares = jnp.concatenate([jnp.sum(q_full * q_full, axis=1), jnp.sum(k_full * k_full, axis=1)])
    squares = from_all(squares, HALF_HEAD, COLUMN_PARTS)
    where = jnp.stack([lax.axis_index("x"), lax.axis_index("core")]).astype(jnp.int32)
    attended, flat_q, flat_k, grad_values, inners, parts = attention(
        where, squares, gain_q[None], gain_k[None], queries, noisy_keys, noisy_values, out_grad, pairs
    )
    piece_width = width_dev // FRAMES
    pieces = parts.reshape(2, FRAMES, piece_width).transpose(1, 0, 2)
    piece = jnp.sum(lax.all_to_all(pieces, FRAME, 0, 0), axis=0)
    sent = jnp.concatenate([inners.reshape(2 * length), piece.reshape(2 * piece_width)])
    got = from_all(sent, FSDP_HEAD, 2 * VIDEOS * HEAD_PARTS).reshape(2, VIDEOS, HEAD_PARTS, sent.shape[0])
    video = lax.axis_index(("video_z", "video_y"))
    same_video = lax.dynamic_index_in_dim(got[:, :, :, : 2 * length], video, 1, keepdims=False)
    inners = jnp.sum(same_video, axis=(0, 1)).reshape(2, length)
    gains = jnp.sum(got[:, :, :, 2 * length :], axis=1)
    gains = from_all(gains.reshape(COLUMN_PARTS * 2 * piece_width), FRAME, FRAMES)
    gains = gains.reshape(FRAMES, COLUMN_PARTS, 2, piece_width).transpose(2, 1, 0, 3).reshape(2, D)
    totals = jnp.sum(squares, axis=0)
    rate_q = lax.rsqrt(totals[:length] / D + EPSILON)
    rate_k = lax.rsqrt(totals[length:] / D + EPSILON)
    cube_q = rate_q * rate_q * rate_q * inners[0] / D
    cube_k = rate_k * rate_k * rate_k * inners[1] / D
    grad_queries = (rate_q[:, None] * flat_q - q_full * cube_q[:, None]).astype(jnp.bfloat16)
    grad_keys = (rate_k[:, None] * flat_k - k_full * cube_k[:, None]).astype(jnp.bfloat16)
    return (attended, grad_queries, grad_keys, grad_values, gains[0], gains[1])


def solution(mesh):
    torus = Mesh(
        mesh.devices.reshape(4, 2, 2, 6, 2, HEAD_PARTS),
        ("x", "core", "half", "video_z", "video_y", "head"),
    )
    in_specs = (
        P(FRAME, FSDP_HEAD),
        P(FRAME, FSDP_HEAD),
        P(FRAME, FSDP_HEAD),
        P(FRAME, FSDP_HEAD),
        P(FRAME, FSDP_HEAD),
        P(),
        P(),
        P(FRAME, FSDP_HEAD),
    )
    out_specs = (
        P(FRAME, FSDP_HEAD),
        P(FRAME, FSDP_HEAD),
        P(FRAME, FSDP_HEAD),
        P(FRAME, FSDP_HEAD),
        P(),
        P(),
    )
    return jax.shard_map(
        on_device, mesh=torus, in_specs=in_specs, out_specs=out_specs, check_vma=False
    )
```

time: 175 us -> 152 us (0.87)
  starting transfers between devices: 48 us -> 84.7 us
  matrix products: 30.5 us -> 0 us
  between operations: 14.4 us -> 0.94 us
  waiting for transfers between devices: 47.2 us -> 38.5 us
  Pallas kernels: 0 us -> 7.63 us
  other arithmetic: 10.6 us -> 3.02 us
  local copies, waits for them, and re-layouts: 23.3 us -> 15.8 us
    ppermute x0 -> x11, starting transfers between devices: none -> 36.8 us  [the longest x5 19.5 us: other_core(): return lax.ppermute(block, 'core', [(0, 1), (1, 0)])]
    dot_general x10 -> x0, matrix products: 30.5 us -> none  [the longest x1 10.3 us: attend_back(): jnp.einsum('hqk,khd->qhd', weighted, reflect_key_piece, preferred_element...]
    all_gather x1 -> x0, waiting for transfers between devices: 18.2 us -> none  [side_by_side(): out = lax.all_gather(both, axis, axis=dim, tiled=True)]
    all_to_all x3, starting transfers between devices: 43.7 us -> 34 us  [from_all(): lax.all_to_all(jnp.broadcast_to(x[None], (devices,) + x.shape), axes, 0, 0)]
    all_to_all x1, starting transfers between devices: 4.23 us -> 13.9 us  [on_device(): piece = jnp.sum(lax.all_to_all(pieces, FRAME, 0, 0), axis=0)]
    pallas_call x0 -> x1, Pallas kernels: none -> 7.63 us  [attention(): pl.pallas_call(attention_kernel, in_specs=[pl.BlockSpec(memory_space=pltp...]
    all_to_all x3, waiting for transfers between devices: 24.4 us -> 31.9 us  [from_all(): lax.all_to_all(jnp.broadcast_to(x[None], (devices,) + x.shape), axes, 0, 0)]
    reduce_sum x7 -> x1, other arithmetic: 6.51 us -> 0.03 us  [on_device(): totals = jnp.sum(squares, axis=0)]
  transfers between devices with their start and end apart: 5 -> 15, of which waited for: 5 -> 5; matrix products, arithmetic and copies ran while one was open for 8% -> 4% of each run, Pallas kernels for 0% -> 0%
where the time goes in v2:
time: 152 us; the launch traced here: 151 us
  starting transfers between devices  84.7 us (56%)
  waiting for transfers between devices  38.5 us (25%)
  local copies, waits for them, and re-layouts  15.8 us (10%)
  Pallas kernels  7.63 us (5%)
  other arithmetic  3.02 us (2%)
    all_to_all x3, starting transfers between devices, from_all(): lax.all_to_all(jnp.broadcast_to(x[None], (devices,) + x.shape), axes, 0, 0)  34 us
    all_to_all x3, waiting for transfers between devices, from_all(): lax.all_to_all(jnp.broadcast_to(x[None], (devices,) + x.shape), axes, 0, 0)  31.9 us
    ppermute x5, starting transfers between devices, other_core(): return lax.ppermute(block, 'core', [(0, 1), (1, 0)])  19.5 us
    all_to_all x1, starting transfers between devices, on_device(): piece = jnp.sum(lax.all_to_all(pieces, FRAME, 0, 0), axis=0)  13.9 us
    unnamed x25, local copies, waits for them, and re-layouts  7.65 us
    pallas_call x1, Pallas kernels, attention(): pl.pallas_call(attention_kernel, in_specs=[pl.BlockSpec(memory_space=pltp...  7.63 us
    ppermute x1, starting transfers between devices, gather_before(): middle_high = lax.ppermute(far_high, 'x', [(0, 3), (3, 2)])  6.05 us
    all_to_all x1, waiting for transfers between devices, on_device(): piece = jnp.sum(lax.all_to_all(pieces, FRAME, 0, 0), axis=0)  4.61 us
  transfers between devices with their start and end apart: 15, of which 5 were waited for; matrix products, arithmetic and copies ran while one was open for 4% of the time, Pallas kernels for 0%

profile of v2, /device:TPU:1, one launch (start us, length us, event | category | flops | bytes accessed | tf_op | source)
XLA Modules:
  0.0 150.6 jit_solution(8155129023914071430)
XLA Ops:
  0.6 1.8 %constant_dynamic-update-slice_fusion.1 = bf16[256,1280]{1,0:T(8,128)(2,1)} fusion(bf16[256,640]{1,0:T(8,128)(2,1)} %param.11), kind=kLoop, calls=%fused_computation.16 | loop fusion | bytes 655360
  2.5 0.8 constant_dynamic-update-slice_fusion
  3.3 4.0 %collective-permute-start.1 = (bf16[256,1280]{1,0:T(8,128)(2,1)}, bf16[256,1280]{1,0:T(8,128)(2,1)S(1)}, u32[]{:S(2)}, u32[]{:S(2)}) collective-permute-start(bf16[256,1280]{1,0:T(8,128)(2,1)} %constant_dynamic-update-slice_fusion), channel_id=1, source_target_pairs={{0,192},{192,384},{384,576},{1,193},{193,385},{385,577},{2,194},{1... | collective-permute-start | bytes 1966088 | tf_op jit(solution)/shard_map/ppermute | solution.py:42
  7.2 1.1 fusion.10
  8.4 2.5 %collective-permute-start.6 = (bf16[128,1280]{1,0:T(8,128)(2,1)S(1)}, bf16[128,1280]{1,0:T(8,128)(2,1)S(1)}, u32[]{:S(2)}, u32[]{:S(2)}) collective-permute-start(bf16[128,1280]{1,0:T(8,128)(2,1)S(1)} %get-tuple-element.18), channel_id=1, source_target_pairs={{0,576},{1,577},{2,578},{3,579},{4,580},{5,581},{6,582},{7,583},{8... | collective-permute-start | bytes 983048 | tf_op jit(solution)/shard_map/ppermute | solution.py:44
  10.9 1.9 %collective-permute-start.3 = (bf16[128,1280]{1,0:T(8,128)(2,1)S(1)}, bf16[128,1280]{1,0:T(8,128)(2,1)}, u32[]{:S(2)}, u32[]{:S(2)}) collective-permute-start(bf16[128,1280]{1,0:T(8,128)(2,1)S(1)} %get-tuple-element.19), channel_id=1, source_target_pairs={{0,576},{192,0},{1,577},{193,1},{2,578},{194,2},{3,579},{195,3},{4... | collective-permute-start | bytes 983048 | tf_op jit(solution)/shard_map/ppermute | solution.py:43
  12.9 2.0 %collective-permute-done.6.refs_9_ = bf16[128,1280]{1,0:T(8,128)(2,1)S(1)} collective-permute-done((bf16[128,1280]{1,0:T(8,128)(2,1)S(1)}, bf16[128,1280]{1,0:T(8,128)(2,1)S(1)}, u32[]{:S(2)}, u32[]{:S(2)}) %collective-permute-start.6) | collective-permute-done | bytes 327712 | tf_op jit(solution)/shard_map/ppermute | solution.py:44
  14.9 9.3 %collective-permute-start.10 = (bf16[128,1280]{1,0:T(8,128)(2,1)S(1)}, bf16[128,1280]{1,0:T(8,128)(2,1)S(1)}, u32[]{:S(2)}, u32[]{:S(2)}) collective-permute-start(bf16[128,1280]{1,0:T(8,128)(2,1)S(1)} %collective-permute-done.6.refs_9_), channel_id=1, source_target_pairs={{0,96},{96,0},{1,97},{97,1},{2,98},{98,2},{3,99},{99,3},{4,100},{1... | collective-permute-start | bytes 983048 | tf_op jit(solution)/shard_map/ppermute | solution.py:37
  24.2 6.1 %collective-permute-start.4 = (bf16[128,1280]{1,0:T(8,128)(2,1)}, bf16[128,1280]{1,0:T(8,128)(2,1)}, u32[]{:S(2)}, u32[]{:S(2)}) collective-permute-start(bf16[128,1280]{1,0:T(8,128)(2,1)} %collective-permute-done.3.refs_7_), channel_id=1, source_target_pairs={{0,576},{576,384},{1,577},{577,385},{2,578},{578,386},{3,579},{579... | collective-permute-start | bytes 983048 | tf_op jit(solution)/shard_map/ppermute | solution.py:46
  30.3 1.5 %collective-permute-start.7 = (bf16[128,1280]{1,0:T(8,128)(2,1)S(1)}, bf16[128,1280]{1,0:T(8,128)(2,1)}, u32[]{:S(2)}, u32[]{:S(2)}) collective-permute-start(bf16[128,1280]{1,0:T(8,128)(2,1)S(1)} %slice_select_fusion), channel_id=1, source_target_pairs={{384,576},{576,384},{385,577},{577,385},{386,578},{578,386},{387,5... | collective-permute-start | bytes 983048 | tf_op jit(solution)/shard_map/ppermute | solution.py:48
  31.9 1.3 collective-permute-start
  33.1 3.9 %collective-permute-start.2 = (bf16[256,1280]{1,0:T(8,128)(2,1)S(1)}, bf16[256,1280]{1,0:T(8,128)(2,1)S(1)}, u32[]{:S(2)}, u32[]{:S(2)}) collective-permute-start(bf16[256,1280]{1,0:T(8,128)(2,1)S(1)} %collective-permute-done.1.refs_1_), channel_id=1, source_target_pairs={{0,96},{96,0},{1,97},{97,1},{2,98},{98,2},{3,99},{99,3},{4,100},{1... | collective-permute-start | bytes 1966088 | tf_op jit(solution)/shard_map/ppermute | solution.py:37
  37.1 1.9 %collective-permute-start.9 = (bf16[128,1280]{1,0:T(8,128)(2,1)}, bf16[128,1280]{1,0:T(8,128)(2,1)}, u32[]{:S(2)}, u32[]{:S(2)}) collective-permute-start(bf16[128,1280]{1,0:T(8,128)(2,1)} %collective-permute-done.3.refs_7_), channel_id=1, source_target_pairs={{0,96},{96,0},{1,97},{97,1},{2,98},{98,2},{3,99},{99,3},{4,100},{1... | collective-permute-start | bytes 983048 | tf_op jit(solution)/shard_map/ppermute | solution.py:37
  39.0 2.4 %collective-permute-start.5 = (bf16[128,1280]{1,0:T(8,128)(2,1)}, bf16[128,1280]{1,0:T(8,128)(2,1)}, u32[]{:S(2)}, u32[]{:S(2)}) collective-permute-start(bf16[128,1280]{1,0:T(8,128)(2,1)} %collective-permute-done.4.refs_3_), channel_id=1, source_target_pairs={{0,96},{96,0},{1,97},{97,1},{2,98},{98,2},{3,99},{99,3},{4,100},{1... | collective-permute-start | bytes 983048 | tf_op jit(solution)/shard_map/ppermute | solution.py:37
  41.5 1.9 %collective-permute-start.8 = (bf16[128,1280]{1,0:T(8,128)(2,1)}, bf16[128,1280]{1,0:T(8,128)(2,1)}, u32[]{:S(2)}, u32[]{:S(2)}) collective-permute-start(bf16[128,1280]{1,0:T(8,128)(2,1)} %collective-permute-done.7.refs_5_), channel_id=1, source_target_pairs={{0,96},{96,0},{1,97},{97,1},{2,98},{98,2},{3,99},{99,3},{4,100},{1... | collective-permute-start | bytes 983048 | tf_op jit(solution)/shard_map/ppermute | solution.py:37
  43.4 0.2 fusion
  43.6 0.6 broadcast_in_dim.12
  44.2 19.5 %all-to-all-start = ((f32[8,1,512]{2,1,0:T(1,128)}), f32[8,1,512]{2,1,0:T(1,128)S(1)}, u32[]{:S(2)}, u32[]{:S(2)}) async-start(f32[8,1,512]{2,1,0:T(1,128)} %broadcast_in_dim.12), calls=%async_computation | async-start | bytes 32768 | tf_op jit(solution)/shard_map/all_to_all | solution.py:33
  63.8 0.8 dynamic_slice.10
  64.6 0.8 dynamic_slice.11
  65.4 12.2 %all-to-all-done = f32[8,1,512]{2,1,0:T(1,128)S(1)} async-done(((f32[8,1,512]{2,1,0:T(1,128)}), f32[8,1,512]{2,1,0:T(1,128)S(1)}, u32[]{:S(2)}, u32[]{:S(2)}) %all-to-all-start) | async-done | bytes 16416 | tf_op jit(solution)/shard_map/all_to_all | solution.py:33
  77.5 0.8 copy-done.2
  78.4 0.8 copy-done.4
  79.2 1.1 copy-done.3
  80.3 1.1 copy-done.5
  81.4 1.0 copy-done.7
  82.4 1.0 copy-done.9
  83.4 7.6 %attention.1 = (bf16[256,640]{1,0:T(8,128)(2,1)}, f32[256,640]{1,0:T(8,128)S(1)}, f32[256,640]{1,0:T(8,128)S(1)}, bf16[256,640]{1,0:T(8,128)(2,1)}, f32[2,256]{1,0:T(2,128)S(1)}, /*index=5*/f32[2,640]{1,0:T(2,128)S(1)}) custom-call(s32[2]{0:T(128)S(1)} %pad_add_fusion.where_ref, f32[8,512]{1,0:T(8,128)S(1)} %bitcast.15, ...), custom_call_target="tpu_custom_call" | custom-call | flops 8000000000 | bytes 10000000 | tf_op jit(solution)/shard_map/attention/pallas_call | solution.py:149
  91.0 0.1 reshape.64
  91.1 0.6 copy.31
  91.7 13.9 %all-to-all-start.1 = ((f32[8,2,80]{2,1,0:T(2,128)}), f32[8,2,80]{2,1,0:T(2,128)S(1)}, u32[]{:S(2)}, u32[]{:S(2)}) async-start(f32[8,2,80]{2,1,0:T(2,128)} %bitcast.14), calls=%async_computation.1 | async-start | bytes 16384 | tf_op jit(solution)/shard_map/all_to_all | solution.py:183
  105.6 4.6 %all-to-all-done.1 = f32[8,2,80]{2,1,0:T(2,128)S(1)} async-done(((f32[8,2,80]{2,1,0:T(2,128)}), f32[8,2,80]{2,1,0:T(2,128)S(1)}, u32[]{:S(2)}, u32[]{:S(2)}) %all-to-all-start.1) | async-done | bytes 5152 | tf_op jit(solution)/shard_map/all_to_all | solution.py:183
  110.2 0.1 reshape.65
  110.3 0.9 broadcast_in_dim.15
  111.2 7.8 %all-to-all-start.2 = ((f32[96,1,672]{2,1,0:T(1,128)}), f32[96,1,672]{2,1,0:T(1,128)S(1)}, u32[]{:S(2)}, u32[]{:S(2)}) async-start(f32[96,1,672]{2,1,0:T(1,128)} %broadcast_in_dim.15), calls=%async_computation.2 | async-start | bytes 589824 | tf_op jit(solution)/shard_map/all_to_all | solution.py:33
  119.1 16.8 %all-to-all-done.2 = f32[96,1,672]{2,1,0:T(1,128)S(1)} async-done(((f32[96,1,672]{2,1,0:T(1,128)}), f32[96,1,672]{2,1,0:T(1,128)S(1)}, u32[]{:S(2)}, u32[]{:S(2)}) %all-to-all-start.2) | async-done | bytes 258080 | tf_op jit(solution)/shard_map/all_to_all | solution.py:33
  135.9 0.7 reduce.2
  136.6 0.1 reshape.66
  136.7 0.1 broadcast_in_dim.16
  136.8 0.6 broadcast_in_dim.34
  137.4 6.7 %all-to-all-start.3 = ((f32[8,1,1280]{2,1,0:T(1,128)}), f32[8,1,1280]{2,1,0:T(1,128)S(1)}, u32[]{:S(2)}, u32[]{:S(2)}) async-start(f32[8,1,1280]{2,1,0:T(1,128)} %broadcast_in_dim.34), calls=%async_computation.3 | async-start | bytes 81920 | tf_op jit(solution)/shard_map/all_to_all | solution.py:33
  144.1 0.9 fusion.2
  145.0 0.9 fusion.5
  145.9 2.9 %all-to-all-done.3 = f32[8,1,1280]{2,1,0:T(1,128)S(1)} async-done(((f32[8,1,1280]{2,1,0:T(1,128)}), f32[8,1,1280]{2,1,0:T(1,128)S(1)}, u32[]{:S(2)}, u32[]{:S(2)}) %all-to-all-start.3) | async-done | bytes 40992 | tf_op jit(solution)/shard_map/all_to_all | solution.py:33
  148.9 0.1 reduce.3
  149.0 0.2 reshape.67
  149.2 0.7 squeeze.11
  149.9 0.7 squeeze.10
  (43 shorter events, 0.4 us)
Async XLA Ops:
  0.6 1.8 %copy-start.10 = (bf16[256,640]{1,0:T(8,128)(2,1)S(1)}, bf16[256,640]{1,0:T(8,128)(2,1)}, u32[]{:S(2)}) copy-start(bf16[256,640]{1,0:T(8,128)(2,1)} %param.12) | copy-start | bytes 983044
  3.3 27.0 %collective-permute-start.1 = (bf16[256,1280]{1,0:T(8,128)(2,1)}, bf16[256,1280]{1,0:T(8,128)(2,1)S(1)}, u32[]{:S(2)}, u32[]{:S(2)}) collective-permute-start(bf16[256,1280]{1,0:T(8,128)(2,1)} %constant_dynamic-update-slice_fusion), channel_id=1, source_target_pairs={{0,192},{192,384},{384,576},{1,193},{193,385},{385,577},{2,194},{1... | collective-permute-start | bytes 1966088 | tf_op jit(solution)/shard_map/ppermute | solution.py:42
  8.4 6.5 %collective-permute-start.6 = (bf16[128,1280]{1,0:T(8,128)(2,1)S(1)}, bf16[128,1280]{1,0:T(8,128)(2,1)S(1)}, u32[]{:S(2)}, u32[]{:S(2)}) collective-permute-start(bf16[128,1280]{1,0:T(8,128)(2,1)S(1)} %get-tuple-element.18), channel_id=1, source_target_pairs={{0,576},{1,577},{2,578},{3,579},{4,580},{5,581},{6,582},{7,583},{8... | collective-permute-start | bytes 983048 | tf_op jit(solution)/shard_map/ppermute | solution.py:44
  10.9 13.3 %collective-permute-start.3 = (bf16[128,1280]{1,0:T(8,128)(2,1)S(1)}, bf16[128,1280]{1,0:T(8,128)(2,1)}, u32[]{:S(2)}, u32[]{:S(2)}) collective-permute-start(bf16[128,1280]{1,0:T(8,128)(2,1)S(1)} %get-tuple-element.19), channel_id=1, source_target_pairs={{0,576},{192,0},{1,577},{193,1},{2,578},{194,2},{3,579},{195,3},{4... | collective-permute-start | bytes 983048 | tf_op jit(solution)/shard_map/ppermute | solution.py:43
  12.8 30.5 %copy-start = (bf16[256,640]{1,0:T(8,128)(2,1)S(1)}, bf16[256,640]{1,0:T(8,128)(2,1)}, u32[]{:S(2)}) copy-start(bf16[256,640]{1,0:T(8,128)(2,1)} %q_ref.1) | copy-start | bytes 983044
  12.9 30.5 %copy-start.1 = (bf16[256,640]{1,0:T(8,128)(2,1)S(1)}, bf16[256,640]{1,0:T(8,128)(2,1)}, u32[]{:S(2)}) copy-start(bf16[256,640]{1,0:T(8,128)(2,1)} %k_ref.1) | copy-start | bytes 983044
  14.9 22.2 %collective-permute-start.10 = (bf16[128,1280]{1,0:T(8,128)(2,1)S(1)}, bf16[128,1280]{1,0:T(8,128)(2,1)S(1)}, u32[]{:S(2)}, u32[]{:S(2)}) collective-permute-start(bf16[128,1280]{1,0:T(8,128)(2,1)S(1)} %collective-permute-done.6.refs_9_), channel_id=1, source_target_pairs={{0,96},{96,0},{1,97},{97,1},{2,98},{98,2},{3,99},{99,3},{4,100},{1... | collective-permute-start | bytes 983048 | tf_op jit(solution)/shard_map/ppermute | solution.py:37
  24.2 14.8 %collective-permute-start.4 = (bf16[128,1280]{1,0:T(8,128)(2,1)}, bf16[128,1280]{1,0:T(8,128)(2,1)}, u32[]{:S(2)}, u32[]{:S(2)}) collective-permute-start(bf16[128,1280]{1,0:T(8,128)(2,1)} %collective-permute-done.3.refs_7_), channel_id=1, source_target_pairs={{0,576},{576,384},{1,577},{577,385},{2,578},{578,386},{3,579},{579... | collective-permute-start | bytes 983048 | tf_op jit(solution)/shard_map/ppermute | solution.py:46
  30.3 48.9 %copy-start.6 = (bf16[256,640]{1,0:T(8,128)(2,1)S(1)}, bf16[256,640]{1,0:T(8,128)(2,1)}, u32[]{:S(2)}) copy-start(bf16[256,640]{1,0:T(8,128)(2,1)} %v_ref.1) | copy-start | bytes 983044
  30.3 11.1 %collective-permute-start.7 = (bf16[128,1280]{1,0:T(8,128)(2,1)S(1)}, bf16[128,1280]{1,0:T(8,128)(2,1)}, u32[]{:S(2)}, u32[]{:S(2)}) collective-permute-start(bf16[128,1280]{1,0:T(8,128)(2,1)S(1)} %slice_select_fusion), channel_id=1, source_target_pairs={{384,576},{576,384},{385,577},{577,385},{386,578},{578,386},{387,5... | collective-permute-start | bytes 983048 | tf_op jit(solution)/shard_map/ppermute | solution.py:48
  31.9 45.7 %collective-permute-start = (bf16[256,1280]{1,0:T(8,128)(2,1)}, bf16[256,1280]{1,0:T(8,128)(2,1)S(1)}, u32[]{:S(2)}, u32[]{:S(2)}) collective-permute-start(bf16[256,1280]{1,0:T(8,128)(2,1)} %constant_dynamic-update-slice_fusion), channel_id=1, source_target_pairs={{0,96},{1,97},{2,98},{3,99},{4,100},{5,101},{6,102},{7,103},{8,104... | collective-permute-start | bytes 1966088 | tf_op jit(solution)/shard_map/ppermute | solution.py:45
  33.1 45.2 %collective-permute-start.2 = (bf16[256,1280]{1,0:T(8,128)(2,1)S(1)}, bf16[256,1280]{1,0:T(8,128)(2,1)S(1)}, u32[]{:S(2)}, u32[]{:S(2)}) collective-permute-start(bf16[256,1280]{1,0:T(8,128)(2,1)S(1)} %collective-permute-done.1.refs_1_), channel_id=1, source_target_pairs={{0,96},{96,0},{1,97},{97,1},{2,98},{98,2},{3,99},{99,3},{4,100},{1... | collective-permute-start | bytes 1966088 | tf_op jit(solution)/shard_map/ppermute | solution.py:37
  37.1 6.5 %copy-start.8 = (bf16[128,1280]{1,0:T(8,128)(2,1)}, bf16[128,1280]{1,0:T(8,128)(2,1)S(1)}, u32[]{:S(2)}) copy-start(bf16[128,1280]{1,0:T(8,128)(2,1)S(1)} %collective-permute-done.10.refs_10_) | copy-start | bytes 983044
  37.1 40.4 %collective-permute-start.9 = (bf16[128,1280]{1,0:T(8,128)(2,1)}, bf16[128,1280]{1,0:T(8,128)(2,1)}, u32[]{:S(2)}, u32[]{:S(2)}) collective-permute-start(bf16[128,1280]{1,0:T(8,128)(2,1)} %collective-permute-done.3.refs_7_), channel_id=1, source_target_pairs={{0,96},{96,0},{1,97},{97,1},{2,98},{98,2},{3,99},{99,3},{4,100},{1... | collective-permute-start | bytes 983048 | tf_op jit(solution)/shard_map/ppermute | solution.py:37
  39.0 39.4 %collective-permute-start.5 = (bf16[128,1280]{1,0:T(8,128)(2,1)}, bf16[128,1280]{1,0:T(8,128)(2,1)}, u32[]{:S(2)}, u32[]{:S(2)}) collective-permute-start(bf16[128,1280]{1,0:T(8,128)(2,1)} %collective-permute-done.4.refs_3_), channel_id=1, source_target_pairs={{0,96},{96,0},{1,97},{97,1},{2,98},{98,2},{3,99},{99,3},{4,100},{1... | collective-permute-start | bytes 983048 | tf_op jit(solution)/shard_map/ppermute | solution.py:37
  41.5 36.9 %collective-permute-start.8 = (bf16[128,1280]{1,0:T(8,128)(2,1)}, bf16[128,1280]{1,0:T(8,128)(2,1)}, u32[]{:S(2)}, u32[]{:S(2)}) collective-permute-start(bf16[128,1280]{1,0:T(8,128)(2,1)} %collective-permute-done.7.refs_5_), channel_id=1, source_target_pairs={{0,96},{96,0},{1,97},{97,1},{2,98},{98,2},{3,99},{99,3},{4,100},{1... | collective-permute-start | bytes 983048 | tf_op jit(solution)/shard_map/ppermute | solution.py:37
  44.2 33.3 %all-to-all-start = ((f32[8,1,512]{2,1,0:T(1,128)}), f32[8,1,512]{2,1,0:T(1,128)S(1)}, u32[]{:S(2)}, u32[]{:S(2)}) async-start(f32[8,1,512]{2,1,0:T(1,128)} %broadcast_in_dim.12), calls=%async_computation | async-start | bytes 32768 | tf_op jit(solution)/shard_map/all_to_all | solution.py:33
  77.5 0.8 copy-start.2
  78.4 0.8 copy-start.4
  79.2 1.1 copy-start.3
  80.3 1.1 copy-start.5
  81.4 1.0 copy-start.7
  82.4 1.0 copy-start.9
  91.7 18.5 %all-to-all-start.1 = ((f32[8,2,80]{2,1,0:T(2,128)}), f32[8,2,80]{2,1,0:T(2,128)S(1)}, u32[]{:S(2)}, u32[]{:S(2)}) async-start(f32[8,2,80]{2,1,0:T(2,128)} %bitcast.14), calls=%async_computation.1 | async-start | bytes 16384 | tf_op jit(solution)/shard_map/all_to_all | solution.py:183
  111.2 24.7 %all-to-all-start.2 = ((f32[96,1,672]{2,1,0:T(1,128)}), f32[96,1,672]{2,1,0:T(1,128)S(1)}, u32[]{:S(2)}, u32[]{:S(2)}) async-start(f32[96,1,672]{2,1,0:T(1,128)} %broadcast_in_dim.15), calls=%async_computation.2 | async-start | bytes 589824 | tf_op jit(solution)/shard_map/all_to_all | solution.py:33
  137.4 11.4 %all-to-all-start.3 = ((f32[8,1,1280]{2,1,0:T(1,128)}), f32[8,1,1280]{2,1,0:T(1,128)S(1)}, u32[]{:S(2)}, u32[]{:S(2)}) async-start(f32[8,1,1280]{2,1,0:T(1,128)} %broadcast_in_dim.34), calls=%async_computation.3 | async-start | bytes 81920 | tf_op jit(solution)/shard_map/all_to_all | solution.py:33

commit v3 on v2

--- a/solution.py
+++ b/solution.py
@@ -37,19 +37,21 @@
     return lax.ppermute(block, "core", [(0, 1), (1, 0)])
 
 
-def gather_before(block):
+def gather_first(block):
     rows = block.shape[0] // 2
     near = lax.ppermute(block, "x", [(0, 1), (1, 2), (2, 3)])
     far_high = lax.ppermute(block[rows:], "x", [(0, 3), (1, 0)])
     far_low = lax.ppermute(block[:rows], "x", [(0, 3)])
     sibling = lax.ppermute(block, "core", [(0, 1)])
+    return sibling, near, far_high, far_low
+
+
+def gather_second(near, far_high, far_low):
     middle_high = lax.ppermute(far_high, "x", [(0, 3), (3, 2)])
-    onward = jnp.where(lax.axis_index("x") == 3, far_low, near[:rows])
+    onward = jnp.where(lax.axis_index("x") == 3, far_low, near[: far_low.shape[0]])
     middle_low = lax.ppermute(onward, "x", [(2, 3), (3, 2)])
-    halves = [far_high, far_low, middle_high, middle_low]
-    near_other = other_core(near)
-    others = [other_core(half) for half in halves]
-    return [sibling, near, near_other, halves[2], others[2], halves[3], others[3], halves[0], others[0], halves[1], others[1]]
+    blocks = (near, middle_high, middle_low, far_high, far_low)
+    return [b for block in blocks for b in (block, other_core(block))]
 
 
 def dot(a, b, dims):
@@ -65,15 +67,26 @@
     return jnp.transpose(jnp.broadcast_to(row, (8, row.shape[1])))[:, :1]
 
 
-def attention_kernel(where_ref, squares_ref, gain_q_ref, gain_k_ref, q_ref, k_ref, v_ref, do_ref, *refs):
-    pairs = refs[:KEY_BLOCKS]
-    att_ref, flat_q_ref, flat_k_ref, gv_ref, inner_ref, part_ref, expo_ref, sum_q_ref, sum_k_ref = refs[KEY_BLOCKS:]
+def attention_kernel(where_ref, squares_ref, gain_q_ref, gain_k_ref, *refs):
+    sources, refs = refs[: 4 + KEY_BLOCKS], refs[4 + KEY_BLOCKS :]
+    att_ref, flat_q_ref, flat_k_ref, gv_ref, inner_ref, part_ref, expo_ref, sum_q_ref, sum_k_ref = refs[:9]
+    local, arrived = refs[9:-1], refs[-1]
+    copies = [
+        pltpu.make_async_copy(source, target, arrived.at[i])
+        for i, (source, target) in enumerate(zip(sources, local))
+    ]
+    for copy in copies:
+        copy.start()
+    q_ref, k_ref, v_ref, do_ref = local[:4]
+    pairs = local[4:]
     rows, width = q_ref.shape
     rates = lax.rsqrt(jnp.sum(squares_ref[...], axis=0, keepdims=True) / D + EPSILON)
     rate_q, rate_k = column(rates[:, :rows]), column(rates[:, rows:])
     own_x, own_core = where_ref[0], where_ref[1]
     sum_q_ref[...] = jnp.zeros_like(sum_q_ref)
     sum_k_ref[...] = jnp.zeros_like(sum_k_ref)
+    for copy in copies:
+        copy.wait()
 
     def one_head(remote, start):
         lanes = pl.ds(pl.multiple_of(start, DH), DH)
@@ -146,20 +159,23 @@
     f32 = lambda *shape: jax.ShapeDtypeStruct(shape, jnp.float32)
     low = jax.ShapeDtypeStruct((rows, width), jnp.bfloat16)
     whole = pl.BlockSpec(memory_space=pltpu.VMEM)
+    fetched = [queries, noisy_keys, noisy_values, out_grad, *pairs]
     return pl.pallas_call(
         attention_kernel,
-        in_specs=[pl.BlockSpec(memory_space=pltpu.SMEM)] + [whole] * (7 + KEY_BLOCKS),
+        in_specs=[pl.BlockSpec(memory_space=pltpu.SMEM)] + [whole] * 3 + [pl.BlockSpec(memory_space=pl.ANY)] * len(fetched),
         out_specs=[whole] * 6,
         scratch_shapes=[
             pltpu.VMEM((FRAMES * rows, rows), jnp.float32),
             pltpu.VMEM((rows, DH), jnp.float32),
             pltpu.VMEM((rows, DH), jnp.float32),
+            *[pltpu.VMEM(x.shape, x.dtype) for x in fetched],
+            pltpu.SemaphoreType.DMA((len(fetched),)),
         ],
         out_shape=[low, f32(rows, width), f32(rows, width), low, f32(2, rows), f32(2, width)],
-        compiler_params=pltpu.CompilerParams(vmem_limit_bytes=40 * 1024 * 1024),
+        compiler_params=pltpu.CompilerParams(vmem_limit_bytes=56 * 1024 * 1024),
         cost_estimate=pl.CostEstimate(flops=8_000_000_000, bytes_accessed=10_000_000, transcendentals=2_600_000),
         name="attention",
-    )(where, squares, gain_q, gain_k, queries, noisy_keys, noisy_values, out_grad, *pairs)
+    )(where, squares, gain_q, gain_k, *fetched)
 
 
 def on_device(
@@ -169,11 +185,13 @@
     column_start = lax.axis_index(HALF_HEAD) * width_dev
     gain_q = lax.dynamic_slice_in_dim(gain_query, column_start, width_dev)
     gain_k = lax.dynamic_slice_in_dim(gain_key, column_start, width_dev)
-    pairs = gather_before(jnp.concatenate([clean_keys, clean_values], axis=1))
+    first = gather_first(jnp.concatenate([clean_keys, clean_values], axis=1))
     q_full = queries.astype(jnp.float32)
     k_full = noisy_keys.astype(jnp.float32)
     squares = jnp.concatenate([jnp.sum(q_full * q_full, axis=1), jnp.sum(k_full * k_full, axis=1)])
     squares = from_all(squares, HALF_HEAD, COLUMN_PARTS)
+    squares, (sibling, *received) = lax.optimization_barrier((squares, first))
+    pairs = [sibling] + gather_second(*received)
     where = jnp.stack([lax.axis_index("x"), lax.axis_index("core")]).astype(jnp.int32)
     attended, flat_q, flat_k, grad_values, inners, parts = attention(
         where, squares, gain_q[None], gain_k[None], queries, noisy_keys, noisy_values, out_grad, pairs

time: 152 us -> 137 us (0.901)
  starting transfers between devices: 84.7 us -> 71.6 us
  local copies, waits for them, and re-layouts: 15.8 us -> 13.2 us
  Pallas kernels: 7.63 us -> 10.1 us
  waiting for transfers between devices: 38.5 us -> 36.3 us
    ppermute x5, starting transfers between devices: 19.5 us -> 14.8 us  [other_core(): return lax.ppermute(block, 'core', [(0, 1), (1, 0)])]
    all_to_all x1, starting transfers between devices: 13.9 us -> 9.55 us  [on_device(): piece = jnp.sum(lax.all_to_all(pieces, FRAME, 0, 0), axis=0)]
    ppermute x6, starting transfers between devices: 17.3 us -> 13.3 us  [the longest x1 3.99 us: gather_first(): near = lax.ppermute(block, 'x', [(0, 1), (1, 2), (2, 3)])]
    unnamed x25 -> x35, local copies, waits for them, and re-layouts: 7.65 us -> 4.99 us
    pallas_call x1, Pallas kernels: 7.63 us -> 10.1 us  [attention(): pl.pallas_call(attention_kernel, in_specs=[pl.BlockSpec(memory_space=pltp...]
    ppermute x6, waiting for transfers between devices: 2.03 us -> 0.02 us  [the longest x1 0.01 us: gather_first(): far_high = lax.ppermute(block[rows:], 'x', [(0, 3), (1, 0)])]
  transfers between devices with their start and end apart: 15 -> 15, of which waited for: 5 -> 4; matrix products, arithmetic and copies ran while one was open for 4% -> 5% of each run, Pallas kernels for 0% -> 0%
where the time goes in v3:
time: 137 us; the launch traced here: 136 us
  starting transfers between devices  71.6 us (52%)
  waiting for transfers between devices  36.3 us (26%)
  local copies, waits for them, and re-layouts  13.2 us (10%)
  Pallas kernels  10.1 us (7%)
  other arithmetic  3.6 us (3%)
    all_to_all x3, starting transfers between devices, from_all(): lax.all_to_all(jnp.broadcast_to(x[None], (devices,) + x.shape), axes, 0, 0)  34 us
    all_to_all x3, waiting for transfers between devices, from_all(): lax.all_to_all(jnp.broadcast_to(x[None], (devices,) + x.shape), axes, 0, 0)  32.4 us
    ppermute x5, starting transfers between devices, other_core(): return lax.ppermute(block, 'core', [(0, 1), (1, 0)])  14.8 us
    pallas_call x1, Pallas kernels, attention(): pl.pallas_call(attention_kernel, in_specs=[pl.BlockSpec(memory_space=pltp...  10.1 us
    all_to_all x1, starting transfers between devices, on_device(): piece = jnp.sum(lax.all_to_all(pieces, FRAME, 0, 0), axis=0)  9.55 us
    unnamed x35, local copies, waits for them, and re-layouts  4.99 us
    ppermute x1, starting transfers between devices, gather_first(): near = lax.ppermute(block, 'x', [(0, 1), (1, 2), (2, 3)])  3.99 us
    all_to_all x1, waiting for transfers between devices, on_device(): piece = jnp.sum(lax.all_to_all(pieces, FRAME, 0, 0), axis=0)  3.94 us
  transfers between devices with their start and end apart: 15, of which 4 were waited for; matrix products, arithmetic and copies ran while one was open for 5% of the time, Pallas kernels for 0%

profile of v3, /device:TPU:1, one launch (start us, length us, event | category | flops | bytes accessed | tf_op | source)
XLA Modules:
  0.0 135.9 jit_solution(9730002286172345925)
XLA Ops:
  0.6 1.0 constant_dynamic-update-slice_fusion.1
  1.8 1.4 %collective-permute-start = (bf16[256,1280]{1,0:T(8,128)(2,1)S(1)}, bf16[256,1280]{1,0:T(8,128)(2,1)}, u32[]{:S(2)}, u32[]{:S(2)}) collective-permute-start(bf16[256,1280]{1,0:T(8,128)(2,1)S(1)} %constant_dynamic-update-slice_fusion), channel_id=1, source_target_pairs={{0,96},{1,97},{2,98},{3,99},{4,100},{5,101},{6,102},{7,103},{8,104... | collective-permute-start | bytes 1966088 | tf_op jit(solution)/shard_map/ppermute | solution.py:45
  3.2 4.0 %collective-permute-start.1 = (bf16[256,1280]{1,0:T(8,128)(2,1)S(1)}, bf16[256,1280]{1,0:T(8,128)(2,1)S(1)}, u32[]{:S(2)}, u32[]{:S(2)}) collective-permute-start(bf16[256,1280]{1,0:T(8,128)(2,1)S(1)} %constant_dynamic-update-slice_fusion), channel_id=1, source_target_pairs={{0,192},{192,384},{384,576},{1,193},{193,385},{385,577},{2,194},{1... | collective-permute-start | bytes 1966088 | tf_op jit(solution)/shard_map/ppermute | solution.py:42
  7.3 2.5 %collective-permute-start.2 = (bf16[128,1280]{1,0:T(8,128)(2,1)S(1)}, bf16[128,1280]{1,0:T(8,128)(2,1)S(1)}, u32[]{:S(2)}, u32[]{:S(2)}) collective-permute-start(bf16[128,1280]{1,0:T(8,128)(2,1)S(1)} %get-tuple-element.29), channel_id=1, source_target_pairs={{0,576},{192,0},{1,577},{193,1},{2,578},{194,2},{3,579},{195,3},{4... | collective-permute-start | bytes 983048 | tf_op jit(solution)/shard_map/ppermute | solution.py:43
  9.8 1.3 collective-permute-start.3
  11.1 0.2 fusion
  11.3 0.6 broadcast_in_dim.12
  12.0 19.5 %all-to-all-start = ((f32[8,1,512]{2,1,0:T(1,128)}), f32[8,1,512]{2,1,0:T(1,128)S(1)}, u32[]{:S(2)}, u32[]{:S(2)}) async-start(f32[8,1,512]{2,1,0:T(1,128)} %broadcast_in_dim.12), calls=%async_computation | async-start | bytes 32768 | tf_op jit(solution)/shard_map/all_to_all | solution.py:33
  31.4 13.8 %all-to-all-done = f32[8,1,512]{2,1,0:T(1,128)S(1)} async-done(((f32[8,1,512]{2,1,0:T(1,128)}), f32[8,1,512]{2,1,0:T(1,128)S(1)}, u32[]{:S(2)}, u32[]{:S(2)}) %all-to-all-start) | async-done | bytes 16416 | tf_op jit(solution)/shard_map/all_to_all | solution.py:33
  45.2 0.6 copy.30
  45.9 0.7 collective-permute-start.7
  46.6 3.4 %collective-permute-start.5 = (bf16[128,1280]{1,0:T(8,128)(2,1)S(1)}, bf16[128,1280]{1,0:T(8,128)(2,1)S(1)}, u32[]{:S(2)}, u32[]{:S(2)}) collective-permute-start(bf16[128,1280]{1,0:T(8,128)(2,1)S(1)} %collective-permute-done.2.refs_11_), channel_id=1, source_target_pairs={{0,576},{576,384},{1,577},{577,385},{2,578},{578,386},{3,579},{579... | collective-permute-start | bytes 983048 | tf_op jit(solution)/shard_map/ppermute | solution.py:50
  50.0 6.1 %collective-permute-start.4 = (bf16[256,1280]{1,0:T(8,128)(2,1)S(1)}, bf16[256,1280]{1,0:T(8,128)(2,1)S(1)}, u32[]{:S(2)}, u32[]{:S(2)}) collective-permute-start(bf16[256,1280]{1,0:T(8,128)(2,1)S(1)} %collective-permute-done.1.refs_5_), channel_id=1, source_target_pairs={{0,96},{96,0},{1,97},{97,1},{2,98},{98,2},{3,99},{99,3},{4,100},{1... | collective-permute-start | bytes 1966088 | tf_op jit(solution)/shard_map/ppermute | solution.py:37
  56.2 1.9 %collective-permute-start.10 = (bf16[128,1280]{1,0:T(8,128)(2,1)S(1)}, bf16[128,1280]{1,0:T(8,128)(2,1)S(1)}, u32[]{:S(2)}, u32[]{:S(2)}) collective-permute-start(bf16[128,1280]{1,0:T(8,128)(2,1)S(1)} %collective-permute-done.3.refs_13_), channel_id=1, source_target_pairs={{0,96},{96,0},{1,97},{97,1},{2,98},{98,2},{3,99},{99,3},{4,100},{1... | collective-permute-start | bytes 983048 | tf_op jit(solution)/shard_map/ppermute | solution.py:37
  58.1 2.4 %collective-permute-start.9 = (bf16[128,1280]{1,0:T(8,128)(2,1)S(1)}, bf16[128,1280]{1,0:T(8,128)(2,1)}, u32[]{:S(2)}, u32[]{:S(2)}) collective-permute-start(bf16[128,1280]{1,0:T(8,128)(2,1)S(1)} %collective-permute-done.2.refs_11_), channel_id=1, source_target_pairs={{0,96},{96,0},{1,97},{97,1},{2,98},{98,2},{3,99},{99,3},{4,100},{1... | collective-permute-start | bytes 983048 | tf_op jit(solution)/shard_map/ppermute | solution.py:37
  60.5 1.9 %collective-permute-start.8 = (bf16[128,1280]{1,0:T(8,128)(2,1)S(1)}, bf16[128,1280]{1,0:T(8,128)(2,1)}, u32[]{:S(2)}, u32[]{:S(2)}) collective-permute-start(bf16[128,1280]{1,0:T(8,128)(2,1)S(1)} %collective-permute-done.7.refs_9_), channel_id=1, source_target_pairs={{0,96},{96,0},{1,97},{97,1},{2,98},{98,2},{3,99},{99,3},{4,100},{1... | collective-permute-start | bytes 983048 | tf_op jit(solution)/shard_map/ppermute | solution.py:37
  62.5 2.4 %collective-permute-start.6 = (bf16[128,1280]{1,0:T(8,128)(2,1)S(1)}, bf16[128,1280]{1,0:T(8,128)(2,1)}, u32[]{:S(2)}, u32[]{:S(2)}) collective-permute-start(bf16[128,1280]{1,0:T(8,128)(2,1)S(1)} %collective-permute-done.5.refs_7_), channel_id=1, source_target_pairs={{0,96},{96,0},{1,97},{97,1},{2,98},{98,2},{3,99},{99,3},{4,100},{1... | collective-permute-start | bytes 983048 | tf_op jit(solution)/shard_map/ppermute | solution.py:37
  64.9 0.8 dynamic_slice.10
  65.7 0.6 broadcast_in_dim.13.gain_q_ref
  66.3 0.8 dynamic_slice.11
  67.0 0.6 broadcast_in_dim.14.gain_k_ref
  67.6 0.7 pad_add_fusion.where_ref
  68.4 0.7 copy-done.15
  69.1 0.8 copy-done.11
  69.9 10.1 %attention.1 = (bf16[256,640]{1,0:T(8,128)(2,1)}, f32[256,640]{1,0:T(8,128)}, f32[256,640]{1,0:T(8,128)}, bf16[256,640]{1,0:T(8,128)(2,1)}, f32[2,256]{1,0:T(2,128)}, /*index=5*/f32[2,640]{1,0:T(2,128)}) custom-call(s32[2]{0:T(128)} %pad_add_fusion.where_ref, f32[8,512]{1,0:T(8,128)} %bitcast.16, f32[1,640]{1,0:T(1,128)} %broadcast_in_dim.13.gain_q_ref, ...), custom_call_target="tpu_custom_call" | custom-call | flops 8000000000 | bytes 10000000 | tf_op jit(solution)/shard_map/attention/pallas_call | solution.py:163
  80.0 0.8 reshape.64
  80.7 0.6 copy.31
  81.3 9.5 %all-to-all-start.1 = ((f32[8,2,80]{2,1,0:T(2,128)}), f32[8,2,80]{2,1,0:T(2,128)S(1)}, u32[]{:S(2)}, u32[]{:S(2)}) async-start(f32[8,2,80]{2,1,0:T(2,128)} %bitcast.14), calls=%async_computation.1 | async-start | bytes 16384 | tf_op jit(solution)/shard_map/all_to_all | solution.py:201
  90.9 0.7 copy-done.10
  91.6 3.9 %all-to-all-done.1 = f32[8,2,80]{2,1,0:T(2,128)S(1)} async-done(((f32[8,2,80]{2,1,0:T(2,128)}), f32[8,2,80]{2,1,0:T(2,128)S(1)}, u32[]{:S(2)}, u32[]{:S(2)}) %all-to-all-start.1) | async-done | bytes 5152 | tf_op jit(solution)/shard_map/all_to_all | solution.py:201
  95.5 0.1 reshape.65
  95.6 0.9 broadcast_in_dim.15
  96.5 7.8 %all-to-all-start.2 = ((f32[96,1,672]{2,1,0:T(1,128)}), f32[96,1,672]{2,1,0:T(1,128)S(1)}, u32[]{:S(2)}, u32[]{:S(2)}) async-start(f32[96,1,672]{2,1,0:T(1,128)} %broadcast_in_dim.15), calls=%async_computation.2 | async-start | bytes 589824 | tf_op jit(solution)/shard_map/all_to_all | solution.py:33
  104.4 0.7 copy-done.9
  105.1 16.1 %all-to-all-done.2 = f32[96,1,672]{2,1,0:T(1,128)S(1)} async-done(((f32[96,1,672]{2,1,0:T(1,128)}), f32[96,1,672]{2,1,0:T(1,128)S(1)}, u32[]{:S(2)}, u32[]{:S(2)}) %all-to-all-start.2) | async-done | bytes 258080 | tf_op jit(solution)/shard_map/all_to_all | solution.py:33
  121.2 0.7 reduce.1
  121.9 0.1 reshape.66
  122.0 0.1 broadcast_in_dim.16
  122.1 0.6 broadcast_in_dim.34
  122.7 6.7 %all-to-all-start.3 = ((f32[8,1,1280]{2,1,0:T(1,128)}), f32[8,1,1280]{2,1,0:T(1,128)S(1)}, u32[]{:S(2)}, u32[]{:S(2)}) async-start(f32[8,1,1280]{2,1,0:T(1,128)} %broadcast_in_dim.34), calls=%async_computation.3 | async-start | bytes 81920 | tf_op jit(solution)/shard_map/all_to_all | solution.py:33
  129.5 0.9 fusion.5
  130.4 0.3 copy-done.4
  130.8 0.9 fusion.2
  131.7 2.5 %all-to-all-done.3 = f32[8,1,1280]{2,1,0:T(1,128)S(1)} async-done(((f32[8,1,1280]{2,1,0:T(1,128)}), f32[8,1,1280]{2,1,0:T(1,128)S(1)}, u32[]{:S(2)}, u32[]{:S(2)}) %all-to-all-start.3) | async-done | bytes 40992 | tf_op jit(solution)/shard_map/all_to_all | solution.py:33
  134.2 0.1 reduce.2
  134.3 0.2 reshape.67
  134.5 0.7 squeeze.10
  135.2 0.7 squeeze.11
  (53 shorter events, 0.5 us)
Async XLA Ops:
  0.6 1.1 copy-start.7
  1.8 9.4 %copy-start = (bf16[256,640]{1,0:T(8,128)(2,1)S(1)}, bf16[256,640]{1,0:T(8,128)(2,1)}, u32[]{:S(2)}) copy-start(bf16[256,640]{1,0:T(8,128)(2,1)} %refs_1_.1) | copy-start | bytes 983044
  1.8 9.4 %copy-start.2 = (bf16[256,640]{1,0:T(8,128)(2,1)S(1)}, bf16[256,640]{1,0:T(8,128)(2,1)}, u32[]{:S(2)}) copy-start(bf16[256,640]{1,0:T(8,128)(2,1)} %refs_0_.1) | copy-start | bytes 983044
  1.8 44.1 %collective-permute-start = (bf16[256,1280]{1,0:T(8,128)(2,1)S(1)}, bf16[256,1280]{1,0:T(8,128)(2,1)}, u32[]{:S(2)}, u32[]{:S(2)}) collective-permute-start(bf16[256,1280]{1,0:T(8,128)(2,1)S(1)} %constant_dynamic-update-slice_fusion), channel_id=1, source_target_pairs={{0,96},{1,97},{2,98},{3,99},{4,100},{5,101},{6,102},{7,103},{8,104... | collective-permute-start | bytes 1966088 | tf_op jit(solution)/shard_map/ppermute | solution.py:45
  3.2 42.7 %collective-permute-start.1 = (bf16[256,1280]{1,0:T(8,128)(2,1)S(1)}, bf16[256,1280]{1,0:T(8,128)(2,1)S(1)}, u32[]{:S(2)}, u32[]{:S(2)}) collective-permute-start(bf16[256,1280]{1,0:T(8,128)(2,1)S(1)} %constant_dynamic-update-slice_fusion), channel_id=1, source_target_pairs={{0,192},{192,384},{384,576},{1,193},{193,385},{385,577},{2,194},{1... | collective-permute-start | bytes 1966088 | tf_op jit(solution)/shard_map/ppermute | solution.py:42
  7.3 38.6 %collective-permute-start.2 = (bf16[128,1280]{1,0:T(8,128)(2,1)S(1)}, bf16[128,1280]{1,0:T(8,128)(2,1)S(1)}, u32[]{:S(2)}, u32[]{:S(2)}) collective-permute-start(bf16[128,1280]{1,0:T(8,128)(2,1)S(1)} %get-tuple-element.29), channel_id=1, source_target_pairs={{0,576},{192,0},{1,577},{193,1},{2,578},{194,2},{3,579},{195,3},{4... | collective-permute-start | bytes 983048 | tf_op jit(solution)/shard_map/ppermute | solution.py:43
  9.8 36.1 %collective-permute-start.3 = (bf16[128,1280]{1,0:T(8,128)(2,1)S(1)}, bf16[128,1280]{1,0:T(8,128)(2,1)S(1)}, u32[]{:S(2)}, u32[]{:S(2)}) collective-permute-start(bf16[128,1280]{1,0:T(8,128)(2,1)S(1)} %get-tuple-element.28), channel_id=1, source_target_pairs={{0,576},{1,577},{2,578},{3,579},{4,580},{5,581},{6,582},{7,583},{8... | collective-permute-start | bytes 983048 | tf_op jit(solution)/shard_map/ppermute | solution.py:44
  12.0 33.3 %all-to-all-start = ((f32[8,1,512]{2,1,0:T(1,128)}), f32[8,1,512]{2,1,0:T(1,128)S(1)}, u32[]{:S(2)}, u32[]{:S(2)}) async-start(f32[8,1,512]{2,1,0:T(1,128)} %broadcast_in_dim.12), calls=%async_computation | async-start | bytes 32768 | tf_op jit(solution)/shard_map/all_to_all | solution.py:33
  45.8 22.5 %copy-start.12 = (bf16[128,1280]{1,0:T(8,128)(2,1)}, bf16[128,1280]{1,0:T(8,128)(2,1)S(1)}, u32[]{:S(2)}) copy-start(bf16[128,1280]{1,0:T(8,128)(2,1)S(1)} %collective-permute-done.2.refs_11_) | copy-start | bytes 983044
  45.9 10.3 %copy-start.6 = (bf16[128,1280]{1,0:T(8,128)(2,1)}, bf16[128,1280]{1,0:T(8,128)(2,1)S(1)}, u32[]{:S(2)}) copy-start(bf16[128,1280]{1,0:T(8,128)(2,1)S(1)} %collective-permute-done.3.refs_13_) | copy-start | bytes 983044
  45.9 22.5 %copy-start.8 = (bf16[256,1280]{1,0:T(8,128)(2,1)}, bf16[256,1280]{1,0:T(8,128)(2,1)S(1)}, u32[]{:S(2)}) copy-start(bf16[256,1280]{1,0:T(8,128)(2,1)S(1)} %collective-permute-done.1.refs_5_) | copy-start | bytes 1966084
  45.9 14.6 %collective-permute-start.7 = (bf16[128,1280]{1,0:T(8,128)(2,1)S(1)}, bf16[128,1280]{1,0:T(8,128)(2,1)S(1)}, u32[]{:S(2)}, u32[]{:S(2)}) collective-permute-start(bf16[128,1280]{1,0:T(8,128)(2,1)S(1)} %slice_select_fusion), channel_id=1, source_target_pairs={{384,576},{576,384},{385,577},{577,385},{386,578},{578,386},{387,5... | collective-permute-start | bytes 983048 | tf_op jit(solution)/shard_map/ppermute | solution.py:52
  46.6 15.8 %collective-permute-start.5 = (bf16[128,1280]{1,0:T(8,128)(2,1)S(1)}, bf16[128,1280]{1,0:T(8,128)(2,1)S(1)}, u32[]{:S(2)}, u32[]{:S(2)}) collective-permute-start(bf16[128,1280]{1,0:T(8,128)(2,1)S(1)} %collective-permute-done.2.refs_11_), channel_id=1, source_target_pairs={{0,576},{576,384},{1,577},{577,385},{2,578},{578,386},{3,579},{579... | collective-permute-start | bytes 983048 | tf_op jit(solution)/shard_map/ppermute | solution.py:50
  50.0 18.3 %collective-permute-start.4 = (bf16[256,1280]{1,0:T(8,128)(2,1)S(1)}, bf16[256,1280]{1,0:T(8,128)(2,1)S(1)}, u32[]{:S(2)}, u32[]{:S(2)}) collective-permute-start(bf16[256,1280]{1,0:T(8,128)(2,1)S(1)} %collective-permute-done.1.refs_5_), channel_id=1, source_target_pairs={{0,96},{96,0},{1,97},{97,1},{2,98},{98,2},{3,99},{99,3},{4,100},{1... | collective-permute-start | bytes 1966088 | tf_op jit(solution)/shard_map/ppermute | solution.py:37
  56.2 12.1 %collective-permute-start.10 = (bf16[128,1280]{1,0:T(8,128)(2,1)S(1)}, bf16[128,1280]{1,0:T(8,128)(2,1)S(1)}, u32[]{:S(2)}, u32[]{:S(2)}) collective-permute-start(bf16[128,1280]{1,0:T(8,128)(2,1)S(1)} %collective-permute-done.3.refs_13_), channel_id=1, source_target_pairs={{0,96},{96,0},{1,97},{97,1},{2,98},{98,2},{3,99},{99,3},{4,100},{1... | collective-permute-start | bytes 983048 | tf_op jit(solution)/shard_map/ppermute | solution.py:37
  58.1 10.2 %collective-permute-start.9 = (bf16[128,1280]{1,0:T(8,128)(2,1)S(1)}, bf16[128,1280]{1,0:T(8,128)(2,1)}, u32[]{:S(2)}, u32[]{:S(2)}) collective-permute-start(bf16[128,1280]{1,0:T(8,128)(2,1)S(1)} %collective-permute-done.2.refs_11_), channel_id=1, source_target_pairs={{0,96},{96,0},{1,97},{97,1},{2,98},{98,2},{3,99},{99,3},{4,100},{1... | collective-permute-start | bytes 983048 | tf_op jit(solution)/shard_map/ppermute | solution.py:37
  60.5 7.8 %copy-start.13 = (bf16[128,1280]{1,0:T(8,128)(2,1)}, bf16[128,1280]{1,0:T(8,128)(2,1)S(1)}, u32[]{:S(2)}) copy-start(bf16[128,1280]{1,0:T(8,128)(2,1)S(1)} %collective-permute-done.7.refs_9_) | copy-start | bytes 983044
  60.5 7.8 %collective-permute-start.8 = (bf16[128,1280]{1,0:T(8,128)(2,1)S(1)}, bf16[128,1280]{1,0:T(8,128)(2,1)}, u32[]{:S(2)}, u32[]{:S(2)}) collective-permute-start(bf16[128,1280]{1,0:T(8,128)(2,1)S(1)} %collective-permute-done.7.refs_9_), channel_id=1, source_target_pairs={{0,96},{96,0},{1,97},{97,1},{2,98},{98,2},{3,99},{99,3},{4,100},{1... | collective-permute-start | bytes 983048 | tf_op jit(solution)/shard_map/ppermute | solution.py:37
  62.5 5.9 %copy-start.14 = (bf16[128,1280]{1,0:T(8,128)(2,1)}, bf16[128,1280]{1,0:T(8,128)(2,1)S(1)}, u32[]{:S(2)}) copy-start(bf16[128,1280]{1,0:T(8,128)(2,1)S(1)} %collective-permute-done.5.refs_7_) | copy-start | bytes 983044
  62.5 5.8 %collective-permute-start.6 = (bf16[128,1280]{1,0:T(8,128)(2,1)S(1)}, bf16[128,1280]{1,0:T(8,128)(2,1)}, u32[]{:S(2)}, u32[]{:S(2)}) collective-permute-start(bf16[128,1280]{1,0:T(8,128)(2,1)S(1)} %collective-permute-done.5.refs_7_), channel_id=1, source_target_pairs={{0,96},{96,0},{1,97},{97,1},{2,98},{98,2},{3,99},{99,3},{4,100},{1... | collective-permute-start | bytes 983048 | tf_op jit(solution)/shard_map/ppermute | solution.py:37
  68.3 0.7 copy-start.15
  69.1 0.8 copy-start.11
  81.3 14.2 %all-to-all-start.1 = ((f32[8,2,80]{2,1,0:T(2,128)}), f32[8,2,80]{2,1,0:T(2,128)S(1)}, u32[]{:S(2)}, u32[]{:S(2)}) async-start(f32[8,2,80]{2,1,0:T(2,128)} %bitcast.14), calls=%async_computation.1 | async-start | bytes 16384 | tf_op jit(solution)/shard_map/all_to_all | solution.py:201
  90.9 0.7 copy-start.10
  96.5 24.7 %all-to-all-start.2 = ((f32[96,1,672]{2,1,0:T(1,128)}), f32[96,1,672]{2,1,0:T(1,128)S(1)}, u32[]{:S(2)}, u32[]{:S(2)}) async-start(f32[96,1,672]{2,1,0:T(1,128)} %broadcast_in_dim.15), calls=%async_computation.2 | async-start | bytes 589824 | tf_op jit(solution)/shard_map/all_to_all | solution.py:33
  104.3 0.7 copy-start.9
  121.9 7.6 %copy-start.5 = (f32[256,640]{1,0:T(8,128)S(1)}, f32[256,640]{1,0:T(8,128)}, u32[]{:S(2)}) copy-start(f32[256,640]{1,0:T(8,128)} %get-tuple-element.26) | copy-start | bytes 1966084
  122.0 7.5 %copy-start.1 = (bf16[256,640]{1,0:T(8,128)(2,1)S(1)}, bf16[256,640]{1,0:T(8,128)(2,1)}, u32[]{:S(2)}) copy-start(bf16[256,640]{1,0:T(8,128)(2,1)} %refs_1_.1) | copy-start | bytes 983044
  122.7 11.4 %all-to-all-start.3 = ((f32[8,1,1280]{2,1,0:T(1,128)}), f32[8,1,1280]{2,1,0:T(1,128)S(1)}, u32[]{:S(2)}, u32[]{:S(2)}) async-start(f32[8,1,1280]{2,1,0:T(1,128)} %broadcast_in_dim.34), calls=%async_computation.3 | async-start | bytes 81920 | tf_op jit(solution)/shard_map/all_to_all | solution.py:33
  129.5 1.0 copy-start.3
  129.5 1.3 copy-start.4

commit v4 on v3

--- a/solution.py
+++ b/solution.py
@@ -25,8 +25,8 @@
 NT = ((1,), (1,))
 NN = ((1,), (0,))
 TN = ((0,), (0,))
-KEY_BLOCKS = 11
-BLOCKS_USED = (1, 3, 7, 11)
+KEY_BLOCKS = 7
+BLOCKS_USED = (1, 3, 5, 7)
 
 
 def from_all(x, axes, devices):
@@ -38,20 +38,19 @@
 
 
 def gather_first(block):
-    rows = block.shape[0] // 2
     near = lax.ppermute(block, "x", [(0, 1), (1, 2), (2, 3)])
-    far_high = lax.ppermute(block[rows:], "x", [(0, 3), (1, 0)])
-    far_low = lax.ppermute(block[:rows], "x", [(0, 3)])
+    far = lax.ppermute(block, FRAME, [(0, 6), (1, 7), (3, 1)])
     sibling = lax.ppermute(block, "core", [(0, 1)])
-    return sibling, near, far_high, far_low
-
-
-def gather_second(near, far_high, far_low):
-    middle_high = lax.ppermute(far_high, "x", [(0, 3), (3, 2)])
-    onward = jnp.where(lax.axis_index("x") == 3, far_low, near[: far_low.shape[0]])
-    middle_low = lax.ppermute(onward, "x", [(2, 3), (3, 2)])
-    blocks = (near, middle_high, middle_low, far_high, far_low)
-    return [b for block in blocks for b in (block, other_core(block))]
+    return sibling, near, far
+
+
+def gather_second(near, far, squares):
+    onward = jnp.where(lax.axis_index("x") == 2, near, far)
+    middle = lax.ppermute(onward, FRAME, [(4, 6), (1, 7), (6, 4), (7, 5)])
+    half_squares = lax.ppermute(squares, "half", [(0, 1), (1, 0)])
+    near_other, far_other = other_core(near), other_core(far)
+    middle, half_squares = lax.optimization_barrier((middle, half_squares))
+    return [near, near_other, middle, other_core(middle), far, far_other], half_squares
 
 
 def dot(a, b, dims):
@@ -67,7 +66,7 @@
     return jnp.transpose(jnp.broadcast_to(row, (8, row.shape[1])))[:, :1]
 
 
-def attention_kernel(where_ref, squares_ref, gain_q_ref, gain_k_ref, *refs):
+def attention_kernel(where_ref, squares_ref, half_squares_ref, gain_q_ref, gain_k_ref, *refs):
     sources, refs = refs[: 4 + KEY_BLOCKS], refs[4 + KEY_BLOCKS :]
     att_ref, flat_q_ref, flat_k_ref, gv_ref, inner_ref, part_ref, expo_ref, sum_q_ref, sum_k_ref = refs[:9]
     local, arrived = refs[9:-1], refs[-1]
@@ -80,7 +79,7 @@
     q_ref, k_ref, v_ref, do_ref = local[:4]
     pairs = local[4:]
     rows, width = q_ref.shape
-    rates = lax.rsqrt(jnp.sum(squares_ref[...], axis=0, keepdims=True) / D + EPSILON)
+    rates = lax.rsqrt((squares_ref[...] + half_squares_ref[...]) / D + EPSILON)
     rate_q, rate_k = column(rates[:, :rows]), column(rates[:, rows:])
     own_x, own_core = where_ref[0], where_ref[1]
     sum_q_ref[...] = jnp.zeros_like(sum_q_ref)
@@ -162,7 +161,7 @@
     fetched = [queries, noisy_keys, noisy_values, out_grad, *pairs]
     return pl.pallas_call(
         attention_kernel,
-        in_specs=[pl.BlockSpec(memory_space=pltpu.SMEM)] + [whole] * 3 + [pl.BlockSpec(memory_space=pl.ANY)] * len(fetched),
+        in_specs=[pl.BlockSpec(memory_space=pltpu.SMEM)] + [whole] * 4 + [pl.BlockSpec(memory_space=pl.ANY)] * len(fetched),
         out_specs=[whole] * 6,
         scratch_shapes=[
             pltpu.VMEM((FRAMES * rows, rows), jnp.float32),
@@ -175,7 +174,7 @@
         compiler_params=pltpu.CompilerParams(vmem_limit_bytes=56 * 1024 * 1024),
         cost_estimate=pl.CostEstimate(flops=8_000_000_000, bytes_accessed=10_000_000, transcendentals=2_600_000),
         name="attention",
-    )(where, squares, gain_q, gain_k, *fetched)
+    )(where, *squares, gain_q, gain_k, *fetched)
 
 
 def on_device(
@@ -188,13 +187,17 @@
     first = gather_first(jnp.concatenate([clean_keys, clean_values], axis=1))
     q_full = queries.astype(jnp.float32)
     k_full = noisy_keys.astype(jnp.float32)
-    squares = jnp.concatenate([jnp.sum(q_full * q_full, axis=1), jnp.sum(k_full * k_full, axis=1)])
-    squares = from_all(squares, HALF_HEAD, COLUMN_PARTS)
-    squares, (sibling, *received) = lax.optimization_barrier((squares, first))
-    pairs = [sibling] + gather_second(*received)
+    squares = jnp.concatenate([jnp.sum(q_full * q_full, axis=1), jnp.sum(k_full * k_full, axis=1)])[None]
+    squares = lax.psum(squares, "head")
     where = jnp.stack([lax.axis_index("x"), lax.axis_index("core")]).astype(jnp.int32)
+    squares, (sibling, *received), gain_q, gain_k, where = lax.optimization_barrier(
+        (squares, first, gain_q[None], gain_k[None], where)
+    )
+    before, half_squares = gather_second(*received, squares)
+    pairs = [sibling] + before
+    squares = (squares, half_squares)
     attended, flat_q, flat_k, grad_values, inners, parts = attention(
-        where, squares, gain_q[None], gain_k[None], queries, noisy_keys, noisy_values, out_grad, pairs
+        where, squares, gain_q, gain_k, queries, noisy_keys, noisy_values, out_grad, pairs
     )
     piece_width = width_dev // FRAMES
     pieces = parts.reshape(2, FRAMES, piece_width).transpose(1, 0, 2)
@@ -207,7 +210,7 @@
     gains = jnp.sum(got[:, :, :, 2 * length :], axis=1)
     gains = from_all(gains.reshape(COLUMN_PARTS * 2 * piece_width), FRAME, FRAMES)
     gains = gains.reshape(FRAMES, COLUMN_PARTS, 2, piece_width).transpose(2, 1, 0, 3).reshape(2, D)
-    totals = jnp.sum(squares, axis=0)
+    totals = squares[0][0] + squares[1][0]
     rate_q = lax.rsqrt(totals[:length] / D + EPSILON)
     rate_k = lax.rsqrt(totals[length:] / D + EPSILON)
     cube_q = rate_q * rate_q * rate_q * inners[0] / D

time: 137 us -> 126 us (0.920)
  waiting for transfers between devices: 36.3 us -> 24.2 us
  blocking collectives: 0 us -> 10.9 us
  starting transfers between devices: 71.6 us -> 63.6 us
    all_to_all x3 -> x2, starting transfers between devices: 34 us -> 20.2 us  [from_all(): lax.all_to_all(jnp.broadcast_to(x[None], (devices,) + x.shape), axes, 0, 0)]
    all_to_all x3 -> x2, waiting for transfers between devices: 32.4 us -> 18.6 us  [from_all(): lax.all_to_all(jnp.broadcast_to(x[None], (devices,) + x.shape), axes, 0, 0)]
    ppermute x4 -> x3, starting transfers between devices: 7.89 us -> 20.4 us  [the longest x1 16.5 us: gather_second(): half_squares = lax.ppermute(squares, 'half', [(0, 1), (1, 0)])]
    psum x0 -> x1, blocking collectives: none -> 10.9 us  [on_device(): squares = lax.psum(squares, 'head')]
    ppermute x5 -> x3, starting transfers between devices: 14.8 us -> 7.69 us  [other_core(): return lax.ppermute(block, 'core', [(0, 1), (1, 0)])]
    ppermute x5 -> x3, waiting for transfers between devices: 0.01 us -> 1.67 us  [other_core(): return lax.ppermute(block, 'core', [(0, 1), (1, 0)])]
    unnamed x35 -> x40, local copies, waits for them, and re-layouts: 4.99 us -> 4.46 us
  transfers between devices with their start and end apart: 15 -> 11, of which waited for: 4 -> 4; matrix products, arithmetic and copies ran while one was open for 5% -> 4% of each run, Pallas kernels for 0% -> 0%
where the time goes in v4:
time: 126 us; the launch traced here: 125 us
  starting transfers between devices  63.6 us (50%)
  waiting for transfers between devices  24.2 us (19%)
  local copies, waits for them, and re-layouts  12 us (10%)
  blocking collectives  10.9 us (9%)
  Pallas kernels  10 us (8%)
  other arithmetic  3.57 us (3%)
    all_to_all x2, starting transfers between devices, from_all(): lax.all_to_all(jnp.broadcast_to(x[None], (devices,) + x.shape), axes, 0, 0)  20.2 us
    all_to_all x2, waiting for transfers between devices, from_all(): lax.all_to_all(jnp.broadcast_to(x[None], (devices,) + x.shape), axes, 0, 0)  18.6 us
    ppermute x1, starting transfers between devices, gather_second(): half_squares = lax.ppermute(squares, 'half', [(0, 1), (1, 0)])  16.5 us
    psum x1, blocking collectives, on_device(): squares = lax.psum(squares, 'head')  10.9 us
    pallas_call x1, Pallas kernels, attention(): pl.pallas_call(attention_kernel, in_specs=[pl.BlockSpec(memory_space=pltp...  10 us
    all_to_all x1, starting transfers between devices, on_device(): piece = jnp.sum(lax.all_to_all(pieces, FRAME, 0, 0), axis=0)  9.91 us
    ppermute x3, starting transfers between devices, other_core(): return lax.ppermute(block, 'core', [(0, 1), (1, 0)])  7.69 us
    unnamed x40, local copies, waits for them, and re-layouts  4.46 us
  transfers between devices with their start and end apart: 11, of which 4 were waited for; matrix products, arithmetic and copies ran while one was open for 4% of the time, Pallas kernels for 0%

profile of v4, /device:TPU:1, one launch (start us, length us, event | category | flops | bytes accessed | tf_op | source)
XLA Modules:
  0.0 125.3 jit_solution(5268178881634037148)
XLA Ops:
  0.6 1.0 constant_dynamic-update-slice_fusion.1
  1.7 0.0 copy-done.8
  1.8 1.4 %collective-permute-start = (bf16[256,1280]{1,0:T(8,128)(2,1)S(1)}, bf16[256,1280]{1,0:T(8,128)(2,1)S(1)}, u32[]{:S(2)}, u32[]{:S(2)}) collective-permute-start(bf16[256,1280]{1,0:T(8,128)(2,1)S(1)} %constant_dynamic-update-slice_fusion), channel_id=1, source_target_pairs={{0,96},{1,97},{2,98},{3,99},{4,100},{5,101},{6,102},{7,103},{8,104... | collective-permute-start | bytes 1966088 | tf_op jit(solution)/shard_map/ppermute | solution.py:43
  3.2 4.0 %collective-permute-start.1 = (bf16[256,1280]{1,0:T(8,128)(2,1)S(1)}, bf16[256,1280]{1,0:T(8,128)(2,1)S(1)}, u32[]{:S(2)}, u32[]{:S(2)}) collective-permute-start(bf16[256,1280]{1,0:T(8,128)(2,1)S(1)} %constant_dynamic-update-slice_fusion), channel_id=1, source_target_pairs={{0,192},{192,384},{384,576},{1,193},{193,385},{385,577},{2,194},{1... | collective-permute-start | bytes 1966088 | tf_op jit(solution)/shard_map/ppermute | solution.py:41
  7.2 2.5 %collective-permute-start.2 = (bf16[256,1280]{1,0:T(8,128)(2,1)S(1)}, bf16[256,1280]{1,0:T(8,128)(2,1)S(1)}, u32[]{:S(2)}, u32[]{:S(2)}) collective-permute-start(bf16[256,1280]{1,0:T(8,128)(2,1)S(1)} %constant_dynamic-update-slice_fusion), channel_id=1, source_target_pairs={{0,576},{96,672},{288,96},{1,577},{97,673},{289,97},{2,578},{98,67... | collective-permute-start | bytes 1966088 | tf_op jit(solution)/shard_map/ppermute | solution.py:42
  9.7 0.8 dynamic_slice.10
  10.5 0.6 broadcast_in_dim.13.gain_q_ref
  11.1 0.8 dynamic_slice.11
  11.9 0.6 broadcast_in_dim.28.gain_k_ref
  12.5 0.2 fusion
  12.7 10.9 %psum.7.squares_ref = f32[1,512]{1,0:T(1,128)S(1)} all-reduce(f32[1,512]{1,0:T(1,128)S(1)} %bitcast.21), channel_id=1, replica_groups=mesh['x'=4,'core'=2,'half'=2,'video_z'=6,'video_y'=2,'head'=4] {'head'}, use_global_device_ids=true, to_apply=%region_2.0 | all-reduce | flops 512 | bytes 4096 | tf_op jit(solution)/shard_map/psum | solution.py:191
  23.6 0.6 pad_add_fusion.where_ref
  24.2 0.1 broadcast_select_fusion
  24.3 0.7 copy-done.14
  25.0 1.3 %collective-permute-start.3 = (bf16[256,1280]{1,0:T(8,128)(2,1)S(1)}, bf16[256,1280]{1,0:T(8,128)(2,1)S(1)}, u32[]{:S(2)}, u32[]{:S(2)}) collective-permute-start(bf16[256,1280]{1,0:T(8,128)(2,1)S(1)} %broadcast_select_fusion), channel_id=1, source_target_pairs={{384,576},{96,672},{576,384},{672,480},{385,577},{97,673},{577,385... | collective-permute-start | bytes 1966088 | tf_op jit(solution)/shard_map/ppermute | solution.py:49
  26.4 16.5 %collective-permute-start.4 = (f32[1,512]{1,0:T(1,128)S(1)}, f32[1,512]{1,0:T(1,128)S(1)}, u32[]{:S(2)}, u32[]{:S(2)}) collective-permute-start(f32[1,512]{1,0:T(1,128)S(1)} %psum.7.squares_ref), channel_id=1, source_target_pairs={{0,48},{48,0},{1,49},{49,1},{2,50},{50,2},{3,51},{51,3},{4,52},{52... | collective-permute-start | bytes 6152 | tf_op jit(solution)/shard_map/ppermute | solution.py:50
  42.9 3.4 %collective-permute-start.5 = (bf16[256,1280]{1,0:T(8,128)(2,1)S(1)}, bf16[256,1280]{1,0:T(8,128)(2,1)S(1)}, u32[]{:S(2)}, u32[]{:S(2)}) collective-permute-start(bf16[256,1280]{1,0:T(8,128)(2,1)S(1)} %collective-permute-done.1.refs_5_), channel_id=1, source_target_pairs={{0,96},{96,0},{1,97},{97,1},{2,98},{98,2},{3,99},{99,3},{4,100},{1... | collective-permute-start | bytes 1966088 | tf_op jit(solution)/shard_map/ppermute | solution.py:37
  46.3 1.9 %collective-permute-start.7 = (bf16[256,1280]{1,0:T(8,128)(2,1)S(1)}, bf16[256,1280]{1,0:T(8,128)(2,1)S(1)}, u32[]{:S(2)}, u32[]{:S(2)}) collective-permute-start(bf16[256,1280]{1,0:T(8,128)(2,1)S(1)} %collective-permute-done.2.refs_9_), channel_id=1, source_target_pairs={{0,96},{96,0},{1,97},{97,1},{2,98},{98,2},{3,99},{99,3},{4,100},{1... | collective-permute-start | bytes 1966088 | tf_op jit(solution)/shard_map/ppermute | solution.py:37
  48.3 2.4 %collective-permute-start.6 = (bf16[256,1280]{1,0:T(8,128)(2,1)S(1)}, bf16[256,1280]{1,0:T(8,128)(2,1)S(1)}, u32[]{:S(2)}, u32[]{:S(2)}) collective-permute-start(bf16[256,1280]{1,0:T(8,128)(2,1)S(1)} %collective-permute-done.3.refs_7_), channel_id=1, source_target_pairs={{0,96},{96,0},{1,97},{97,1},{2,98},{98,2},{3,99},{99,3},{4,100},{1... | collective-permute-start | bytes 1966088 | tf_op jit(solution)/shard_map/ppermute | solution.py:37
  50.7 1.7 %collective-permute-done.6.refs_8_ = bf16[256,1280]{1,0:T(8,128)(2,1)S(1)} collective-permute-done((bf16[256,1280]{1,0:T(8,128)(2,1)S(1)}, bf16[256,1280]{1,0:T(8,128)(2,1)S(1)}, u32[]{:S(2)}, u32[]{:S(2)}) %collective-permute-start.6) | collective-permute-done | bytes 655392 | tf_op jit(solution)/shard_map/ppermute | solution.py:37
  52.4 0.8 copy-done.18
  53.2 10.0 %attention.1 = (bf16[256,640]{1,0:T(8,128)(2,1)}, f32[256,640]{1,0:T(8,128)}, f32[256,640]{1,0:T(8,128)}, bf16[256,640]{1,0:T(8,128)(2,1)}, f32[2,256]{1,0:T(2,128)}, /*index=5*/f32[2,640]{1,0:T(2,128)}) custom-call(s32[2]{0:T(128)} %pad_add_fusion.where_ref, f32[1,512]{1,0:T(1,128)} %copy-done.9, f32[1,512]{1,0:T(1,128)} %copy-done.11, ...), custom_call_target="tpu_custom_call" | custom-call | flops 8000000000 | bytes 10000000 | tf_op jit(solution)/shard_map/attention/pallas_call | solution.py:162
  63.3 0.8 reshape.71
  64.1 0.6 copy.28
  64.7 9.9 %all-to-all-start = ((f32[8,2,80]{2,1,0:T(2,128)}), f32[8,2,80]{2,1,0:T(2,128)S(1)}, u32[]{:S(2)}, u32[]{:S(2)}) async-start(f32[8,2,80]{2,1,0:T(2,128)} %bitcast.14), calls=%async_computation | async-start | bytes 16384 | tf_op jit(solution)/shard_map/all_to_all | solution.py:204
  74.6 0.7 copy-done.13
  75.3 3.9 %all-to-all-done = f32[8,2,80]{2,1,0:T(2,128)S(1)} async-done(((f32[8,2,80]{2,1,0:T(2,128)}), f32[8,2,80]{2,1,0:T(2,128)S(1)}, u32[]{:S(2)}, u32[]{:S(2)}) %all-to-all-start) | async-done | bytes 5152 | tf_op jit(solution)/shard_map/all_to_all | solution.py:204
  79.2 0.1 reshape.72
  79.3 0.9 broadcast_in_dim.29
  80.2 13.5 %all-to-all-start.1 = ((f32[96,1,672]{2,1,0:T(1,128)}), f32[96,1,672]{2,1,0:T(1,128)S(1)}, u32[]{:S(2)}, u32[]{:S(2)}) async-start(f32[96,1,672]{2,1,0:T(1,128)} %broadcast_in_dim.29), calls=%async_computation.1 | async-start | bytes 589824 | tf_op jit(solution)/shard_map/all_to_all | solution.py:33
  93.8 0.6 copy-done.12
  94.4 0.0 copy-done.10
  94.5 16.1 %all-to-all-done.1 = f32[96,1,672]{2,1,0:T(1,128)S(1)} async-done(((f32[96,1,672]{2,1,0:T(1,128)}), f32[96,1,672]{2,1,0:T(1,128)S(1)}, u32[]{:S(2)}, u32[]{:S(2)}) %all-to-all-start.1) | async-done | bytes 258080 | tf_op jit(solution)/shard_map/all_to_all | solution.py:33
  110.6 0.7 reduce.1
  111.3 0.1 reshape.73
  111.4 0.1 broadcast_in_dim.30
  111.5 0.6 broadcast_in_dim.31
  112.1 6.7 %all-to-all-start.2 = ((f32[8,1,1280]{2,1,0:T(1,128)}), f32[8,1,1280]{2,1,0:T(1,128)S(1)}, u32[]{:S(2)}, u32[]{:S(2)}) async-start(f32[8,1,1280]{2,1,0:T(1,128)} %broadcast_in_dim.31), calls=%async_computation.2 | async-start | bytes 81920 | tf_op jit(solution)/shard_map/all_to_all | solution.py:33
  118.9 0.9 fusion.5
  119.8 0.1 copy-done.3
  119.8 0.3 copy-done.6
  120.2 0.9 fusion.2
  121.1 2.5 %all-to-all-done.2 = f32[8,1,1280]{2,1,0:T(1,128)S(1)} async-done(((f32[8,1,1280]{2,1,0:T(1,128)}), f32[8,1,1280]{2,1,0:T(1,128)S(1)}, u32[]{:S(2)}, u32[]{:S(2)}) %all-to-all-start.2) | async-done | bytes 40992 | tf_op jit(solution)/shard_map/all_to_all | solution.py:33
  123.6 0.1 reduce.2
  123.7 0.2 reshape.74
  123.8 0.1 fusion.14
  123.9 0.7 squeeze.6
  124.6 0.7 squeeze.7
  (50 shorter events, 0.3 us)
Async XLA Ops:
  0.6 1.1 copy-start.8
  1.7 10.8 %copy-start = (bf16[256,640]{1,0:T(8,128)(2,1)S(1)}, bf16[256,640]{1,0:T(8,128)(2,1)}, u32[]{:S(2)}) copy-start(bf16[256,640]{1,0:T(8,128)(2,1)} %refs_1_.1) | copy-start | bytes 983044
  1.7 10.7 %copy-start.2 = (bf16[256,640]{1,0:T(8,128)(2,1)S(1)}, bf16[256,640]{1,0:T(8,128)(2,1)}, u32[]{:S(2)}) copy-start(bf16[256,640]{1,0:T(8,128)(2,1)} %refs_0_.1) | copy-start | bytes 983044
  1.8 22.4 %collective-permute-start = (bf16[256,1280]{1,0:T(8,128)(2,1)S(1)}, bf16[256,1280]{1,0:T(8,128)(2,1)S(1)}, u32[]{:S(2)}, u32[]{:S(2)}) collective-permute-start(bf16[256,1280]{1,0:T(8,128)(2,1)S(1)} %constant_dynamic-update-slice_fusion), channel_id=1, source_target_pairs={{0,96},{1,97},{2,98},{3,99},{4,100},{5,101},{6,102},{7,103},{8,104... | collective-permute-start | bytes 1966088 | tf_op jit(solution)/shard_map/ppermute | solution.py:43
  3.2 21.0 %collective-permute-start.1 = (bf16[256,1280]{1,0:T(8,128)(2,1)S(1)}, bf16[256,1280]{1,0:T(8,128)(2,1)S(1)}, u32[]{:S(2)}, u32[]{:S(2)}) collective-permute-start(bf16[256,1280]{1,0:T(8,128)(2,1)S(1)} %constant_dynamic-update-slice_fusion), channel_id=1, source_target_pairs={{0,192},{192,384},{384,576},{1,193},{193,385},{385,577},{2,194},{1... | collective-permute-start | bytes 1966088 | tf_op jit(solution)/shard_map/ppermute | solution.py:41
  7.2 17.0 %collective-permute-start.2 = (bf16[256,1280]{1,0:T(8,128)(2,1)S(1)}, bf16[256,1280]{1,0:T(8,128)(2,1)S(1)}, u32[]{:S(2)}, u32[]{:S(2)}) collective-permute-start(bf16[256,1280]{1,0:T(8,128)(2,1)S(1)} %constant_dynamic-update-slice_fusion), channel_id=1, source_target_pairs={{0,576},{96,672},{288,96},{1,577},{97,673},{289,97},{2,578},{98,67... | collective-permute-start | bytes 1966088 | tf_op jit(solution)/shard_map/ppermute | solution.py:42
  23.6 2.8 %copy-start.9 = (f32[1,512]{1,0:T(1,128)}, f32[1,512]{1,0:T(1,128)S(1)}, u32[]{:S(2)}) copy-start(f32[1,512]{1,0:T(1,128)S(1)} %psum.7.squares_ref) | copy-start | bytes 6148
  24.2 0.9 copy-start.14
  24.2 18.7 %copy-start.4 = (bf16[256,1280]{1,0:T(8,128)(2,1)}, bf16[256,1280]{1,0:T(8,128)(2,1)S(1)}, u32[]{:S(2)}) copy-start(bf16[256,1280]{1,0:T(8,128)(2,1)S(1)} %collective-permute-done.1.refs_5_) | copy-start | bytes 1966084
  24.2 22.1 %copy-start.5 = (bf16[256,1280]{1,0:T(8,128)(2,1)}, bf16[256,1280]{1,0:T(8,128)(2,1)S(1)}, u32[]{:S(2)}) copy-start(bf16[256,1280]{1,0:T(8,128)(2,1)S(1)} %collective-permute-done.2.refs_9_) | copy-start | bytes 1966084
  25.0 23.2 %collective-permute-start.3 = (bf16[256,1280]{1,0:T(8,128)(2,1)S(1)}, bf16[256,1280]{1,0:T(8,128)(2,1)S(1)}, u32[]{:S(2)}, u32[]{:S(2)}) collective-permute-start(bf16[256,1280]{1,0:T(8,128)(2,1)S(1)} %broadcast_select_fusion), channel_id=1, source_target_pairs={{384,576},{96,672},{576,384},{672,480},{385,577},{97,673},{577,385... | collective-permute-start | bytes 1966088 | tf_op jit(solution)/shard_map/ppermute | solution.py:49
  26.4 21.9 %collective-permute-start.4 = (f32[1,512]{1,0:T(1,128)S(1)}, f32[1,512]{1,0:T(1,128)S(1)}, u32[]{:S(2)}, u32[]{:S(2)}) collective-permute-start(f32[1,512]{1,0:T(1,128)S(1)} %psum.7.squares_ref), channel_id=1, source_target_pairs={{0,48},{48,0},{1,49},{49,1},{2,50},{50,2},{3,51},{51,3},{4,52},{52... | collective-permute-start | bytes 6152 | tf_op jit(solution)/shard_map/ppermute | solution.py:50
  42.9 7.8 %collective-permute-start.5 = (bf16[256,1280]{1,0:T(8,128)(2,1)S(1)}, bf16[256,1280]{1,0:T(8,128)(2,1)S(1)}, u32[]{:S(2)}, u32[]{:S(2)}) collective-permute-start(bf16[256,1280]{1,0:T(8,128)(2,1)S(1)} %collective-permute-done.1.refs_5_), channel_id=1, source_target_pairs={{0,96},{96,0},{1,97},{97,1},{2,98},{98,2},{3,99},{99,3},{4,100},{1... | collective-permute-start | bytes 1966088 | tf_op jit(solution)/shard_map/ppermute | solution.py:37
  46.3 4.4 %collective-permute-start.7 = (bf16[256,1280]{1,0:T(8,128)(2,1)S(1)}, bf16[256,1280]{1,0:T(8,128)(2,1)S(1)}, u32[]{:S(2)}, u32[]{:S(2)}) collective-permute-start(bf16[256,1280]{1,0:T(8,128)(2,1)S(1)} %collective-permute-done.2.refs_9_), channel_id=1, source_target_pairs={{0,96},{96,0},{1,97},{97,1},{2,98},{98,2},{3,99},{99,3},{4,100},{1... | collective-permute-start | bytes 1966088 | tf_op jit(solution)/shard_map/ppermute | solution.py:37
  48.2 4.1 %copy-start.11 = (f32[1,512]{1,0:T(1,128)}, f32[1,512]{1,0:T(1,128)S(1)}, u32[]{:S(2)}) copy-start(f32[1,512]{1,0:T(1,128)S(1)} %collective-permute-done.4.half_squares_ref) | copy-start | bytes 6148
  48.2 4.1 %copy-start.15 = (bf16[256,1280]{1,0:T(8,128)(2,1)}, bf16[256,1280]{1,0:T(8,128)(2,1)S(1)}, u32[]{:S(2)}) copy-start(bf16[256,1280]{1,0:T(8,128)(2,1)S(1)} %collective-permute-done.3.refs_7_) | copy-start | bytes 1966084
  48.3 4.1 %collective-permute-start.6 = (bf16[256,1280]{1,0:T(8,128)(2,1)S(1)}, bf16[256,1280]{1,0:T(8,128)(2,1)S(1)}, u32[]{:S(2)}, u32[]{:S(2)}) collective-permute-start(bf16[256,1280]{1,0:T(8,128)(2,1)S(1)} %collective-permute-done.3.refs_7_), channel_id=1, source_target_pairs={{0,96},{96,0},{1,97},{97,1},{2,98},{98,2},{3,99},{99,3},{4,100},{1... | collective-permute-start | bytes 1966088 | tf_op jit(solution)/shard_map/ppermute | solution.py:37
  50.7 1.7 %copy-start.16 = (bf16[256,1280]{1,0:T(8,128)(2,1)}, bf16[256,1280]{1,0:T(8,128)(2,1)S(1)}, u32[]{:S(2)}) copy-start(bf16[256,1280]{1,0:T(8,128)(2,1)S(1)} %collective-permute-done.5.refs_6_) | copy-start | bytes 1966084
  50.7 1.7 %copy-start.17 = (bf16[256,1280]{1,0:T(8,128)(2,1)}, bf16[256,1280]{1,0:T(8,128)(2,1)S(1)}, u32[]{:S(2)}) copy-start(bf16[256,1280]{1,0:T(8,128)(2,1)S(1)} %collective-permute-done.7.refs_10_) | copy-start | bytes 1966084
  52.4 0.9 copy-start.18
  64.7 14.5 %all-to-all-start = ((f32[8,2,80]{2,1,0:T(2,128)}), f32[8,2,80]{2,1,0:T(2,128)S(1)}, u32[]{:S(2)}, u32[]{:S(2)}) async-start(f32[8,2,80]{2,1,0:T(2,128)} %bitcast.14), calls=%async_computation | async-start | bytes 16384 | tf_op jit(solution)/shard_map/all_to_all | solution.py:204
  74.6 0.7 copy-start.13
  80.2 30.4 %all-to-all-start.1 = ((f32[96,1,672]{2,1,0:T(1,128)}), f32[96,1,672]{2,1,0:T(1,128)S(1)}, u32[]{:S(2)}, u32[]{:S(2)}) async-start(f32[96,1,672]{2,1,0:T(1,128)} %broadcast_in_dim.29), calls=%async_computation.1 | async-start | bytes 589824 | tf_op jit(solution)/shard_map/all_to_all | solution.py:33
  93.8 0.7 copy-start.12
  93.8 0.7 copy-start.10
  111.3 7.6 %copy-start.7 = (f32[256,640]{1,0:T(8,128)S(1)}, f32[256,640]{1,0:T(8,128)}, u32[]{:S(2)}) copy-start(f32[256,640]{1,0:T(8,128)} %get-tuple-element.34) | copy-start | bytes 1966084
  111.4 7.5 %copy-start.1 = (bf16[256,640]{1,0:T(8,128)(2,1)S(1)}, bf16[256,640]{1,0:T(8,128)(2,1)}, u32[]{:S(2)}) copy-start(bf16[256,640]{1,0:T(8,128)(2,1)} %refs_1_.1) | copy-start | bytes 983044
  112.1 11.4 %all-to-all-start.2 = ((f32[8,1,1280]{2,1,0:T(1,128)}), f32[8,1,1280]{2,1,0:T(1,128)S(1)}, u32[]{:S(2)}, u32[]{:S(2)}) async-start(f32[8,1,1280]{2,1,0:T(1,128)} %broadcast_in_dim.31), calls=%async_computation.2 | async-start | bytes 81920 | tf_op jit(solution)/shard_map/all_to_all | solution.py:33
  118.8 1.0 copy-start.3
  118.9 1.3 %copy-start.6 = (f32[256,640]{1,0:T(8,128)S(1)}, f32[256,640]{1,0:T(8,128)}, u32[]{:S(2)}) copy-start(f32[256,640]{1,0:T(8,128)} %get-tuple-element.31) | copy-start | bytes 1966084

commit v5 on v4

--- a/solution.py
+++ b/solution.py
@@ -70,21 +70,27 @@
     sources, refs = refs[: 4 + KEY_BLOCKS], refs[4 + KEY_BLOCKS :]
     att_ref, flat_q_ref, flat_k_ref, gv_ref, inner_ref, part_ref, expo_ref, sum_q_ref, sum_k_ref = refs[:9]
     local, arrived = refs[9:-1], refs[-1]
-    copies = [
-        pltpu.make_async_copy(source, target, arrived.at[i])
-        for i, (source, target) in enumerate(zip(sources, local))
-    ]
-    for copy in copies:
-        copy.start()
+    width = sources[0].shape[1]
+    copies = []
+    for low, high in ((0, DH), (DH, width)):
+        group = []
+        for source, target in zip(sources, local):
+            for base in range(0, source.shape[1], width):
+                lanes = slice(base + low, base + high)
+                number = len(group) + sum(map(len, copies))
+                group.append(pltpu.make_async_copy(source.at[:, lanes], target.at[:, lanes], arrived.at[number]))
+        copies.append(group)
+        for copy in group:
+            copy.start()
     q_ref, k_ref, v_ref, do_ref = local[:4]
     pairs = local[4:]
-    rows, width = q_ref.shape
+    rows = q_ref.shape[0]
     rates = lax.rsqrt((squares_ref[...] + half_squares_ref[...]) / D + EPSILON)
     rate_q, rate_k = column(rates[:, :rows]), column(rates[:, rows:])
-    own_x, own_core = where_ref[0], where_ref[1]
+    own_x, own_core = where_ref[0] // 2, where_ref[0] % 2
     sum_q_ref[...] = jnp.zeros_like(sum_q_ref)
     sum_k_ref[...] = jnp.zeros_like(sum_k_ref)
-    for copy in copies:
+    for copy in copies[0]:
         copy.wait()
 
     def one_head(remote, start):
@@ -142,13 +148,16 @@
         sum_q_ref[...] += q_full * flat_q
         sum_k_ref[...] += k_full * flat_k
 
-    def run(remote):
-        @pl.loop(0, width, step=DH)
-        def _(start):
-            one_head(remote, start)
-
-    for remote in range(4):
-        pl.when(own_x == remote)(functools.partial(run, remote))
+    @pl.loop(0, width, step=DH)
+    def _(start):
+        @pl.when(start == DH)
+        def _():
+            for copy in copies[1]:
+                copy.wait()
+
+        for remote in range(len(BLOCKS_USED)):
+            pl.when(own_x == remote)(functools.partial(one_head, remote, start))
+
     inner_ref[0:1, :] = jnp.sum(jnp.transpose(sum_q_ref[...]), axis=0, keepdims=True)
     inner_ref[1:2, :] = jnp.sum(jnp.transpose(sum_k_ref[...]), axis=0, keepdims=True)
 
@@ -168,7 +177,7 @@
             pltpu.VMEM((rows, DH), jnp.float32),
             pltpu.VMEM((rows, DH), jnp.float32),
             *[pltpu.VMEM(x.shape, x.dtype) for x in fetched],
-            pltpu.SemaphoreType.DMA((len(fetched),)),
+            pltpu.SemaphoreType.DMA((2 * (4 + 2 * KEY_BLOCKS),)),
         ],
         out_shape=[low, f32(rows, width), f32(rows, width), low, f32(2, rows), f32(2, width)],
         compiler_params=pltpu.CompilerParams(vmem_limit_bytes=56 * 1024 * 1024),
@@ -189,7 +198,7 @@
     k_full = noisy_keys.astype(jnp.float32)
     squares = jnp.concatenate([jnp.sum(q_full * q_full, axis=1), jnp.sum(k_full * k_full, axis=1)])[None]
     squares = lax.psum(squares, "head")
-    where = jnp.stack([lax.axis_index("x"), lax.axis_index("core")]).astype(jnp.int32)
+    where = lax.axis_index(FRAME).astype(jnp.int32).reshape(1)
     squares, (sibling, *received), gain_q, gain_k, where = lax.optimization_barrier(
         (squares, first, gain_q[None], gain_k[None], where)
     )
@@ -200,7 +209,7 @@
         where, squares, gain_q, gain_k, queries, noisy_keys, noisy_values, out_grad, pairs
     )
     piece_width = width_dev // FRAMES
-    pieces = parts.reshape(2, FRAMES, piece_width).transpose(1, 0, 2)
+    pieces = parts.reshape(FRAMES, 2 * piece_width)
     piece = jnp.sum(lax.all_to_all(pieces, FRAME, 0, 0), axis=0)
     sent = jnp.concatenate([inners.reshape(2 * length), piece.reshape(2 * piece_width)])
     got = from_all(sent, FSDP_HEAD, 2 * VIDEOS * HEAD_PARTS).reshape(2, VIDEOS, HEAD_PARTS, sent.shape[0])
@@ -209,7 +218,7 @@
     inners = jnp.sum(same_video, axis=(0, 1)).reshape(2, length)
     gains = jnp.sum(got[:, :, :, 2 * length :], axis=1)
     gains = from_all(gains.reshape(COLUMN_PARTS * 2 * piece_width), FRAME, FRAMES)
-    gains = gains.reshape(FRAMES, COLUMN_PARTS, 2, piece_width).transpose(2, 1, 0, 3).reshape(2, D)
+    gains = gains.reshape(2, FRAMES // 2, COLUMN_PARTS, 2 * piece_width).transpose(0, 2, 1, 3).reshape(2, D)
     totals = squares[0][0] + squares[1][0]
     rate_q = lax.rsqrt(totals[:length] / D + EPSILON)
     rate_k = lax.rsqrt(totals[length:] / D + EPSILON)

time: 126 us -> 125 us (level)
    reshape x4 -> x1, local copies, waits for them, and re-layouts: 1.63 us -> 0.09 us  [on_device(): gains.reshape(2, FRAMES // 2, COLUMN_PARTS, 2 * piece_width)]
    all_to_all x0 -> x1, local copies, waits for them, and re-layouts: none -> 1.38 us  [on_device(): piece = jnp.sum(lax.all_to_all(pieces, FRAME, 0, 0), axis=0)]
where the time goes in v5:
time: 125 us; the launch traced here: 124 us
  starting transfers between devices  63.8 us (51%)
  waiting for transfers between devices  24.2 us (19%)
  local copies, waits for them, and re-layouts  11.8 us (9%)
  blocking collectives  10.9 us (9%)
  Pallas kernels  9.38 us (8%)
  other arithmetic  2.98 us (2%)
    all_to_all x2, starting transfers between devices, from_all(): lax.all_to_all(jnp.broadcast_to(x[None], (devices,) + x.shape), axes, 0, 0)  20.8 us
    all_to_all x2, waiting for transfers between devices, from_all(): lax.all_to_all(jnp.broadcast_to(x[None], (devices,) + x.shape), axes, 0, 0)  18.6 us
    ppermute x1, starting transfers between devices, gather_second(): half_squares = lax.ppermute(squares, 'half', [(0, 1), (1, 0)])  17.1 us
    psum x1, blocking collectives, on_device(): squares = lax.psum(squares, 'head')  10.9 us
    all_to_all x1, starting transfers between devices, on_device(): piece = jnp.sum(lax.all_to_all(pieces, FRAME, 0, 0), axis=0)  9.48 us
    pallas_call x1, Pallas kernels, attention(): pl.pallas_call(attention_kernel, in_specs=[pl.BlockSpec(memory_space=pltp...  9.38 us
    ppermute x3, starting transfers between devices, other_core(): return lax.ppermute(block, 'core', [(0, 1), (1, 0)])  7.09 us
    unnamed x40, local copies, waits for them, and re-layouts  4.45 us
  transfers between devices with their start and end apart: 11, of which 4 were waited for; matrix products, arithmetic and copies ran while one was open for 4% of the time, Pallas kernels for 0%

profile of v5, /device:TPU:1, one launch (start us, length us, event | category | flops | bytes accessed | tf_op | source)
XLA Modules:
  0.0 124.0 jit_solution(9706146690239297090)
XLA Ops:
  0.6 1.0 constant_dynamic-update-slice_fusion.1
  1.7 0.0 copy-done.8
  1.7 0.0 copy-start.2
  1.8 1.4 %collective-permute-start = (bf16[256,1280]{1,0:T(8,128)(2,1)S(1)}, bf16[256,1280]{1,0:T(8,128)(2,1)S(1)}, u32[]{:S(2)}, u32[]{:S(2)}) collective-permute-start(bf16[256,1280]{1,0:T(8,128)(2,1)S(1)} %constant_dynamic-update-slice_fusion), channel_id=1, source_target_pairs={{0,96},{1,97},{2,98},{3,99},{4,100},{5,101},{6,102},{7,103},{8,104... | collective-permute-start | bytes 1966088 | tf_op jit(solution)/shard_map/ppermute | solution.py:43
  3.2 4.0 %collective-permute-start.1 = (bf16[256,1280]{1,0:T(8,128)(2,1)S(1)}, bf16[256,1280]{1,0:T(8,128)(2,1)S(1)}, u32[]{:S(2)}, u32[]{:S(2)}) collective-permute-start(bf16[256,1280]{1,0:T(8,128)(2,1)S(1)} %constant_dynamic-update-slice_fusion), channel_id=1, source_target_pairs={{0,192},{192,384},{384,576},{1,193},{193,385},{385,577},{2,194},{1... | collective-permute-start | bytes 1966088 | tf_op jit(solution)/shard_map/ppermute | solution.py:41
  7.2 2.5 %collective-permute-start.2 = (bf16[256,1280]{1,0:T(8,128)(2,1)S(1)}, bf16[256,1280]{1,0:T(8,128)(2,1)S(1)}, u32[]{:S(2)}, u32[]{:S(2)}) collective-permute-start(bf16[256,1280]{1,0:T(8,128)(2,1)S(1)} %constant_dynamic-update-slice_fusion), channel_id=1, source_target_pairs={{0,576},{96,672},{288,96},{1,577},{97,673},{289,97},{2,578},{98,67... | collective-permute-start | bytes 1966088 | tf_op jit(solution)/shard_map/ppermute | solution.py:42
  9.7 0.8 dynamic_slice.10
  10.5 0.6 broadcast_in_dim.13.gain_q_ref
  11.1 0.8 dynamic_slice.11
  11.9 0.6 broadcast_in_dim.28.gain_k_ref
  12.5 0.2 fusion
  12.7 10.9 %psum.7.squares_ref = f32[1,512]{1,0:T(1,128)S(1)} all-reduce(f32[1,512]{1,0:T(1,128)S(1)} %bitcast.13), channel_id=1, replica_groups=mesh['x'=4,'core'=2,'half'=2,'video_z'=6,'video_y'=2,'head'=4] {'head'}, use_global_device_ids=true, to_apply=%region_2.0 | all-reduce | flops 512 | bytes 4096 | tf_op jit(solution)/shard_map/psum | solution.py:200
  23.6 0.1 broadcast_select_fusion
  23.7 0.7 copy-done.14
  24.4 1.3 %collective-permute-start.3 = (bf16[256,1280]{1,0:T(8,128)(2,1)S(1)}, bf16[256,1280]{1,0:T(8,128)(2,1)S(1)}, u32[]{:S(2)}, u32[]{:S(2)}) collective-permute-start(bf16[256,1280]{1,0:T(8,128)(2,1)S(1)} %broadcast_select_fusion), channel_id=1, source_target_pairs={{384,576},{96,672},{576,384},{672,480},{385,577},{97,673},{577,385... | collective-permute-start | bytes 1966088 | tf_op jit(solution)/shard_map/ppermute | solution.py:49
  25.8 17.1 %collective-permute-start.4 = (f32[1,512]{1,0:T(1,128)S(1)}, f32[1,512]{1,0:T(1,128)S(1)}, u32[]{:S(2)}, u32[]{:S(2)}) collective-permute-start(f32[1,512]{1,0:T(1,128)S(1)} %psum.7.squares_ref), channel_id=1, source_target_pairs={{0,48},{48,0},{1,49},{49,1},{2,50},{50,2},{3,51},{51,3},{4,52},{52... | collective-permute-start | bytes 6152 | tf_op jit(solution)/shard_map/ppermute | solution.py:50
  42.9 2.8 %collective-permute-start.5 = (bf16[256,1280]{1,0:T(8,128)(2,1)S(1)}, bf16[256,1280]{1,0:T(8,128)(2,1)S(1)}, u32[]{:S(2)}, u32[]{:S(2)}) collective-permute-start(bf16[256,1280]{1,0:T(8,128)(2,1)S(1)} %collective-permute-done.1.refs_5_), channel_id=1, source_target_pairs={{0,96},{96,0},{1,97},{97,1},{2,98},{98,2},{3,99},{99,3},{4,100},{1... | collective-permute-start | bytes 1966088 | tf_op jit(solution)/shard_map/ppermute | solution.py:37
  45.7 1.9 %collective-permute-start.7 = (bf16[256,1280]{1,0:T(8,128)(2,1)S(1)}, bf16[256,1280]{1,0:T(8,128)(2,1)S(1)}, u32[]{:S(2)}, u32[]{:S(2)}) collective-permute-start(bf16[256,1280]{1,0:T(8,128)(2,1)S(1)} %collective-permute-done.2.refs_9_), channel_id=1, source_target_pairs={{0,96},{96,0},{1,97},{97,1},{2,98},{98,2},{3,99},{99,3},{4,100},{1... | collective-permute-start | bytes 1966088 | tf_op jit(solution)/shard_map/ppermute | solution.py:37
  47.7 2.4 %collective-permute-start.6 = (bf16[256,1280]{1,0:T(8,128)(2,1)S(1)}, bf16[256,1280]{1,0:T(8,128)(2,1)S(1)}, u32[]{:S(2)}, u32[]{:S(2)}) collective-permute-start(bf16[256,1280]{1,0:T(8,128)(2,1)S(1)} %collective-permute-done.3.refs_7_), channel_id=1, source_target_pairs={{0,96},{96,0},{1,97},{97,1},{2,98},{98,2},{3,99},{99,3},{4,100},{1... | collective-permute-start | bytes 1966088 | tf_op jit(solution)/shard_map/ppermute | solution.py:37
  50.1 1.7 %collective-permute-done.6.refs_8_ = bf16[256,1280]{1,0:T(8,128)(2,1)S(1)} collective-permute-done((bf16[256,1280]{1,0:T(8,128)(2,1)S(1)}, bf16[256,1280]{1,0:T(8,128)(2,1)S(1)}, u32[]{:S(2)}, u32[]{:S(2)}) %collective-permute-start.6) | collective-permute-done | bytes 655392 | tf_op jit(solution)/shard_map/ppermute | solution.py:37
  51.8 0.8 copy-done.18
  52.6 9.4 %attention.1 = (bf16[256,640]{1,0:T(8,128)(2,1)}, f32[256,640]{1,0:T(8,128)}, f32[256,640]{1,0:T(8,128)}, bf16[256,640]{1,0:T(8,128)(2,1)}, f32[2,256]{1,0:T(2,128)}, /*index=5*/f32[2,640]{1,0:T(2,128)}) custom-call(s32[1]{0:T(128)} %bitcast.1.where_ref, f32[1,512]{1,0:T(1,128)} %copy-done.9, f32[1,512]{1,0:T(1,128)} %copy-done.11, ...), custom_call_target="tpu_custom_call" | custom-call | flops 8000000000 | bytes 10000000 | tf_op jit(solution)/shard_map/attention/pallas_call | solution.py:171
  62.0 1.4 %all_to_all.18 = f32[8,1,160]{2,1,0:T(1,128)} reshape(f32[2,640]{1,0:T(2,128)} %get-tuple-element.33) | data formatting | bytes 10240 | tf_op jit(solution)/shard_map/all_to_all | solution.py:213
  63.4 9.5 %all-to-all-start = ((f32[8,1,160]{2,1,0:T(1,128)}), f32[8,1,160]{2,1,0:T(1,128)S(1)}, u32[]{:S(2)}, u32[]{:S(2)}) async-start(f32[8,1,160]{2,1,0:T(1,128)} %all_to_all.18), calls=%async_computation | async-start | bytes 16384 | tf_op jit(solution)/shard_map/all_to_all | solution.py:213
  72.9 0.7 copy-done.13
  73.6 3.9 %all-to-all-done = f32[8,1,160]{2,1,0:T(1,128)S(1)} async-done(((f32[8,1,160]{2,1,0:T(1,128)}), f32[8,1,160]{2,1,0:T(1,128)S(1)}, u32[]{:S(2)}, u32[]{:S(2)}) %all-to-all-start) | async-done | bytes 5152 | tf_op jit(solution)/shard_map/all_to_all | solution.py:213
  77.6 0.9 broadcast_in_dim.29
  78.4 14.1 %all-to-all-start.1 = ((f32[96,1,672]{2,1,0:T(1,128)}), f32[96,1,672]{2,1,0:T(1,128)S(1)}, u32[]{:S(2)}, u32[]{:S(2)}) async-start(f32[96,1,672]{2,1,0:T(1,128)} %broadcast_in_dim.29), calls=%async_computation.1 | async-start | bytes 589824 | tf_op jit(solution)/shard_map/all_to_all | solution.py:33
  92.6 0.0 copy-start.10
  92.6 0.6 copy-done.12
  93.3 0.0 copy-done.10
  93.3 16.1 %all-to-all-done.1 = f32[96,1,672]{2,1,0:T(1,128)S(1)} async-done(((f32[96,1,672]{2,1,0:T(1,128)}), f32[96,1,672]{2,1,0:T(1,128)S(1)}, u32[]{:S(2)}, u32[]{:S(2)}) %all-to-all-start.1) | async-done | bytes 258080 | tf_op jit(solution)/shard_map/all_to_all | solution.py:33
  109.4 0.7 reduce.2
  110.1 0.1 reshape.73
  110.2 0.0 copy-start.1
  110.3 0.1 broadcast_in_dim.30
  110.3 0.6 broadcast_in_dim.31
  111.0 6.7 %all-to-all-start.2 = ((f32[8,1,1280]{2,1,0:T(1,128)}), f32[8,1,1280]{2,1,0:T(1,128)S(1)}, u32[]{:S(2)}, u32[]{:S(2)}) async-start(f32[8,1,1280]{2,1,0:T(1,128)} %broadcast_in_dim.31), calls=%async_computation.2 | async-start | bytes 81920 | tf_op jit(solution)/shard_map/all_to_all | solution.py:33
  117.7 0.0 copy-start.3
  117.7 0.9 fusion.5
  118.6 0.1 copy-done.3
  118.7 0.3 copy-done.6
  119.0 0.9 fusion.2
  119.9 2.5 %all-to-all-done.2 = f32[8,1,1280]{2,1,0:T(1,128)S(1)} async-done(((f32[8,1,1280]{2,1,0:T(1,128)}), f32[8,1,1280]{2,1,0:T(1,128)S(1)}, u32[]{:S(2)}, u32[]{:S(2)}) %all-to-all-start.2) | async-done | bytes 40992 | tf_op jit(solution)/shard_map/all_to_all | solution.py:33
  122.4 0.1 reduce.3
  122.5 0.1 reshape.74
  122.6 0.7 squeeze.6
  123.3 0.7 squeeze.7
  (47 shorter events, 0.3 us)
Async XLA Ops:
  0.6 1.1 copy-start.8
  1.7 10.8 %copy-start = (bf16[256,640]{1,0:T(8,128)(2,1)S(1)}, bf16[256,640]{1,0:T(8,128)(2,1)}, u32[]{:S(2)}) copy-start(bf16[256,640]{1,0:T(8,128)(2,1)} %refs_1_.1) | copy-start | bytes 983044
  1.7 10.8 %copy-start.2 = (bf16[256,640]{1,0:T(8,128)(2,1)S(1)}, bf16[256,640]{1,0:T(8,128)(2,1)}, u32[]{:S(2)}) copy-start(bf16[256,640]{1,0:T(8,128)(2,1)} %refs_0_.1) | copy-start | bytes 983044
  1.8 21.8 %collective-permute-start = (bf16[256,1280]{1,0:T(8,128)(2,1)S(1)}, bf16[256,1280]{1,0:T(8,128)(2,1)S(1)}, u32[]{:S(2)}, u32[]{:S(2)}) collective-permute-start(bf16[256,1280]{1,0:T(8,128)(2,1)S(1)} %constant_dynamic-update-slice_fusion), channel_id=1, source_target_pairs={{0,96},{1,97},{2,98},{3,99},{4,100},{5,101},{6,102},{7,103},{8,104... | collective-permute-start | bytes 1966088 | tf_op jit(solution)/shard_map/ppermute | solution.py:43
  3.2 20.4 %collective-permute-start.1 = (bf16[256,1280]{1,0:T(8,128)(2,1)S(1)}, bf16[256,1280]{1,0:T(8,128)(2,1)S(1)}, u32[]{:S(2)}, u32[]{:S(2)}) collective-permute-start(bf16[256,1280]{1,0:T(8,128)(2,1)S(1)} %constant_dynamic-update-slice_fusion), channel_id=1, source_target_pairs={{0,192},{192,384},{384,576},{1,193},{193,385},{385,577},{2,194},{1... | collective-permute-start | bytes 1966088 | tf_op jit(solution)/shard_map/ppermute | solution.py:41
  7.2 16.4 %collective-permute-start.2 = (bf16[256,1280]{1,0:T(8,128)(2,1)S(1)}, bf16[256,1280]{1,0:T(8,128)(2,1)S(1)}, u32[]{:S(2)}, u32[]{:S(2)}) collective-permute-start(bf16[256,1280]{1,0:T(8,128)(2,1)S(1)} %constant_dynamic-update-slice_fusion), channel_id=1, source_target_pairs={{0,576},{96,672},{288,96},{1,577},{97,673},{289,97},{2,578},{98,67... | collective-permute-start | bytes 1966088 | tf_op jit(solution)/shard_map/ppermute | solution.py:42
  23.6 2.2 %copy-start.9 = (f32[1,512]{1,0:T(1,128)}, f32[1,512]{1,0:T(1,128)S(1)}, u32[]{:S(2)}) copy-start(f32[1,512]{1,0:T(1,128)S(1)} %psum.7.squares_ref) | copy-start | bytes 6148
  23.6 0.9 copy-start.14
  23.6 19.3 %copy-start.4 = (bf16[256,1280]{1,0:T(8,128)(2,1)}, bf16[256,1280]{1,0:T(8,128)(2,1)S(1)}, u32[]{:S(2)}) copy-start(bf16[256,1280]{1,0:T(8,128)(2,1)S(1)} %collective-permute-done.1.refs_5_) | copy-start | bytes 1966084
  23.6 22.1 %copy-start.5 = (bf16[256,1280]{1,0:T(8,128)(2,1)}, bf16[256,1280]{1,0:T(8,128)(2,1)S(1)}, u32[]{:S(2)}) copy-start(bf16[256,1280]{1,0:T(8,128)(2,1)S(1)} %collective-permute-done.2.refs_9_) | copy-start | bytes 1966084
  24.4 23.2 %collective-permute-start.3 = (bf16[256,1280]{1,0:T(8,128)(2,1)S(1)}, bf16[256,1280]{1,0:T(8,128)(2,1)S(1)}, u32[]{:S(2)}, u32[]{:S(2)}) collective-permute-start(bf16[256,1280]{1,0:T(8,128)(2,1)S(1)} %broadcast_select_fusion), channel_id=1, source_target_pairs={{384,576},{96,672},{576,384},{672,480},{385,577},{97,673},{577,385... | collective-permute-start | bytes 1966088 | tf_op jit(solution)/shard_map/ppermute | solution.py:49
  25.8 21.9 %collective-permute-start.4 = (f32[1,512]{1,0:T(1,128)S(1)}, f32[1,512]{1,0:T(1,128)S(1)}, u32[]{:S(2)}, u32[]{:S(2)}) collective-permute-start(f32[1,512]{1,0:T(1,128)S(1)} %psum.7.squares_ref), channel_id=1, source_target_pairs={{0,48},{48,0},{1,49},{49,1},{2,50},{50,2},{3,51},{51,3},{4,52},{52... | collective-permute-start | bytes 6152 | tf_op jit(solution)/shard_map/ppermute | solution.py:50
  42.9 7.2 %collective-permute-start.5 = (bf16[256,1280]{1,0:T(8,128)(2,1)S(1)}, bf16[256,1280]{1,0:T(8,128)(2,1)S(1)}, u32[]{:S(2)}, u32[]{:S(2)}) collective-permute-start(bf16[256,1280]{1,0:T(8,128)(2,1)S(1)} %collective-permute-done.1.refs_5_), channel_id=1, source_target_pairs={{0,96},{96,0},{1,97},{97,1},{2,98},{98,2},{3,99},{99,3},{4,100},{1... | collective-permute-start | bytes 1966088 | tf_op jit(solution)/shard_map/ppermute | solution.py:37
  45.7 4.4 %collective-permute-start.7 = (bf16[256,1280]{1,0:T(8,128)(2,1)S(1)}, bf16[256,1280]{1,0:T(8,128)(2,1)S(1)}, u32[]{:S(2)}, u32[]{:S(2)}) collective-permute-start(bf16[256,1280]{1,0:T(8,128)(2,1)S(1)} %collective-permute-done.2.refs_9_), channel_id=1, source_target_pairs={{0,96},{96,0},{1,97},{97,1},{2,98},{98,2},{3,99},{99,3},{4,100},{1... | collective-permute-start | bytes 1966088 | tf_op jit(solution)/shard_map/ppermute | solution.py:37
  47.6 4.1 %copy-start.11 = (f32[1,512]{1,0:T(1,128)}, f32[1,512]{1,0:T(1,128)S(1)}, u32[]{:S(2)}) copy-start(f32[1,512]{1,0:T(1,128)S(1)} %collective-permute-done.4.half_squares_ref) | copy-start | bytes 6148
  47.7 4.1 %copy-start.15 = (bf16[256,1280]{1,0:T(8,128)(2,1)}, bf16[256,1280]{1,0:T(8,128)(2,1)S(1)}, u32[]{:S(2)}) copy-start(bf16[256,1280]{1,0:T(8,128)(2,1)S(1)} %collective-permute-done.3.refs_7_) | copy-start | bytes 1966084
  47.7 4.1 %collective-permute-start.6 = (bf16[256,1280]{1,0:T(8,128)(2,1)S(1)}, bf16[256,1280]{1,0:T(8,128)(2,1)S(1)}, u32[]{:S(2)}, u32[]{:S(2)}) collective-permute-start(bf16[256,1280]{1,0:T(8,128)(2,1)S(1)} %collective-permute-done.3.refs_7_), channel_id=1, source_target_pairs={{0,96},{96,0},{1,97},{97,1},{2,98},{98,2},{3,99},{99,3},{4,100},{1... | collective-permute-start | bytes 1966088 | tf_op jit(solution)/shard_map/ppermute | solution.py:37
  50.1 1.7 %copy-start.16 = (bf16[256,1280]{1,0:T(8,128)(2,1)}, bf16[256,1280]{1,0:T(8,128)(2,1)S(1)}, u32[]{:S(2)}) copy-start(bf16[256,1280]{1,0:T(8,128)(2,1)S(1)} %collective-permute-done.5.refs_6_) | copy-start | bytes 1966084
  50.1 1.7 %copy-start.17 = (bf16[256,1280]{1,0:T(8,128)(2,1)}, bf16[256,1280]{1,0:T(8,128)(2,1)S(1)}, u32[]{:S(2)}) copy-start(bf16[256,1280]{1,0:T(8,128)(2,1)S(1)} %collective-permute-done.7.refs_10_) | copy-start | bytes 1966084
  51.8 0.9 copy-start.18
  63.4 14.1 %all-to-all-start = ((f32[8,1,160]{2,1,0:T(1,128)}), f32[8,1,160]{2,1,0:T(1,128)S(1)}, u32[]{:S(2)}, u32[]{:S(2)}) async-start(f32[8,1,160]{2,1,0:T(1,128)} %all_to_all.18), calls=%async_computation | async-start | bytes 16384 | tf_op jit(solution)/shard_map/all_to_all | solution.py:213
  72.9 0.7 copy-start.13
  78.4 31.0 %all-to-all-start.1 = ((f32[96,1,672]{2,1,0:T(1,128)}), f32[96,1,672]{2,1,0:T(1,128)S(1)}, u32[]{:S(2)}, u32[]{:S(2)}) async-start(f32[96,1,672]{2,1,0:T(1,128)} %broadcast_in_dim.29), calls=%async_computation.1 | async-start | bytes 589824 | tf_op jit(solution)/shard_map/all_to_all | solution.py:33
  92.6 0.7 copy-start.12
  92.6 0.7 copy-start.10
  110.1 7.6 %copy-start.7 = (f32[256,640]{1,0:T(8,128)S(1)}, f32[256,640]{1,0:T(8,128)}, u32[]{:S(2)}) copy-start(f32[256,640]{1,0:T(8,128)} %get-tuple-element.34) | copy-start | bytes 1966084
  110.2 7.5 %copy-start.1 = (bf16[256,640]{1,0:T(8,128)(2,1)S(1)}, bf16[256,640]{1,0:T(8,128)(2,1)}, u32[]{:S(2)}) copy-start(bf16[256,640]{1,0:T(8,128)(2,1)} %refs_1_.1) | copy-start | bytes 983044
  111.0 11.4 %all-to-all-start.2 = ((f32[8,1,1280]{2,1,0:T(1,128)}), f32[8,1,1280]{2,1,0:T(1,128)S(1)}, u32[]{:S(2)}, u32[]{:S(2)}) async-start(f32[8,1,1280]{2,1,0:T(1,128)} %broadcast_in_dim.31), calls=%async_computation.2 | async-start | bytes 81920 | tf_op jit(solution)/shard_map/all_to_all | solution.py:33
  117.7 1.0 copy-start.3
  117.7 1.3 %copy-start.6 = (f32[256,640]{1,0:T(8,128)S(1)}, f32[256,640]{1,0:T(8,128)}, u32[]{:S(2)}) copy-start(f32[256,640]{1,0:T(8,128)} %get-tuple-element.31) | copy-start | bytes 1966084

commit v6 on v5

--- a/solution.py
+++ b/solution.py
@@ -66,7 +66,7 @@
     return jnp.transpose(jnp.broadcast_to(row, (8, row.shape[1])))[:, :1]
 
 
-def attention_kernel(where_ref, squares_ref, half_squares_ref, gain_q_ref, gain_k_ref, *refs):
+def attention_kernel(where_ref, part_of_ref, squares_ref, half_squares_ref, gain_q_ref, gain_k_ref, *refs):
     sources, refs = refs[: 4 + KEY_BLOCKS], refs[4 + KEY_BLOCKS :]
     att_ref, flat_q_ref, flat_k_ref, gv_ref, inner_ref, part_ref, expo_ref, sum_q_ref, sum_k_ref = refs[:9]
     local, arrived = refs[9:-1], refs[-1]
@@ -96,7 +96,8 @@
     def one_head(remote, start):
         lanes = pl.ds(pl.multiple_of(start, DH), DH)
         value_lanes = pl.ds(pl.multiple_of(start + width, DH), DH)
-        gain_q, gain_k = gain_q_ref[:, lanes], gain_k_ref[:, lanes]
+        gain_lanes = pl.ds(pl.multiple_of(part_of_ref[0] * width + start, DH), DH)
+        gain_q, gain_k = gain_q_ref[:, gain_lanes], gain_k_ref[:, gain_lanes]
         q_full, k_full = q_ref[:, lanes].astype(jnp.float32), k_ref[:, lanes].astype(jnp.float32)
         normed_q = (q_full * rate_q * gain_q).astype(jnp.bfloat16)
         normed_k = (k_full * rate_k * gain_k).astype(jnp.bfloat16)
@@ -162,7 +163,7 @@
     inner_ref[1:2, :] = jnp.sum(jnp.transpose(sum_k_ref[...]), axis=0, keepdims=True)
 
 
-def attention(where, squares, gain_q, gain_k, queries, noisy_keys, noisy_values, out_grad, pairs):
+def attention(where, part_of, squares, gain_q, gain_k, queries, noisy_keys, noisy_values, out_grad, pairs):
     rows, width = queries.shape
     f32 = lambda *shape: jax.ShapeDtypeStruct(shape, jnp.float32)
     low = jax.ShapeDtypeStruct((rows, width), jnp.bfloat16)
@@ -170,7 +171,7 @@
     fetched = [queries, noisy_keys, noisy_values, out_grad, *pairs]
     return pl.pallas_call(
         attention_kernel,
-        in_specs=[pl.BlockSpec(memory_space=pltpu.SMEM)] + [whole] * 4 + [pl.BlockSpec(memory_space=pl.ANY)] * len(fetched),
+        in_specs=[pl.BlockSpec(memory_space=pltpu.SMEM)] * 2 + [whole] * 4 + [pl.BlockSpec(memory_space=pl.ANY)] * len(fetched),
         out_specs=[whole] * 6,
         scratch_shapes=[
             pltpu.VMEM((FRAMES * rows, rows), jnp.float32),
@@ -183,30 +184,26 @@
         compiler_params=pltpu.CompilerParams(vmem_limit_bytes=56 * 1024 * 1024),
         cost_estimate=pl.CostEstimate(flops=8_000_000_000, bytes_accessed=10_000_000, transcendentals=2_600_000),
         name="attention",
-    )(where, *squares, gain_q, gain_k, *fetched)
+    )(where, part_of, *squares, gain_q, gain_k, *fetched)
 
 
 def on_device(
     queries, noisy_keys, noisy_values, clean_keys, clean_values, gain_query, gain_key, out_grad
 ):
     length, width_dev = queries.shape
-    column_start = lax.axis_index(HALF_HEAD) * width_dev
-    gain_q = lax.dynamic_slice_in_dim(gain_query, column_start, width_dev)
-    gain_k = lax.dynamic_slice_in_dim(gain_key, column_start, width_dev)
+    part_of = lax.axis_index(HALF_HEAD).astype(jnp.int32).reshape(1)
     first = gather_first(jnp.concatenate([clean_keys, clean_values], axis=1))
     q_full = queries.astype(jnp.float32)
     k_full = noisy_keys.astype(jnp.float32)
     squares = jnp.concatenate([jnp.sum(q_full * q_full, axis=1), jnp.sum(k_full * k_full, axis=1)])[None]
     squares = lax.psum(squares, "head")
     where = lax.axis_index(FRAME).astype(jnp.int32).reshape(1)
-    squares, (sibling, *received), gain_q, gain_k, where = lax.optimization_barrier(
-        (squares, first, gain_q[None], gain_k[None], where)
-    )
+    squares, (sibling, *received) = lax.optimization_barrier((squares, first))
     before, half_squares = gather_second(*received, squares)
     pairs = [sibling] + before
     squares = (squares, half_squares)
     attended, flat_q, flat_k, grad_values, inners, parts = attention(
-        where, squares, gain_q, gain_k, queries, noisy_keys, noisy_values, out_grad, pairs
+        where, part_of, squares, gain_query[None], gain_key[None], queries, noisy_keys, noisy_values, out_grad, pairs
     )
     piece_width = width_dev // FRAMES
     pieces = parts.reshape(FRAMES, 2 * piece_width)

time: 125 us -> 124 us (level)
  local copies, waits for them, and re-layouts: 11.8 us -> 7.49 us
  starting transfers between devices: 63.8 us -> 66.8 us
    ppermute x1, starting transfers between devices: 1.32 us -> 4.51 us  [gather_second(): middle = lax.ppermute(onward, FRAME, [(4, 6), (1, 7), (6, 4), (7, 5)])]
    unnamed x40 -> x34, local copies, waits for them, and re-layouts: 4.45 us -> 2.87 us
    dynamic_slice x2 -> x0, local copies, waits for them, and re-layouts: 1.55 us -> none  [the longest x1 0.78 us: on_device(): gain_q = lax.dynamic_slice_in_dim(gain_query, column_start, width_dev)]
  transfers between devices with their start and end apart: 11 -> 11, of which waited for: 4 -> 4; matrix products, arithmetic and copies ran while one was open for 4% -> 2% of each run, Pallas kernels for 0% -> 0%
where the time goes in v6:
time: 124 us; the launch traced here: 123 us
  starting transfers between devices  66.8 us (54%)
  waiting for transfers between devices  24.7 us (20%)
  blocking collectives  10.9 us (9%)
  Pallas kernels  9.43 us (8%)
  local copies, waits for them, and re-layouts  7.49 us (6%)
  other arithmetic  2.98 us (2%)
    all_to_all x2, starting transfers between devices, from_all(): lax.all_to_all(jnp.broadcast_to(x[None], (devices,) + x.shape), axes, 0, 0)  21.6 us
    all_to_all x2, waiting for transfers between devices, from_all(): lax.all_to_all(jnp.broadcast_to(x[None], (devices,) + x.shape), axes, 0, 0)  18.6 us
    ppermute x1, starting transfers between devices, gather_second(): half_squares = lax.ppermute(squares, 'half', [(0, 1), (1, 0)])  17.4 us
    psum x1, blocking collectives, on_device(): squares = lax.psum(squares, 'head')  10.9 us
    pallas_call x1, Pallas kernels, attention(): pl.pallas_call(attention_kernel, in_specs=[pl.BlockSpec(memory_space=pltp...  9.43 us
    all_to_all x1, starting transfers between devices, on_device(): piece = jnp.sum(lax.all_to_all(pieces, FRAME, 0, 0), axis=0)  9.14 us
    ppermute x3, starting transfers between devices, other_core(): return lax.ppermute(block, 'core', [(0, 1), (1, 0)])  6.25 us
    ppermute x1, starting transfers between devices, gather_second(): middle = lax.ppermute(onward, FRAME, [(4, 6), (1, 7), (6, 4), (7, 5)])  4.51 us
  transfers between devices with their start and end apart: 11, of which 4 were waited for; matrix products, arithmetic and copies ran while one was open for 2% of the time, Pallas kernels for 0%

profile of v6, /device:TPU:1, one launch (start us, length us, event | category | flops | bytes accessed | tf_op | source)
XLA Modules:
  0.0 123.4 jit_solution(11320257721951688701)
XLA Ops:
  0.6 1.0 constant_dynamic-update-slice_fusion.1
  1.7 0.0 copy-done.8
  1.7 0.0 copy-start
  1.7 0.0 copy-start.2
  1.8 1.4 %collective-permute-start = (bf16[256,1280]{1,0:T(8,128)(2,1)S(1)}, bf16[256,1280]{1,0:T(8,128)(2,1)S(1)}, u32[]{:S(2)}, u32[]{:S(2)}) collective-permute-start(bf16[256,1280]{1,0:T(8,128)(2,1)S(1)} %constant_dynamic-update-slice_fusion), channel_id=1, source_target_pairs={{0,96},{1,97},{2,98},{3,99},{4,100},{5,101},{6,102},{7,103},{8,104... | collective-permute-start | bytes 1966088 | tf_op jit(solution)/shard_map/ppermute | solution.py:43
  3.2 4.0 %collective-permute-start.1 = (bf16[256,1280]{1,0:T(8,128)(2,1)S(1)}, bf16[256,1280]{1,0:T(8,128)(2,1)S(1)}, u32[]{:S(2)}, u32[]{:S(2)}) collective-permute-start(bf16[256,1280]{1,0:T(8,128)(2,1)S(1)} %constant_dynamic-update-slice_fusion), channel_id=1, source_target_pairs={{0,192},{192,384},{384,576},{1,193},{193,385},{385,577},{2,194},{1... | collective-permute-start | bytes 1966088 | tf_op jit(solution)/shard_map/ppermute | solution.py:41
  7.2 2.5 %collective-permute-start.2 = (bf16[256,1280]{1,0:T(8,128)(2,1)S(1)}, bf16[256,1280]{1,0:T(8,128)(2,1)S(1)}, u32[]{:S(2)}, u32[]{:S(2)}) collective-permute-start(bf16[256,1280]{1,0:T(8,128)(2,1)S(1)} %constant_dynamic-update-slice_fusion), channel_id=1, source_target_pairs={{0,576},{96,672},{288,96},{1,577},{97,673},{289,97},{2,578},{98,67... | collective-permute-start | bytes 1966088 | tf_op jit(solution)/shard_map/ppermute | solution.py:42
  9.8 0.2 fusion
  10.0 10.9 %psum.7.squares_ref = f32[1,512]{1,0:T(1,128)S(1)} all-reduce(f32[1,512]{1,0:T(1,128)S(1)} %bitcast.16), channel_id=1, replica_groups=mesh['x'=4,'core'=2,'half'=2,'video_z'=6,'video_y'=2,'head'=4] {'head'}, use_global_device_ids=true, to_apply=%region_2.0 | all-reduce | flops 512 | bytes 4096 | tf_op jit(solution)/shard_map/psum | solution.py:199
  20.9 0.0 collective-permute-done.refs_4_
  20.9 0.0 collective-permute-done.1.refs_5_
  20.9 0.1 broadcast_select_fusion
  21.0 4.5 %collective-permute-start.3 = (bf16[256,1280]{1,0:T(8,128)(2,1)S(1)}, bf16[256,1280]{1,0:T(8,128)(2,1)S(1)}, u32[]{:S(2)}, u32[]{:S(2)}) collective-permute-start(bf16[256,1280]{1,0:T(8,128)(2,1)S(1)} %broadcast_select_fusion), channel_id=1, source_target_pairs={{384,576},{96,672},{576,384},{672,480},{385,577},{97,673},{577,385... | collective-permute-start | bytes 1966088 | tf_op jit(solution)/shard_map/ppermute | solution.py:49
  25.5 17.4 %collective-permute-start.4 = (f32[1,512]{1,0:T(1,128)S(1)}, f32[1,512]{1,0:T(1,128)S(1)}, u32[]{:S(2)}, u32[]{:S(2)}) collective-permute-start(f32[1,512]{1,0:T(1,128)S(1)} %psum.7.squares_ref), channel_id=1, source_target_pairs={{0,48},{48,0},{1,49},{49,1},{2,50},{50,2},{3,51},{51,3},{4,52},{52... | collective-permute-start | bytes 6152 | tf_op jit(solution)/shard_map/ppermute | solution.py:50
  42.9 1.9 %collective-permute-start.5 = (bf16[256,1280]{1,0:T(8,128)(2,1)S(1)}, bf16[256,1280]{1,0:T(8,128)(2,1)}, u32[]{:S(2)}, u32[]{:S(2)}) collective-permute-start(bf16[256,1280]{1,0:T(8,128)(2,1)S(1)} %collective-permute-done.1.refs_5_), channel_id=1, source_target_pairs={{0,96},{96,0},{1,97},{97,1},{2,98},{98,2},{3,99},{99,3},{4,100},{1... | collective-permute-start | bytes 1966088 | tf_op jit(solution)/shard_map/ppermute | solution.py:37
  44.8 2.4 %collective-permute-start.7 = (bf16[256,1280]{1,0:T(8,128)(2,1)S(1)}, bf16[256,1280]{1,0:T(8,128)(2,1)}, u32[]{:S(2)}, u32[]{:S(2)}) collective-permute-start(bf16[256,1280]{1,0:T(8,128)(2,1)S(1)} %collective-permute-done.2.refs_9_), channel_id=1, source_target_pairs={{0,96},{96,0},{1,97},{97,1},{2,98},{98,2},{3,99},{99,3},{4,100},{1... | collective-permute-start | bytes 1966088 | tf_op jit(solution)/shard_map/ppermute | solution.py:37
  47.3 0.0 collective-permute-done.4.half_squares_ref
  47.3 0.0 collective-permute-done.3.refs_7_
  47.3 1.9 %collective-permute-start.6 = (bf16[256,1280]{1,0:T(8,128)(2,1)S(1)}, bf16[256,1280]{1,0:T(8,128)(2,1)}, u32[]{:S(2)}, u32[]{:S(2)}) collective-permute-start(bf16[256,1280]{1,0:T(8,128)(2,1)S(1)} %collective-permute-done.3.refs_7_), channel_id=1, source_target_pairs={{0,96},{96,0},{1,97},{97,1},{2,98},{98,2},{3,99},{99,3},{4,100},{1... | collective-permute-start | bytes 1966088 | tf_op jit(solution)/shard_map/ppermute | solution.py:37
  49.2 0.0 collective-permute-done.5.refs_6_
  49.3 2.1 %collective-permute-done.6.refs_8_ = bf16[256,1280]{1,0:T(8,128)(2,1)} collective-permute-done((bf16[256,1280]{1,0:T(8,128)(2,1)S(1)}, bf16[256,1280]{1,0:T(8,128)(2,1)}, u32[]{:S(2)}, u32[]{:S(2)}) %collective-permute-start.6) | collective-permute-done | bytes 655392 | tf_op jit(solution)/shard_map/ppermute | solution.py:37
  51.4 9.4 %attention.1 = (bf16[256,640]{1,0:T(8,128)(2,1)}, f32[256,640]{1,0:T(8,128)}, f32[256,640]{1,0:T(8,128)}, bf16[256,640]{1,0:T(8,128)(2,1)}, f32[2,256]{1,0:T(2,128)}, /*index=5*/f32[2,640]{1,0:T(2,128)}) custom-call(s32[1]{0:T(128)} %bitcast.where_ref, s32[1]{0:T(128)} %bitcast.1.part_of_ref, f32[1,512]{1,0:T(1,128)} %copy-done.9, f32[1,512]{1,0:T(1,128)} %copy-done.11, ...), custom_call_target="tpu_custom_call" | custom-call | flops 8000000000 | bytes 10000000 | tf_op jit(solution)/shard_map/attention/pallas_call | solution.py:172
  60.9 1.4 %all_to_all.18 = f32[8,1,160]{2,1,0:T(1,128)} reshape(f32[2,640]{1,0:T(2,128)} %get-tuple-element.27) | data formatting | bytes 10240 | tf_op jit(solution)/shard_map/all_to_all | solution.py:210
  62.2 9.1 %all-to-all-start = ((f32[8,1,160]{2,1,0:T(1,128)}), f32[8,1,160]{2,1,0:T(1,128)S(1)}, u32[]{:S(2)}, u32[]{:S(2)}) async-start(f32[8,1,160]{2,1,0:T(1,128)} %all_to_all.18), calls=%async_computation | async-start | bytes 16384 | tf_op jit(solution)/shard_map/all_to_all | solution.py:210
  71.4 0.7 copy-done.13
  72.1 3.9 %all-to-all-done = f32[8,1,160]{2,1,0:T(1,128)S(1)} async-done(((f32[8,1,160]{2,1,0:T(1,128)}), f32[8,1,160]{2,1,0:T(1,128)S(1)}, u32[]{:S(2)}, u32[]{:S(2)}) %all-to-all-start) | async-done | bytes 5152 | tf_op jit(solution)/shard_map/all_to_all | solution.py:210
  76.0 0.9 broadcast_in_dim.29
  76.9 15.0 %all-to-all-start.1 = ((f32[96,1,672]{2,1,0:T(1,128)}), f32[96,1,672]{2,1,0:T(1,128)S(1)}, u32[]{:S(2)}, u32[]{:S(2)}) async-start(f32[96,1,672]{2,1,0:T(1,128)} %broadcast_in_dim.29), calls=%async_computation.1 | async-start | bytes 589824 | tf_op jit(solution)/shard_map/all_to_all | solution.py:33
  91.9 0.0 copy-start.10
  91.9 0.6 copy-done.12
  92.6 0.0 copy-done.10
  92.6 16.1 %all-to-all-done.1 = f32[96,1,672]{2,1,0:T(1,128)S(1)} async-done(((f32[96,1,672]{2,1,0:T(1,128)}), f32[96,1,672]{2,1,0:T(1,128)S(1)}, u32[]{:S(2)}, u32[]{:S(2)}) %all-to-all-start.1) | async-done | bytes 258080 | tf_op jit(solution)/shard_map/all_to_all | solution.py:33
  108.7 0.7 reduce.2
  109.4 0.1 reshape.77
  109.5 0.0 copy-start.1
  109.6 0.1 broadcast_in_dim.30
  109.7 0.6 broadcast_in_dim.31
  110.3 6.7 %all-to-all-start.2 = ((f32[8,1,1280]{2,1,0:T(1,128)}), f32[8,1,1280]{2,1,0:T(1,128)S(1)}, u32[]{:S(2)}, u32[]{:S(2)}) async-start(f32[8,1,1280]{2,1,0:T(1,128)} %broadcast_in_dim.31), calls=%async_computation.2 | async-start | bytes 81920 | tf_op jit(solution)/shard_map/all_to_all | solution.py:33
  117.0 0.0 copy-start.3
  117.0 0.9 fusion.5
  117.9 0.1 copy-done.3
  118.0 0.3 copy-done.4
  118.3 0.9 fusion.2
  119.2 2.5 %all-to-all-done.2 = f32[8,1,1280]{2,1,0:T(1,128)S(1)} async-done(((f32[8,1,1280]{2,1,0:T(1,128)}), f32[8,1,1280]{2,1,0:T(1,128)S(1)}, u32[]{:S(2)}, u32[]{:S(2)}) %all-to-all-start.2) | async-done | bytes 40992 | tf_op jit(solution)/shard_map/all_to_all | solution.py:33
  121.7 0.1 reduce.3
  121.8 0.1 reshape.78
  121.9 0.7 squeeze.6
  122.7 0.7 squeeze.7
  (37 shorter events, 0.3 us)
Async XLA Ops:
  0.6 1.1 copy-start.8
  1.7 8.0 %copy-start = (bf16[256,640]{1,0:T(8,128)(2,1)S(1)}, bf16[256,640]{1,0:T(8,128)(2,1)}, u32[]{:S(2)}) copy-start(bf16[256,640]{1,0:T(8,128)(2,1)} %refs_1_.1) | copy-start | bytes 983044
  1.7 8.0 %copy-start.2 = (bf16[256,640]{1,0:T(8,128)(2,1)S(1)}, bf16[256,640]{1,0:T(8,128)(2,1)}, u32[]{:S(2)}) copy-start(bf16[256,640]{1,0:T(8,128)(2,1)} %refs_0_.1) | copy-start | bytes 983044
  1.8 19.1 %collective-permute-start = (bf16[256,1280]{1,0:T(8,128)(2,1)S(1)}, bf16[256,1280]{1,0:T(8,128)(2,1)S(1)}, u32[]{:S(2)}, u32[]{:S(2)}) collective-permute-start(bf16[256,1280]{1,0:T(8,128)(2,1)S(1)} %constant_dynamic-update-slice_fusion), channel_id=1, source_target_pairs={{0,96},{1,97},{2,98},{3,99},{4,100},{5,101},{6,102},{7,103},{8,104... | collective-permute-start | bytes 1966088 | tf_op jit(solution)/shard_map/ppermute | solution.py:43
  3.2 17.7 %collective-permute-start.1 = (bf16[256,1280]{1,0:T(8,128)(2,1)S(1)}, bf16[256,1280]{1,0:T(8,128)(2,1)S(1)}, u32[]{:S(2)}, u32[]{:S(2)}) collective-permute-start(bf16[256,1280]{1,0:T(8,128)(2,1)S(1)} %constant_dynamic-update-slice_fusion), channel_id=1, source_target_pairs={{0,192},{192,384},{384,576},{1,193},{193,385},{385,577},{2,194},{1... | collective-permute-start | bytes 1966088 | tf_op jit(solution)/shard_map/ppermute | solution.py:41
  7.2 13.7 %collective-permute-start.2 = (bf16[256,1280]{1,0:T(8,128)(2,1)S(1)}, bf16[256,1280]{1,0:T(8,128)(2,1)S(1)}, u32[]{:S(2)}, u32[]{:S(2)}) collective-permute-start(bf16[256,1280]{1,0:T(8,128)(2,1)S(1)} %constant_dynamic-update-slice_fusion), channel_id=1, source_target_pairs={{0,576},{96,672},{288,96},{1,577},{97,673},{289,97},{2,578},{98,67... | collective-permute-start | bytes 1966088 | tf_op jit(solution)/shard_map/ppermute | solution.py:42
  20.9 4.7 %copy-start.9 = (f32[1,512]{1,0:T(1,128)}, f32[1,512]{1,0:T(1,128)S(1)}, u32[]{:S(2)}) copy-start(f32[1,512]{1,0:T(1,128)S(1)} %psum.7.squares_ref) | copy-start | bytes 6148
  20.9 30.6 %copy-start.14 = (bf16[256,1280]{1,0:T(8,128)(2,1)}, bf16[256,1280]{1,0:T(8,128)(2,1)S(1)}, u32[]{:S(2)}) copy-start(bf16[256,1280]{1,0:T(8,128)(2,1)S(1)} %collective-permute-done.refs_4_) | copy-start | bytes 1966084
  20.9 22.0 %copy-start.6 = (bf16[256,1280]{1,0:T(8,128)(2,1)}, bf16[256,1280]{1,0:T(8,128)(2,1)S(1)}, u32[]{:S(2)}) copy-start(bf16[256,1280]{1,0:T(8,128)(2,1)S(1)} %collective-permute-done.1.refs_5_) | copy-start | bytes 1966084
  20.9 23.9 %copy-start.7 = (bf16[256,1280]{1,0:T(8,128)(2,1)}, bf16[256,1280]{1,0:T(8,128)(2,1)S(1)}, u32[]{:S(2)}) copy-start(bf16[256,1280]{1,0:T(8,128)(2,1)S(1)} %collective-permute-done.2.refs_9_) | copy-start | bytes 1966084
  21.0 26.3 %collective-permute-start.3 = (bf16[256,1280]{1,0:T(8,128)(2,1)S(1)}, bf16[256,1280]{1,0:T(8,128)(2,1)S(1)}, u32[]{:S(2)}, u32[]{:S(2)}) collective-permute-start(bf16[256,1280]{1,0:T(8,128)(2,1)S(1)} %broadcast_select_fusion), channel_id=1, source_target_pairs={{384,576},{96,672},{576,384},{672,480},{385,577},{97,673},{577,385... | collective-permute-start | bytes 1966088 | tf_op jit(solution)/shard_map/ppermute | solution.py:49
  25.5 21.7 %collective-permute-start.4 = (f32[1,512]{1,0:T(1,128)S(1)}, f32[1,512]{1,0:T(1,128)S(1)}, u32[]{:S(2)}, u32[]{:S(2)}) collective-permute-start(f32[1,512]{1,0:T(1,128)S(1)} %psum.7.squares_ref), channel_id=1, source_target_pairs={{0,48},{48,0},{1,49},{49,1},{2,50},{50,2},{3,51},{51,3},{4,52},{52... | collective-permute-start | bytes 6152 | tf_op jit(solution)/shard_map/ppermute | solution.py:50
  42.9 6.4 %collective-permute-start.5 = (bf16[256,1280]{1,0:T(8,128)(2,1)S(1)}, bf16[256,1280]{1,0:T(8,128)(2,1)}, u32[]{:S(2)}, u32[]{:S(2)}) collective-permute-start(bf16[256,1280]{1,0:T(8,128)(2,1)S(1)} %collective-permute-done.1.refs_5_), channel_id=1, source_target_pairs={{0,96},{96,0},{1,97},{97,1},{2,98},{98,2},{3,99},{99,3},{4,100},{1... | collective-permute-start | bytes 1966088 | tf_op jit(solution)/shard_map/ppermute | solution.py:37
  44.8 4.4 %collective-permute-start.7 = (bf16[256,1280]{1,0:T(8,128)(2,1)S(1)}, bf16[256,1280]{1,0:T(8,128)(2,1)}, u32[]{:S(2)}, u32[]{:S(2)}) collective-permute-start(bf16[256,1280]{1,0:T(8,128)(2,1)S(1)} %collective-permute-done.2.refs_9_), channel_id=1, source_target_pairs={{0,96},{96,0},{1,97},{97,1},{2,98},{98,2},{3,99},{99,3},{4,100},{1... | collective-permute-start | bytes 1966088 | tf_op jit(solution)/shard_map/ppermute | solution.py:37
  47.3 2.0 %copy-start.11 = (f32[1,512]{1,0:T(1,128)}, f32[1,512]{1,0:T(1,128)S(1)}, u32[]{:S(2)}) copy-start(f32[1,512]{1,0:T(1,128)S(1)} %collective-permute-done.4.half_squares_ref) | copy-start | bytes 6148
  47.3 4.1 %copy-start.15 = (bf16[256,1280]{1,0:T(8,128)(2,1)}, bf16[256,1280]{1,0:T(8,128)(2,1)S(1)}, u32[]{:S(2)}) copy-start(bf16[256,1280]{1,0:T(8,128)(2,1)S(1)} %collective-permute-done.3.refs_7_) | copy-start | bytes 1966084
  47.3 4.1 %collective-permute-start.6 = (bf16[256,1280]{1,0:T(8,128)(2,1)S(1)}, bf16[256,1280]{1,0:T(8,128)(2,1)}, u32[]{:S(2)}, u32[]{:S(2)}) collective-permute-start(bf16[256,1280]{1,0:T(8,128)(2,1)S(1)} %collective-permute-done.3.refs_7_), channel_id=1, source_target_pairs={{0,96},{96,0},{1,97},{97,1},{2,98},{98,2},{3,99},{99,3},{4,100},{1... | collective-permute-start | bytes 1966088 | tf_op jit(solution)/shard_map/ppermute | solution.py:37
  62.2 13.8 %all-to-all-start = ((f32[8,1,160]{2,1,0:T(1,128)}), f32[8,1,160]{2,1,0:T(1,128)S(1)}, u32[]{:S(2)}, u32[]{:S(2)}) async-start(f32[8,1,160]{2,1,0:T(1,128)} %all_to_all.18), calls=%async_computation | async-start | bytes 16384 | tf_op jit(solution)/shard_map/all_to_all | solution.py:210
  71.4 0.7 copy-start.13
  76.9 31.8 %all-to-all-start.1 = ((f32[96,1,672]{2,1,0:T(1,128)}), f32[96,1,672]{2,1,0:T(1,128)S(1)}, u32[]{:S(2)}, u32[]{:S(2)}) async-start(f32[96,1,672]{2,1,0:T(1,128)} %broadcast_in_dim.29), calls=%async_computation.1 | async-start | bytes 589824 | tf_op jit(solution)/shard_map/all_to_all | solution.py:33
  91.9 0.7 copy-start.12
  91.9 0.7 copy-start.10
  109.4 7.6 %copy-start.5 = (f32[256,640]{1,0:T(8,128)S(1)}, f32[256,640]{1,0:T(8,128)}, u32[]{:S(2)}) copy-start(f32[256,640]{1,0:T(8,128)} %get-tuple-element.28) | copy-start | bytes 1966084
  109.5 7.5 %copy-start.1 = (bf16[256,640]{1,0:T(8,128)(2,1)S(1)}, bf16[256,640]{1,0:T(8,128)(2,1)}, u32[]{:S(2)}) copy-start(bf16[256,640]{1,0:T(8,128)(2,1)} %refs_1_.1) | copy-start | bytes 983044
  110.3 11.4 %all-to-all-start.2 = ((f32[8,1,1280]{2,1,0:T(1,128)}), f32[8,1,1280]{2,1,0:T(1,128)S(1)}, u32[]{:S(2)}, u32[]{:S(2)}) async-start(f32[8,1,1280]{2,1,0:T(1,128)} %broadcast_in_dim.31), calls=%async_computation.2 | async-start | bytes 81920 | tf_op jit(solution)/shard_map/all_to_all | solution.py:33
  117.0 1.0 copy-start.3
  117.0 1.3 %copy-start.4 = (f32[256,640]{1,0:T(8,128)S(1)}, f32[256,640]{1,0:T(8,128)}, u32[]{:S(2)}) copy-start(f32[256,640]{1,0:T(8,128)} %get-tuple-element.25) | copy-start | bytes 1966084
